TPU v7x, 32 devices: a whole 2x2x4 slice. The times are simulated.
32 devices in a mesh: groups: 2 (over x), row: 16 (over z, y, core).
Axes of the slice: x: 2, y: 2, z: 4, core: 2. Of those that a mesh axis runs over, the one named last changes fastest.
Arguments:
- atom_feat: bfloat16 [8192, 128], P(('groups', 'row')), parts along dimension 0, may hold values from -8 to 8
- window_start: int32 [256], P(('groups', 'row')), parts along dimension 0, may hold values from -64 to 4032, as said below
- atom_count: int32 [512], P(('groups', 'row')), parts along dimension 0, may hold values from 1 to 24, as said below
- residue_type: int32 [512], P(('groups', 'row')), parts along dimension 0, may hold values from 0 to 31
- chain_id: int32 [512], P(('groups', 'row')), parts along dimension 0, may hold values from 0 to 5, never falling along the last dimension, each value on 1 to 64 neighbouring positions
- token_single: bfloat16 [512, 768], P(('groups', 'row')), parts along dimension 0, may hold values from -6 to 6
- pair: bfloat16 [512, 256, 128], P(('groups', 'row')), parts along dimension 0, may hold values from -8 to 8
- atom_gain: float32 [128], replicated, may hold values from 0.25 to 1.75
- atom_qkv: bfloat16 [128, 384], replicated, may hold values from -1 to 1
- atom_out: bfloat16 [128, 128], replicated, may hold values from -0.5 to 0.5
- pool_weight: bfloat16 [128, 768], replicated, may hold values from -0.5 to 0.5
- restype_table: bfloat16 [32, 768], replicated, may hold values from -3 to 3
- token_gain: float32 [768], replicated, may hold values from 0.25 to 1.75
- token_proj: bfloat16 [768, 3072], replicated, may hold values from -0.21875 to 0.21875
- token_out: bfloat16 [768, 768], replicated, may hold values from -0.21875 to 0.21875
- pair_gain: float32 [128], replicated, may hold values from 0.1 to 1.9
- pair_bias_weight: bfloat16 [128, 16], replicated, may hold values from -16 to 16
- chain_weight: float32 [16], replicated, may hold values from -2 to 2
- back_weight: bfloat16 [768, 128], replicated, may hold values from -0.21875 to 0.21875
Outputs:
- atoms_out: bfloat16 [8192, 128], P(('groups', 'row')), parts along dimension 0
- tokens_out: bfloat16 [512, 768], P(('groups', 'row')), parts along dimension 0
There are 2 independent parts, one for each index of `groups`. A program takes and returns all parts, laid end to end along the dimension named above; an argument that names none is the same for every part. Nothing has to cross between parts.
Inputs may be any that keep to these rules, and one draw needn't show every extreme that they name: `window_start`: key window b begins within 16 of b * 32 + 32 // 2 - 128 // 2. `atom_count`: atoms of token t follow those of token t - 1 and the counts sum to 4096; for every k, the first atom of token k * 16 lies within 64 of atom k * 256. `chain_id`: chain numbers never fall along the tokens.
All inputs are finite; a program needn't handle non-finite values.
Results may differ from a plain program's by a relative error of at most 0.008.
Values may be sent and summed in bfloat16 or wider, within the bound.
No kernel may reach another device: no remote copies, remote signals or barrier semaphores. Data moves between devices by JAX's collectives and lax.ppermute only.
A program may use at most 64 MiB of HBM per device.

v0:
```python
import math

import jax
import jax.numpy as jnp
from jax import lax
from jax.sharding import PartitionSpec as P

CA = 128
CS = 768
HEADS = 16
AHEADS = 4
RESTYPES = 32
QBLK = 32
KWIN = 128
HDIM = 48
ADIM = 32
HALO = 64


def extended(x, sides, width):
    for axis, dim in sides:
        size, length = (lax.axis_size(axis), x.shape[dim])
        up = [(i, (i + 1) % size) for i in range(size - 1)]
        down = [(j, i) for i, j in up]
        last = lax.slice_in_dim(x, length - width, length, axis=dim)
        initial = lax.slice_in_dim(x, 0, width, axis=dim)
        before = lax.ppermute(last, axis, up)
        after = lax.ppermute(initial, axis, down)
        x = jnp.concatenate([before, x, after], axis=dim)
    return x


def layer_norm(values, gain):
    centered = values - jnp.mean(values, axis=-1, keepdims=True)
    variance = jnp.mean(centered * centered, axis=-1, keepdims=True)
    return centered * lax.rsqrt(variance + 1e-05) * gain


def window_attend(queries, windows, inside):
    blocks = queries.shape[0]
    keys = windows[:, :, :CA].reshape(blocks, KWIN, AHEADS, ADIM)
    values = windows[:, :, CA:].reshape(blocks, KWIN, AHEADS, ADIM)
    scores = jnp.einsum(
        "bqhd,bkhd->bhqk", queries, keys, preferred_element_type=jnp.float32
    ) / math.sqrt(ADIM)
    scores = jnp.where(inside[:, None, None, :], scores, -1000000000.0)
    weights = jnp.exp(scores - jnp.max(scores, axis=-1, keepdims=True))
    denom = jnp.sum(weights, axis=-1, keepdims=True)
    mixed = jnp.einsum(
        "bhqk,bkhd->bqhd", weights.astype(jnp.bfloat16), values, preferred_element_type=jnp.float32
    )
    mixed = mixed / jnp.transpose(denom, (0, 2, 1, 3))
    return mixed.reshape(blocks * QBLK, CA).astype(jnp.bfloat16)


def shards(
    atom_feat,
    window_start,
    atom_count,
    residue_type,
    chain_id,
    token_single,
    pair,
    atom_gain,
    atom_qkv,
    atom_out,
    pool_weight,
    restype_table,
    token_gain,
    token_proj,
    token_out,
    pair_gain,
    pair_bias_weight,
    chain_weight,
    back_weight,
):
    atom_rows = atom_feat.shape[0]
    token_rows = token_single.shape[0]
    device = lax.axis_index("row")
    all_atoms = atom_rows * lax.axis_size("row")
    counts_all = lax.all_gather(atom_count, "row", axis=0, tiled=True)
    ends = jnp.cumsum(counts_all)
    first_atom = device * atom_rows
    own_tokens = jnp.searchsorted(
        ends, first_atom + jnp.arange(atom_rows, dtype=jnp.int32), side="right"
    )
    nearby = (device - 1) * token_rows + jnp.arange(3 * token_rows, dtype=jnp.int32)
    normed = layer_norm(atom_feat.astype(jnp.float32), atom_gain).astype(jnp.bfloat16)
    atom_proj = jnp.dot(normed, atom_qkv, preferred_element_type=jnp.float32).astype(jnp.bfloat16)
    queries = atom_proj[:, :CA].reshape(atom_rows // QBLK, QBLK, AHEADS, ADIM)
    padded = extended(atom_proj[:, CA:], (("row", 0),), HALO)
    anchors = window_start - first_atom + HALO
    windows = jax.vmap(lambda anchor: lax.dynamic_slice_in_dim(padded, anchor, KWIN, 0))(anchors)
    position = window_start[:, None] + jnp.arange(KWIN, dtype=jnp.int32)[None, :]
    inside = (position >= 0) & (position < all_atoms)
    attended = window_attend(queries, windows, inside)
    atoms_mid = (
        atom_feat.astype(jnp.float32)
        + jnp.dot(attended, atom_out, preferred_element_type=jnp.float32)
    ).astype(jnp.bfloat16)
    lifted = jax.nn.relu(
        jnp.dot(atoms_mid, pool_weight, preferred_element_type=jnp.float32)
    ).astype(jnp.bfloat16)
    select = (nearby[:, None] == own_tokens[None, :]).astype(jnp.bfloat16)
    partial_value = jnp.dot(select, lifted, preferred_element_type=jnp.float32)
    edges = extended(partial_value.astype(jnp.bfloat16), (("row", 0),), token_rows).astype(
        partial_value.dtype
    )
    pooled = edges[:token_rows] + edges[2 * token_rows : 3 * token_rows] + edges[4 * token_rows :]
    onehot = (residue_type[:, None] == jnp.arange(RESTYPES, dtype=jnp.int32)[None, :]).astype(
        jnp.bfloat16
    )
    state = token_single.astype(jnp.float32) + pooled / atom_count[:, None].astype(jnp.float32)
    state = state + jnp.dot(onehot, restype_table, preferred_element_type=jnp.float32)
    token_normed = layer_norm(state, token_gain).astype(jnp.bfloat16)
    token_all = jnp.dot(token_normed, token_proj, preferred_element_type=jnp.float32)
    query = token_all[:, :CS].astype(jnp.bfloat16).reshape(token_rows, HEADS, HDIM)
    gate = jax.nn.sigmoid(token_all[:, 3 * CS :])
    pair_normed = layer_norm(pair.astype(jnp.float32), pair_gain).astype(jnp.bfloat16)
    bias = jnp.einsum(
        "tkc,ch->thk", pair_normed, pair_bias_weight, preferred_element_type=jnp.float32
    )
    projected = jnp.dot(
        lax.all_gather(token_normed, "row", axis=0, tiled=True),
        token_proj[:, CS : 3 * CS],
        preferred_element_type=jnp.float32,
    ).astype(jnp.bfloat16)
    keys = projected[:, :CS]
    running_max = jnp.full((token_rows, HEADS), -1e30, jnp.float32)
    extent = keys.shape[0]
    keys_heads = keys.reshape(extent, HEADS, HDIM)
    values_heads = projected[:, CS:].reshape(extent, HEADS, HDIM)
    scores = jnp.einsum(
        "thd,khd->thk", query, keys_heads, preferred_element_type=jnp.float32
    ) / math.sqrt(HDIM)
    scores = scores + bias
    same = (
        chain_id[:, None] == lax.all_gather(chain_id, "row", axis=0, tiled=True)[None, :]
    ).astype(jnp.float32)
    scores = scores + chain_weight[None, :, None] * same[:, None, :]
    newest = jnp.maximum(running_max, jnp.max(scores, axis=-1))
    weights = jnp.exp(scores - newest[:, :, None])
    summed = jnp.sum(weights, axis=-1)
    product = jnp.einsum(
        "thk,khd->thd",
        weights.astype(jnp.bfloat16),
        values_heads,
        preferred_element_type=jnp.float32,
    )
    mixed = product / summed[:, :, None]
    gated = (mixed.reshape(token_rows, CS) * gate).astype(jnp.bfloat16)
    tokens_out = (state + jnp.dot(gated, token_out, preferred_element_type=jnp.float32)).astype(
        jnp.bfloat16
    )
    back = jnp.dot(tokens_out, back_weight, preferred_element_type=jnp.float32).astype(jnp.bfloat16)
    beside_all = extended(back, (("row", 0),), token_rows)
    select_back = (own_tokens[:, None] == nearby[None, :]).astype(jnp.bfloat16)
    spread = jnp.dot(select_back, beside_all, preferred_element_type=jnp.float32)
    atoms_out = (atoms_mid.astype(jnp.float32) + spread).astype(jnp.bfloat16)
    return (atoms_out, tokens_out)


def solution(mesh):
    return jax.shard_map(
        shards,
        mesh=mesh,
        in_specs=(
            P(("groups", "row"), None),
            P(("groups", "row")),
            P(("groups", "row")),
            P(("groups", "row")),
            P(("groups", "row")),
            P(("groups", "row"), None),
            P(("groups", "row"), None, None),
            P(),
            P(),
            P(),
            P(),
            P(),
            P(),
            P(),
            P(),
            P(),
            P(),
            P(),
            P(),
        ),
        out_specs=(P(("groups", "row"), None), P(("groups", "row"), None)),
        check_vma=False,
    )
```

profile of v0, /device:TPU:1, one launch (start us, length us, event | category | flops | bytes accessed | tf_op | source)
XLA Modules:
  0.0 107.3 jit_solution(10534046000898941628)
XLA Ops:
  0.6 1.0 convert_reduce_fusion.1
  1.7 1.0 fusion.38
  2.7 1.2 %convolution_convert_fusion.1 = bf16[256,384]{1,0:T(8,128)(2,1)S(1)} fusion(bf16[128,384]{1,0:T(8,128)(2,1)} %param.29, bf16[256,128]{1,0:T(8,128)(2,1)} %param.21, f32[128]{0:T(128)} %param.28, f32[256]{0:T(256)S(1)} %add_rsqrt_fusion.1, f32[256]{0:T(256)S(1)} %broadcast_multiply_fusion.1), kind=kOutput, calls=%fused_computation.28 | convolution fusion | flops 25427968 | bytes 363008 | tf_op jit(solution)/shard_map/dot_general | solution.py:89
  4.0 4.5 %collective-permute-start = (bf16[64,256]{1,0:T(8,128)(2,1)S(1)}, bf16[64,256]{1,0:T(8,128)(2,1)S(1)}, u32[]{:S(2)}, u32[]{:S(2)}) collective-permute-start(bf16[64,256]{1,0:T(8,128)(2,1)S(1)} %get-tuple-element.123), channel_id=1, source_target_pairs={{0,1},{1,2},{2,3},{3,4},{4,5},{5,6},{6,7},{7,8},{8,9},{9,10},{10,1... | collective-permute-start | bytes 98312 | tf_op jit(solution)/shard_map/ppermute | solution.py:27
  8.5 1.9 %collective-permute-start.1 = (bf16[64,256]{1,0:T(8,128)(2,1)S(1)}, bf16[64,256]{1,0:T(8,128)(2,1)S(1)}, u32[]{:S(2)}, u32[]{:S(2)}) collective-permute-start(bf16[64,256]{1,0:T(8,128)(2,1)S(1)} %get-tuple-element.124), channel_id=1, source_target_pairs={{1,0},{2,1},{3,2},{4,3},{5,4},{6,5},{7,6},{8,7},{9,8},{10,9},{11,1... | collective-permute-start | bytes 98312 | tf_op jit(solution)/shard_map/ppermute | solution.py:28
  10.5 0.7 fusion.73
  11.2 0.7 fusion.74
  11.9 1.2 %dynamic-slice.4 = u32[1]{0:T(128)} dynamic-slice(u32[32]{0:T(128)} %constant.113, u32[]{:T(128)S(6)} %add.148), dynamic_slice_sizes={1} | dynamic-slice | bytes 12
  13.7 0.9 dynamic-update-slice.2
  14.5 0.8 dynamic-update-slice.3
  15.4 9.8 %all-reduce.3 = (s32[256]{0:T(256)S(1)}, s32[256]{0:T(256)S(1)}) all-reduce(s32[256]{0:T(256)S(1)} %dynamic-update-slice.2, s32[256]{0:T(256)S(1)} %dynamic-update-slice.3), channel_id=1, replica_groups=mesh['groups'=2,'row'=16] {'row'}, use_global_device_ids=true, to_apply=%add.1 | all-reduce | flops 512 | bytes 4096
  25.2 0.3 reduce-window.9
  25.8 18.1 %while.26 = (s32[]{:T(128)}, u32[256]{0:T(256)S(1)}, u32[256]{0:T(256)S(1)}, s32[256]{0:T(256)S(1)}, s32[]{:T(128)}, /*index=5*/s32[]{:T(128)}, s32[]{:T(128)}, s32[]{}) while((s32[]{:T(128)}, u32[256]{0:T(256)S(1)}, u32[256]{0:T(256)S(1)}, s32[256]{0:T(256)S(1)}, s32[]{:T(128)}, /*index=5*/s32[]{:T(128)}, s32[]{:T(128)}, s32[]{}) %tuple.58), condition=%wide.region_7.8_spmd.clone, body=%wide.region_6.7_spmd.clone.sunk | while | flops 4612 | bytes 16496 | solution.py:84
  25.8 1.9 %gather_fusion = s32[256]{0:T(256)S(1)} fusion(s32[256]{0:T(256)S(1)} %get-tuple-element.227, u32[1024]{0:T(1024)S(1)} %pad_clamp_fusion.2), kind=kCustom, calls=%fused_computation.clone.clone.1 | custom fusion | bytes 3072 | tf_op jit(solution)/shard_map/jit(searchsorted)/jit(_searchsorted_scan_impl)/vmap(jit(_searchsorted_scan_impl))/while/body/eval_jaxpr/gather | solution.py:84
  27.8 1.9 %gather_fusion = s32[256]{0:T(256)S(1)} fusion(s32[256]{0:T(256)S(1)} %get-tuple-element.227, u32[1024]{0:T(1024)S(1)} %pad_clamp_fusion.2), kind=kCustom, calls=%fused_computation.clone.clone.1 | custom fusion | bytes 3072 | tf_op jit(solution)/shard_map/jit(searchsorted)/jit(_searchsorted_scan_impl)/vmap(jit(_searchsorted_scan_impl))/while/body/eval_jaxpr/gather | solution.py:84
  29.8 1.9 %gather_fusion = s32[256]{0:T(256)S(1)} fusion(s32[256]{0:T(256)S(1)} %get-tuple-element.227, u32[1024]{0:T(1024)S(1)} %pad_clamp_fusion.2), kind=kCustom, calls=%fused_computation.clone.clone.1 | custom fusion | bytes 3072 | tf_op jit(solution)/shard_map/jit(searchsorted)/jit(_searchsorted_scan_impl)/vmap(jit(_searchsorted_scan_impl))/while/body/eval_jaxpr/gather | solution.py:84
  31.9 1.9 %gather_fusion = s32[256]{0:T(256)S(1)} fusion(s32[256]{0:T(256)S(1)} %get-tuple-element.227, u32[1024]{0:T(1024)S(1)} %pad_clamp_fusion.2), kind=kCustom, calls=%fused_computation.clone.clone.1 | custom fusion | bytes 3072 | tf_op jit(solution)/shard_map/jit(searchsorted)/jit(_searchsorted_scan_impl)/vmap(jit(_searchsorted_scan_impl))/while/body/eval_jaxpr/gather | solution.py:84
  33.9 1.9 %gather_fusion = s32[256]{0:T(256)S(1)} fusion(s32[256]{0:T(256)S(1)} %get-tuple-element.227, u32[1024]{0:T(1024)S(1)} %pad_clamp_fusion.2), kind=kCustom, calls=%fused_computation.clone.clone.1 | custom fusion | bytes 3072 | tf_op jit(solution)/shard_map/jit(searchsorted)/jit(_searchsorted_scan_impl)/vmap(jit(_searchsorted_scan_impl))/while/body/eval_jaxpr/gather | solution.py:84
  35.9 1.9 %gather_fusion = s32[256]{0:T(256)S(1)} fusion(s32[256]{0:T(256)S(1)} %get-tuple-element.227, u32[1024]{0:T(1024)S(1)} %pad_clamp_fusion.2), kind=kCustom, calls=%fused_computation.clone.clone.1 | custom fusion | bytes 3072 | tf_op jit(solution)/shard_map/jit(searchsorted)/jit(_searchsorted_scan_impl)/vmap(jit(_searchsorted_scan_impl))/while/body/eval_jaxpr/gather | solution.py:84
  37.9 1.9 %gather_fusion = s32[256]{0:T(256)S(1)} fusion(s32[256]{0:T(256)S(1)} %get-tuple-element.227, u32[1024]{0:T(1024)S(1)} %pad_clamp_fusion.2), kind=kCustom, calls=%fused_computation.clone.clone.1 | custom fusion | bytes 3072 | tf_op jit(solution)/shard_map/jit(searchsorted)/jit(_searchsorted_scan_impl)/vmap(jit(_searchsorted_scan_impl))/while/body/eval_jaxpr/gather | solution.py:84
  39.9 1.9 %gather_fusion = s32[256]{0:T(256)S(1)} fusion(s32[256]{0:T(256)S(1)} %get-tuple-element.227, u32[1024]{0:T(1024)S(1)} %pad_clamp_fusion.2), kind=kCustom, calls=%fused_computation.clone.clone.1 | custom fusion | bytes 3072 | tf_op jit(solution)/shard_map/jit(searchsorted)/jit(_searchsorted_scan_impl)/vmap(jit(_searchsorted_scan_impl))/while/body/eval_jaxpr/gather | solution.py:84
  41.9 1.9 %gather_fusion = s32[256]{0:T(256)S(1)} fusion(s32[256]{0:T(256)S(1)} %get-tuple-element.227, u32[1024]{0:T(1024)S(1)} %pad_clamp_fusion.2), kind=kCustom, calls=%fused_computation.clone.clone.1 | custom fusion | bytes 3072 | tf_op jit(solution)/shard_map/jit(searchsorted)/jit(_searchsorted_scan_impl)/vmap(jit(_searchsorted_scan_impl))/while/body/eval_jaxpr/gather | solution.py:84
  43.9 0.4 convert_reduce_fusion
  44.3 1.3 %fusion.7 = f32[16,256]{1,0:T(8,128)S(1)} fusion(bf16[16,256,128]{2,1,0:T(8,128)(2,1)S(1)} %copy-done.1, f32[16,256]{1,0:T(8,128)S(1)} %broadcast_multiply_fusion), kind=kLoop, calls=%fused_computation.17 | loop fusion | flops 2093056 | bytes 1081344 | tf_op jit(solution)/shard_map/reduce_sum | solution.py:35
  45.6 2.6 %fusion.23 = f32[16,256,16]{1,2,0:T(8,128)S(1)} fusion(bf16[16,256,128]{2,1,0:T(8,128)(2,1)S(1)} %copy-done.1, f32[128]{0:T(128)S(1)} %copy-done.13, f32[16,256]{1,0:T(8,128)S(1)} %add_rsqrt_fusion, f32[16,256]{1,0:T(8,128)S(1)} %broadcast_multiply_fusion, bf16[128,16]{0,1:T(8,128)(2,1)S(1)} %copy-done.12), kind=kOutput, calls=%fused_computation.44 | convolution fusion | flops 19398656 | bytes 1348096 | tf_op jit(solution)/shard_map/tkc,ch->thk/dot_general | solution.py:120
  48.5 10.2 %while.25 = (s32[]{:T(128)}, bf16[384,256]{1,0:T(8,128)(2,1)S(1)}, s32[8,2]{0,1:T(2,128)S(1)}, bf16[8,128,256]{2,1,0:T(8,128)(2,1)S(1)}, s32[]{:T(128)}) while((s32[]{:T(128)}, bf16[384,256]{1,0:T(8,128)(2,1)S(1)}, s32[8,2]{0,1:T(2,128)S(1)}, bf16[8,128,256]{2,1,0:T(8,128)(2,1)S(1)}, s32[]{:T(128)}) %tuple.55), condition=%wide.while_cond, body=%wide.while_body.sunk | while | flops 2 | bytes 131169 | solution.py:93
  48.6 0.5 slice.126
  49.1 0.7 bitcast_dynamic-update-slice_fusion.2
  49.9 0.5 slice.126
  50.4 0.7 bitcast_dynamic-update-slice_fusion.2
  51.2 0.5 slice.126
  51.7 0.7 bitcast_dynamic-update-slice_fusion.2
  52.5 0.5 slice.126
  53.0 0.7 bitcast_dynamic-update-slice_fusion.2
  53.7 0.5 slice.126
  54.2 0.7 bitcast_dynamic-update-slice_fusion.2
  55.0 0.5 slice.126
  55.5 0.7 bitcast_dynamic-update-slice_fusion.2
  56.3 0.5 slice.126
  56.8 0.7 bitcast_dynamic-update-slice_fusion.2
  57.6 0.5 slice.126
  58.1 0.7 bitcast_dynamic-update-slice_fusion.2
  59.3 0.4 fusion.82
  59.7 0.4 fusion.28
  60.2 0.3 fusion.14
  60.9 0.2 fusion.20
  61.1 0.4 fusion.19
  61.5 6.0 %collective-permute-start.2 = (bf16[16,768]{1,0:T(8,128)(2,1)S(1)}, bf16[16,768]{1,0:T(8,128)(2,1)S(1)}, u32[]{:S(2)}, u32[]{:S(2)}) collective-permute-start(bf16[16,768]{1,0:T(8,128)(2,1)S(1)} %get-tuple-element.125), channel_id=1, source_target_pairs={{0,1},{1,2},{2,3},{3,4},{4,5},{5,6},{6,7},{7,8},{8,9},{9,10},{10,1... | collective-permute-start | bytes 73736 | tf_op jit(solution)/shard_map/ppermute | solution.py:27
  67.5 1.9 %collective-permute-start.3 = (bf16[16,768]{1,0:T(8,128)(2,1)S(1)}, bf16[16,768]{1,0:T(8,128)(2,1)S(1)}, u32[]{:S(2)}, u32[]{:S(2)}) collective-permute-start(bf16[16,768]{1,0:T(8,128)(2,1)S(1)} %get-tuple-element.126), channel_id=1, source_target_pairs={{1,0},{2,1},{3,2},{4,3},{5,4},{6,5},{7,6},{8,7},{9,8},{10,9},{11,1... | collective-permute-start | bytes 73736 | tf_op jit(solution)/shard_map/ppermute | solution.py:28
  69.6 3.1 %collective-permute-done.3 = bf16[16,768]{1,0:T(8,128)(2,1)S(1)} collective-permute-done((bf16[16,768]{1,0:T(8,128)(2,1)S(1)}, bf16[16,768]{1,0:T(8,128)(2,1)S(1)}, u32[]{:S(2)}, u32[]{:S(2)}) %collective-permute-start.3) | collective-permute-done | bytes 24608 | tf_op jit(solution)/shard_map/ppermute | solution.py:28
  72.7 0.3 fusion.83
  73.0 0.2 multiply_reduce_fusion
  73.3 18.6 %all_gather.10 = bf16[256,768]{1,0:T(8,128)(2,1)S(1)} all-gather(bf16[16,768]{1,0:T(8,128)(2,1)S(1)} %multiply_convert_fusion), channel_id=1, replica_groups=mesh['groups'=2,'row'=16] {'row'}, dimensions={0}, use_global_device_ids=true | all-gather | bytes 417792 | tf_op jit(solution)/shard_map/all_gather | solution.py:124
  91.9 3.1 %fusion.85 = f32[16,3072]{1,0:T(8,128)S(1)} fusion(bf16[16,768]{1,0:T(8,128)(2,1)S(1)} %multiply_convert_fusion, bf16[768,3072]{1,0:T(8,128)(2,1)} %param.34), kind=kOutput, calls=%fused_computation.127 | convolution fusion | flops 75497472 | bytes 4939776 | tf_op jit(solution)/shard_map/dot_general | solution.py:116
  94.9 2.4 %convolution_convert_fusion = bf16[256,1536]{1,0:T(8,128)(2,1)S(1)} fusion(bf16[256,768]{1,0:T(8,128)(2,1)S(1)} %all_gather.10, bf16[768,3072]{1,0:T(8,128)(2,1)} %param.34), kind=kOutput, calls=%fused_computation.13 | convolution fusion | flops 604372992 | bytes 3538944 | tf_op jit(solution)/shard_map/dot_general | solution.py:123
  97.7 0.3 copy-done.7
  98.0 0.3 fusion.84
  98.5 0.2 fusion.34
  98.7 0.3 fusion.18
  99.2 0.3 fusion.22
  99.6 1.9 %collective-permute-start.4 = (bf16[16,128]{1,0:T(8,128)(2,1)S(1)}, bf16[16,128]{1,0:T(8,128)(2,1)S(1)}, u32[]{:S(2)}, u32[]{:S(2)}) collective-permute-start(bf16[16,128]{1,0:T(8,128)(2,1)S(1)} %convolution_convert_fusion.2), channel_id=1, source_target_pairs={{0,1},{1,2},{2,3},{3,4},{4,5},{5,6},{6,7},{7,8},{8,9},{9,10},{10,1... | collective-permute-start | bytes 12296 | tf_op jit(solution)/shard_map/ppermute | solution.py:27
  101.5 2.4 %collective-permute-start.5 = (bf16[16,128]{1,0:T(8,128)(2,1)S(1)}, bf16[16,128]{1,0:T(8,128)(2,1)S(1)}, u32[]{:S(2)}, u32[]{:S(2)}) collective-permute-start(bf16[16,128]{1,0:T(8,128)(2,1)S(1)} %convolution_convert_fusion.2), channel_id=1, source_target_pairs={{1,0},{2,1},{3,2},{4,3},{5,4},{6,5},{7,6},{8,7},{9,8},{10,9},{11,1... | collective-permute-start | bytes 12296 | tf_op jit(solution)/shard_map/ppermute | solution.py:28
  104.0 2.5 %collective-permute-done.5 = bf16[16,128]{1,0:T(8,128)(2,1)S(1)} collective-permute-done((bf16[16,128]{1,0:T(8,128)(2,1)S(1)}, bf16[16,128]{1,0:T(8,128)(2,1)S(1)}, u32[]{:S(2)}, u32[]{:S(2)}) %collective-permute-start.5) | collective-permute-done | bytes 4128 | tf_op jit(solution)/shard_map/ppermute | solution.py:28
  106.5 0.9 fusion.21
  (111 shorter events, 3.4 us)
Async XLA Ops:
  0.6 98.5 %copy-start = (bf16[768,768]{1,0:T(8,128)(2,1)S(1)}, bf16[768,768]{1,0:T(8,128)(2,1)}, u32[]{:S(2)}) copy-start(bf16[768,768]{1,0:T(8,128)(2,1)} %param.35) | copy-start | bytes 3538948
  4.0 44.5 %collective-permute-start = (bf16[64,256]{1,0:T(8,128)(2,1)S(1)}, bf16[64,256]{1,0:T(8,128)(2,1)S(1)}, u32[]{:S(2)}, u32[]{:S(2)}) collective-permute-start(bf16[64,256]{1,0:T(8,128)(2,1)S(1)} %get-tuple-element.123), channel_id=1, source_target_pairs={{0,1},{1,2},{2,3},{3,4},{4,5},{5,6},{6,7},{7,8},{8,9},{9,10},{10,1... | collective-permute-start | bytes 98312 | tf_op jit(solution)/shard_map/ppermute | solution.py:27
  8.5 40.0 %collective-permute-start.1 = (bf16[64,256]{1,0:T(8,128)(2,1)S(1)}, bf16[64,256]{1,0:T(8,128)(2,1)S(1)}, u32[]{:S(2)}, u32[]{:S(2)}) collective-permute-start(bf16[64,256]{1,0:T(8,128)(2,1)S(1)} %get-tuple-element.124), channel_id=1, source_target_pairs={{1,0},{2,1},{3,2},{4,3},{5,4},{6,5},{7,6},{8,7},{9,8},{10,9},{11,1... | collective-permute-start | bytes 98312 | tf_op jit(solution)/shard_map/ppermute | solution.py:28
  25.8 18.1 %copy-start.1 = (bf16[16,256,128]{2,1,0:T(8,128)(2,1)S(1)}, bf16[16,256,128]{2,1,0:T(8,128)(2,1)}, u32[]{:S(2)}) copy-start(bf16[16,256,128]{2,1,0:T(8,128)(2,1)} %param.27) | copy-start | bytes 3145732
  43.9 1.7 %copy-start.12 = (bf16[128,16]{0,1:T(8,128)(2,1)S(1)}, bf16[128,16]{0,1:T(8,128)(2,1)}, u32[]{:S(2)}) copy-start(bf16[128,16]{0,1:T(8,128)(2,1)} %param.37) | copy-start | bytes 12292
  43.9 1.7 %copy-start.13 = (f32[128]{0:T(128)S(1)}, f32[128]{0:T(128)}, u32[]{:S(2)}) copy-start(f32[128]{0:T(128)} %param.36) | copy-start | bytes 1540
  59.7 1.2 %copy-start.2 = (bf16[256,128]{1,0:T(8,128)(2,1)S(1)}, bf16[256,128]{1,0:T(8,128)(2,1)}, u32[]{:S(2)}) copy-start(bf16[256,128]{1,0:T(8,128)(2,1)} %param.21) | copy-start | bytes 196612
  59.7 1.2 %copy-start.5 = (bf16[128,128]{1,0:T(8,128)(2,1)S(1)}, bf16[128,128]{1,0:T(8,128)(2,1)}, u32[]{:S(2)}) copy-start(bf16[128,128]{1,0:T(8,128)(2,1)} %param.30) | copy-start | bytes 98308
  59.7 1.4 %copy-start.9 = (bf16[128,768]{1,0:T(8,128)(2,1)S(1)}, bf16[128,768]{1,0:T(8,128)(2,1)}, u32[]{:S(2)}) copy-start(bf16[128,768]{1,0:T(8,128)(2,1)} %param.31) | copy-start | bytes 589828
  60.1 9.4 %copy-start.8 = (s32[16]{0:T(128)S(1)}, s32[16]{0:T(128)}, u32[]{:S(2)}) copy-start(s32[16]{0:T(128)} %param.25) | copy-start | bytes 196
  60.1 9.4 %copy-start.14 = (s32[16]{0:T(128)S(1)}, s32[16]{0:T(128)}, u32[]{:S(2)}) copy-start(s32[16]{0:T(128)} %param.23) | copy-start | bytes 196
  60.1 12.6 %copy-start.10 = (bf16[32,768]{1,0:T(8,128)(2,1)S(1)}, bf16[32,768]{1,0:T(8,128)(2,1)}, u32[]{:S(2)}) copy-start(bf16[32,768]{1,0:T(8,128)(2,1)} %param.32) | copy-start | bytes 147460
  60.1 12.6 %copy-start.11 = (bf16[16,768]{1,0:T(8,128)(2,1)S(1)}, bf16[16,768]{1,0:T(8,128)(2,1)}, u32[]{:S(2)}) copy-start(bf16[16,768]{1,0:T(8,128)(2,1)} %param.26) | copy-start | bytes 73732
  60.2 12.5 %copy-start.15 = (s32[16]{0:T(128)S(1)}, s32[16]{0:T(128)}, u32[]{:S(2)}) copy-start(s32[16]{0:T(128)} %param.24) | copy-start | bytes 196
  60.2 13.0 %copy-start.6 = (f32[768]{0:T(1024)S(1)}, f32[768]{0:T(1024)}, u32[]{:S(2)}) copy-start(f32[768]{0:T(1024)} %param.33) | copy-start | bytes 9220
  61.5 8.0 %collective-permute-start.2 = (bf16[16,768]{1,0:T(8,128)(2,1)S(1)}, bf16[16,768]{1,0:T(8,128)(2,1)S(1)}, u32[]{:S(2)}, u32[]{:S(2)}) collective-permute-start(bf16[16,768]{1,0:T(8,128)(2,1)S(1)} %get-tuple-element.125), channel_id=1, source_target_pairs={{0,1},{1,2},{2,3},{3,4},{4,5},{5,6},{6,7},{7,8},{8,9},{9,10},{10,1... | collective-permute-start | bytes 73736 | tf_op jit(solution)/shard_map/ppermute | solution.py:27
  67.5 5.1 %collective-permute-start.3 = (bf16[16,768]{1,0:T(8,128)(2,1)S(1)}, bf16[16,768]{1,0:T(8,128)(2,1)S(1)}, u32[]{:S(2)}, u32[]{:S(2)}) collective-permute-start(bf16[16,768]{1,0:T(8,128)(2,1)S(1)} %get-tuple-element.126), channel_id=1, source_target_pairs={{1,0},{2,1},{3,2},{4,3},{5,4},{6,5},{7,6},{8,7},{9,8},{10,9},{11,1... | collective-permute-start | bytes 73736 | tf_op jit(solution)/shard_map/ppermute | solution.py:28
  97.4 0.7 copy-start.7
  98.3 1.1 %copy-start.3 = (bf16[768,128]{1,0:T(8,128)(2,1)S(1)}, bf16[768,128]{1,0:T(8,128)(2,1)}, u32[]{:S(2)}) copy-start(bf16[768,128]{1,0:T(8,128)(2,1)} %param.39) | copy-start | bytes 589828
  99.5 7.9 %copy-start.4 = (bf16[16,768]{1,0:T(8,128)(2,1)}, bf16[16,768]{1,0:T(8,128)(2,1)S(1)}, u32[]{:S(2)}) copy-start(bf16[16,768]{1,0:T(8,128)(2,1)S(1)} %fusion.22) | copy-start | bytes 73732
  99.6 4.3 %collective-permute-start.4 = (bf16[16,128]{1,0:T(8,128)(2,1)S(1)}, bf16[16,128]{1,0:T(8,128)(2,1)S(1)}, u32[]{:S(2)}, u32[]{:S(2)}) collective-permute-start(bf16[16,128]{1,0:T(8,128)(2,1)S(1)} %convolution_convert_fusion.2), channel_id=1, source_target_pairs={{0,1},{1,2},{2,3},{3,4},{4,5},{5,6},{6,7},{7,8},{8,9},{9,10},{10,1... | collective-permute-start | bytes 12296 | tf_op jit(solution)/shard_map/ppermute | solution.py:27
  101.5 4.9 %collective-permute-start.5 = (bf16[16,128]{1,0:T(8,128)(2,1)S(1)}, bf16[16,128]{1,0:T(8,128)(2,1)S(1)}, u32[]{:S(2)}, u32[]{:S(2)}) collective-permute-start(bf16[16,128]{1,0:T(8,128)(2,1)S(1)} %convolution_convert_fusion.2), channel_id=1, source_target_pairs={{1,0},{2,1},{3,2},{4,3},{5,4},{6,5},{7,6},{8,7},{9,8},{10,9},{11,1... | collective-permute-start | bytes 12296 | tf_op jit(solution)/shard_map/ppermute | solution.py:28
where the time goes:
time: 108 us; the launch traced here: 107 us
  local copies, waits for them, and re-layouts  32.7 us (30%)
  blocking collectives  28.4 us (26%)
  starting transfers between devices  18.7 us (17%)
  matrix products  12.8 us (12%)
  other arithmetic  6.81 us (6%)
  waiting for transfers between devices  5.64 us (5%)
  between operations  1.75 us (2%)
    all_gather x1, blocking collectives, shards(): lax.all_gather(token_normed, 'row', axis=0, tiled=True)  18.6 us
    gather x9, local copies, waits for them, and re-layouts, shards(): jnp.searchsorted(ends, first_atom + jnp.arange(atom_rows, dtype=jnp.int32...  17.5 us
    ppermute x3, starting transfers between devices, extended(): before = lax.ppermute(last, axis, up)  12.5 us
    gather x24, local copies, waits for them, and re-layouts  10.1 us
    unnamed x1, blocking collectives  9.8 us
    ppermute x3, starting transfers between devices, extended(): after = lax.ppermute(initial, axis, down)  6.24 us
    ppermute x3, waiting for transfers between devices, extended(): after = lax.ppermute(initial, axis, down)  5.63 us
    unnamed x37, local copies, waits for them, and re-layouts  3.3 us
  transfers between devices with their start and end apart: 6, of which 2 were waited for; matrix products, arithmetic and copies ran while one was open for 25% of the time, Pallas kernels for 0%

commit v1 on v0

v1 whole, which is shorter than its diff:
```python
import functools
import math

import jax
import jax.numpy as jnp
from jax import lax
from jax.experimental import pallas as pl
from jax.experimental.pallas import tpu as pltpu
from jax.sharding import PartitionSpec as P

CA = 128
CS = 768
HEADS = 16
AHEADS = 4
RESTYPES = 32
QBLK = 32
KWIN = 128
HDIM = 48
ADIM = 32
HALF = 128
REACH = 64
EPS = 1e-05
NEG = -1e30
F32 = jnp.float32
BF16 = jnp.bfloat16
VMEM_LIMIT = 24 * 1024 * 1024

COUNT, CHAIN, RES, WIN = 0, 16, 32, 48
TABLE = 128


def dot(a, b):
    return lax.dot_general(a, b, (((1,), (0,)), ((), ())), preferred_element_type=F32)


def dot_nt(a, b):
    return lax.dot_general(a, b, (((1,), (1,)), ((), ())), preferred_element_type=F32)


def norm(x, gain):
    centered = x - jnp.mean(x, axis=-1, keepdims=True)
    variance = jnp.mean(centered * centered, axis=-1, keepdims=True)
    return centered * lax.rsqrt(variance + EPS) * gain


def iota(shape, axis):
    return lax.broadcasted_iota(jnp.int32, shape, axis)


def table_row(table, row):
    return jnp.sum(jnp.where(iota(table.shape, 0) == row, table, 0), axis=0, keepdims=True)


def column(row, base, size):
    shape = (size, row.shape[1])
    return jnp.sum(jnp.where(iota(shape, 1) == iota(shape, 0) + base, row, 0), axis=1, keepdims=True)


def atoms_before(table, row, tokens):
    keep = (iota(table.shape, 0) < row) & (iota(table.shape, 1) < COUNT + tokens)
    return jnp.sum(jnp.sum(jnp.where(keep, table, 0), axis=0, keepdims=True), axis=1, keepdims=True)


def pair_kernel(pair_ref, gain_ref, weight_ref, bias_ref):
    gain, weight = gain_ref[...], weight_ref[...]
    for t in range(pair_ref.shape[0]):
        normed = norm(pair_ref[t].astype(F32), gain).astype(BF16)
        bias_ref[t * HEADS : (t + 1) * HEADS, :] = dot_nt(weight, normed)


def atom_kernel(
    n,
    feat_ref,
    core_ref,
    far_ref,
    table_ref,
    single_ref,
    gain_ref,
    qkv_ref,
    out_ref,
    pool_ref,
    restype_ref,
    token_gain_ref,
    mid_ref,
    state_ref,
    normed_ref,
):
    me = lax.axis_index("row")
    even = lax.rem(me, 2) == 0
    rows = feat_ref.shape[0]
    tokens = single_ref.shape[0]
    table = table_ref[...]
    own_row = table_row(table, me)
    left = jnp.where(even, far_ref[rows - HALF :, :], core_ref[rows - HALF :, :])
    right = jnp.where(even, core_ref[:HALF, :], far_ref[:HALF, :])
    feat = jnp.concatenate([left, feat_ref[...], right], axis=0)
    normed = norm(feat.astype(F32), gain_ref[...]).astype(BF16)
    proj = dot(normed, qkv_ref[...]).astype(BF16)
    span = rows + 2 * REACH
    windows = rows // QBLK
    edge = REACH // QBLK
    win_left = table_row(table, me - 1)
    win_right = table_row(table, me + 1)
    mids = []
    for s in range(span // HALF):
        begin = REACH + HALF * s
        queries = proj[begin : begin + HALF, :CA]
        keys = proj[HALF * s : HALF * s + 2 * HALF, CA : 2 * CA]
        values = proj[HALF * s : HALF * s + 2 * HALF, 2 * CA :]
        head = iota((HALF, CA), 1) // ADIM
        stacked = jnp.concatenate(
            [jnp.where(head == h, queries, jnp.zeros_like(queries)) for h in range(AHEADS)], axis=0
        )
        scores = dot_nt(stacked, keys) * (1.0 / math.sqrt(ADIM))
        shape = (HALF, TABLE)
        block = iota(shape, 0) // QBLK + (HALF // QBLK) * s - edge
        lane = iota(shape, 1) - WIN
        begins = jnp.where((block >= 0) & (block < windows) & (lane == block), own_row, 0)
        if s == 0:
            begins += jnp.where((block < 0) & (lane == block + windows), win_left, 0)
        if s == span // HALF - 1:
            begins += jnp.where((block >= windows) & (lane == block - windows), win_right, 0)
        start = jnp.sum(begins, axis=1, keepdims=True)
        shape = (HALF, 2 * HALF)
        place = iota(shape, 1) + (me * rows - HALF + HALF * s)
        inside = (place >= start) & (place < start + KWIN) & (place >= 0) & (place < n * rows)
        inside = jnp.concatenate([inside.astype(F32)] * AHEADS, axis=0) > 0.5
        scores = jnp.where(inside, scores, NEG)
        weights = jnp.exp(scores - jnp.max(scores, axis=-1, keepdims=True))
        denom = jnp.sum(weights, axis=-1, keepdims=True)
        mixed = dot(weights.astype(BF16), values) / denom
        total = jnp.zeros((HALF, CA), F32)
        for h in range(AHEADS):
            total = total + jnp.where(head == h, mixed[h * HALF : (h + 1) * HALF], 0.0)
        added = dot(total.astype(BF16), out_ref[...])
        mids.append((feat[begin : begin + HALF].astype(F32) + added).astype(BF16))
    mid = jnp.concatenate(mids, axis=0)
    mid_ref[...] = mid[REACH : REACH + rows]
    lifted = jnp.maximum(dot(mid, pool_ref[...]), 0.0).astype(BF16)
    count = column(own_row, COUNT, tokens)
    shape = (tokens, TABLE)
    ahead = (iota(shape, 1) >= COUNT) & (iota(shape, 1) < COUNT + iota(shape, 0))
    begin = atoms_before(table, me, tokens) + jnp.sum(
        jnp.where(ahead, own_row, 0), axis=1, keepdims=True
    )
    atom = iota((tokens, span), 1) + (me * rows - REACH)
    chosen = (atom >= begin) & (atom < begin + count)
    pooled = dot(jnp.where(chosen, 1.0, 0.0).astype(BF16), lifted)
    kind = column(own_row, RES, tokens)
    onehot = jnp.where(iota((tokens, RESTYPES), 1) == kind, 1.0, 0.0).astype(BF16)
    state = single_ref[...].astype(F32) + pooled / count.astype(F32)
    state = state + dot(onehot, restype_ref[...])
    state_ref[...] = state
    token_normed = norm(state, token_gain_ref[...]).astype(BF16)
    for i in range(normed_ref.shape[0]):
        normed_ref[i] = token_normed


def query_kernel(
    normed_ref, table_ref, bias_ref, chain_weight_ref, wq_ref, wk_ref, wg_ref,
    query_ref, gate_ref, biased_ref, before_ref, own_ref, after_ref,
):
    me = lax.axis_index("row")
    normed = normed_ref[0]
    tokens = normed.shape[0]
    query = dot(normed, wq_ref[...]).astype(BF16)
    gate_ref[...] = jax.nn.sigmoid(dot(normed, wg_ref[...]))
    head = iota((HEADS, CS), 1) // HDIM == iota((HEADS, CS), 0)
    spread = jnp.concatenate(
        [
            jnp.where(head, jnp.broadcast_to(query[t : t + 1].astype(F32), (HEADS, CS)), 0.0)
            for t in range(tokens)
        ],
        axis=0,
    ).astype(BF16)
    query_ref[...] = dot_nt(spread, wk_ref[...]).astype(BF16)
    table = table_ref[...]
    n = table.shape[0]
    keys = n * tokens
    shape = (TABLE, keys)
    pick = jnp.where(iota(shape, 0) == CHAIN + iota(shape, 1) % tokens, 1.0, 0.0).astype(BF16)
    each = dot(table.astype(F32).astype(BF16), pick)
    shape = (n, keys)
    chain_keys = jnp.sum(
        jnp.where(iota(shape, 1) // tokens == iota(shape, 0), each, 0.0), axis=0, keepdims=True
    )
    own_row = table_row(table, me)
    shape = (tokens * HEADS, TABLE)
    mine = iota(shape, 1) == CHAIN + iota(shape, 0) // HEADS
    chain_rows = jnp.sum(jnp.where(mine, own_row, 0), axis=1, keepdims=True).astype(F32)
    shape = (tokens * HEADS, HEADS)
    mine = iota(shape, 1) == iota(shape, 0) % HEADS
    weight = jnp.sum(jnp.where(mine, chain_weight_ref[...], 0.0), axis=1, keepdims=True)
    biased_ref[...] = bias_ref[...] + jnp.where(chain_rows == chain_keys, weight, 0.0)
    rows = own_ref.shape[0]
    counts = jnp.where(iota(table.shape, 1) < COUNT + tokens, table, 0).astype(F32)
    shape = (TABLE, tokens)
    ahead = jnp.where(iota(shape, 0) < COUNT + iota(shape, 1), 1.0, 0.0).astype(BF16)
    starts = dot(counts.astype(BF16), ahead)
    atom = (iota((rows, tokens), 0) + me * rows).astype(F32)
    for step, ref in ((-1, before_ref), (0, own_ref), (1, after_ref)):
        at = iota(starts.shape, 0) == me + step
        begin = jnp.sum(jnp.where(at, starts, 0.0), axis=0, keepdims=True)
        begin = begin + atoms_before(table, me + step, tokens).astype(F32)
        size = jnp.sum(jnp.where(at, counts[:, COUNT : COUNT + tokens], 0.0), axis=0, keepdims=True)
        ref[...] = jnp.where((atom >= begin) & (atom < begin + size), 1.0, 0.0).astype(BF16)


def attend_kernel(
    mine_ref, other_ref, query_ref, biased_ref, gate_ref, state_ref, wv_ref, out_ref, back_ref,
    tokens_ref, result_ref,
):
    even = lax.rem(lax.axis_index("row"), 2) == 0
    tokens = state_ref.shape[0]
    chips = mine_ref.shape[0]
    mine, other = mine_ref[...], other_ref[...]
    first = jnp.where(even, mine, other)
    second = jnp.where(even, other, mine)
    normed = jnp.concatenate(
        [part[c] for c in range(chips) for part in (first, second)], axis=0
    )
    scores = dot_nt(query_ref[...], normed) * (1.0 / math.sqrt(HDIM)) + biased_ref[...]
    values = dot(normed, wv_ref[...]).astype(BF16)
    weights = jnp.exp(scores - jnp.max(scores, axis=-1, keepdims=True))
    denom = jnp.sum(weights, axis=-1, keepdims=True)
    mixed = dot(weights.astype(BF16), values) / denom
    head = iota((HEADS, CS), 1) // HDIM == iota((HEADS, CS), 0)
    mixed = jnp.concatenate(
        [
            jnp.sum(
                jnp.where(head, mixed[t * HEADS : (t + 1) * HEADS], 0.0), axis=0, keepdims=True
            )
            for t in range(tokens)
        ],
        axis=0,
    )
    gated = (mixed * gate_ref[...]).astype(BF16)
    updated = (state_ref[...] + dot(gated, out_ref[...])).astype(BF16)
    tokens_ref[...] = updated
    result_ref[...] = dot(updated, back_ref[...]).astype(BF16)


def spread_kernel(mid_ref, back_ref, core_ref, far_ref, before_ref, own_ref, after_ref, atoms_ref):
    even = lax.rem(lax.axis_index("row"), 2) == 0
    core, far = core_ref[...], far_ref[...]
    total = dot(before_ref[...], jnp.where(even, far, core))
    total = total + dot(own_ref[...], back_ref[...])
    total = total + dot(after_ref[...], jnp.where(even, core, far))
    atoms_ref[...] = (mid_ref[...].astype(F32) + total).astype(BF16)


def call(kernel, outs, *args):
    return pl.pallas_call(
        kernel,
        out_shape=outs,
        in_specs=[pl.BlockSpec(memory_space=pltpu.VMEM)] * len(args),
        out_specs=jax.tree.map(lambda _: pl.BlockSpec(memory_space=pltpu.VMEM), outs),
        compiler_params=pltpu.CompilerParams(vmem_limit_bytes=VMEM_LIMIT),
    )(*args)


def shape_of(shape, dtype):
    return jax.ShapeDtypeStruct(shape, dtype)


def shards(
    atom_feat,
    window_start,
    atom_count,
    residue_type,
    chain_id,
    token_single,
    pair,
    atom_gain,
    atom_qkv,
    atom_out,
    pool_weight,
    restype_table,
    token_gain,
    token_proj,
    token_out,
    pair_gain,
    pair_bias_weight,
    chain_weight,
    back_weight,
):
    n = lax.axis_size("row")
    rows, tokens, extent = atom_feat.shape[0], token_single.shape[0], pair.shape[1]
    cores = [(i, i ^ 1) for i in range(n)]
    far = [(i, i + 1) for i in range(1, n - 1, 2)] + [(i + 1, i) for i in range(1, n - 1, 2)]
    same_core = [[2 * c + core for c in range(n // 2)] for core in range(2)]

    feat_far = lax.ppermute(atom_feat, "row", far)
    feat_core = lax.ppermute(atom_feat, "row", cores)
    ints = jnp.concatenate([atom_count, chain_id, residue_type, window_start])
    ints = jnp.pad(ints, (0, TABLE - ints.shape[0]))
    table = lax.all_to_all(jnp.broadcast_to(ints[None], (n, TABLE)), "row", 0, 0, tiled=True)

    bias = call(
        pair_kernel,
        shape_of((tokens * HEADS, extent), F32),
        pair,
        pair_gain[None],
        pair_bias_weight.T,
    )
    mid, state, normed = call(
        functools.partial(atom_kernel, n),
        (
            shape_of((rows, CA), BF16),
            shape_of((tokens, CS), F32),
            shape_of((n // 2, tokens, CS), BF16),
        ),
        atom_feat,
        feat_core,
        feat_far,
        table,
        token_single,
        atom_gain[None],
        atom_qkv,
        atom_out,
        pool_weight,
        restype_table,
        token_gain[None],
    )
    mine = lax.all_to_all(normed, "row", 0, 0, tiled=True, axis_index_groups=same_core)
    other = lax.ppermute(mine, "row", cores)
    pick = shape_of((rows, tokens), BF16)
    query, gate, biased, before, own, after = call(
        query_kernel,
        (
            shape_of((tokens * HEADS, CS), BF16),
            shape_of((tokens, CS), F32),
            shape_of((tokens * HEADS, extent), F32),
            pick,
            pick,
            pick,
        ),
        normed,
        table,
        bias,
        chain_weight[None],
        token_proj[:, :CS],
        token_proj[:, CS : 2 * CS],
        token_proj[:, 3 * CS :],
    )
    tokens_out, back = call(
        attend_kernel,
        (shape_of((tokens, CS), BF16), shape_of((tokens, CA), BF16)),
        mine,
        other,
        query,
        biased,
        gate,
        state,
        token_proj[:, 2 * CS : 3 * CS],
        token_out,
        back_weight,
    )
    back_far = lax.ppermute(back, "row", far)
    back_core = lax.ppermute(back, "row", cores)
    atoms_out = call(
        spread_kernel, shape_of((rows, CA), BF16),
        mid, back, back_core, back_far, before, own, after,
    )
    return (atoms_out, tokens_out)


def solution(mesh):
    split = P(("groups", "row"), None)
    line = P(("groups", "row"))
    return jax.shard_map(
        shards,
        mesh=mesh,
        in_specs=(split, line, line, line, line, split, P(("groups", "row"), None, None))
        + (P(),) * 12,
        out_specs=(split, split),
        check_vma=False,
    )
```

time: 108 us -> 51.4 us (0.48)
  blocking collectives: 28.4 us -> 0 us
  local copies, waits for them, and re-layouts: 32.7 us -> 10.9 us
  matrix products: 12.8 us -> 0 us
  Pallas kernels: 0 us -> 9.33 us
  other arithmetic: 6.81 us -> 0.78 us
  waiting for transfers between devices: 5.64 us -> 10.5 us
    gather x33 -> x0, local copies, waits for them, and re-layouts: 27.5 us -> none  [the longest x9 17.5 us: shards(): jnp.searchsorted(ends, first_atom + jnp.arange(atom_rows, dtype=jnp.int32...]
    all_gather x1 -> x0, blocking collectives: 18.6 us -> none  [shards(): lax.all_gather(token_normed, 'row', axis=0, tiled=True)]
    dot_general x14 -> x0, matrix products: 12.8 us -> none  [the longest x1 3.06 us: shards(): jnp.dot(token_normed, token_proj, preferred_element_type=jnp.float32)]
    unnamed x1 -> x0, blocking collectives: 9.8 us -> none
    pallas_call x0 -> x5, Pallas kernels: none -> 9.33 us  [call(): pl.pallas_call(kernel, out_shape=outs, in_specs=[pl.BlockSpec(memory_spac...]
    ppermute x6 -> x5, starting transfers between devices: 18.7 us -> 9.85 us  [the longest x1 4.63 us: shards(): feat_far = lax.ppermute(atom_feat, 'row', far)]
    all_to_all x0 -> x2, waiting for transfers between devices: none -> 8.59 us  [the longest x1 5.02 us: shards(): lax.all_to_all(jnp.broadcast_to(ints[None], (n, TABLE)), 'row', 0, 0, til...]
    all_to_all x0 -> x2, starting transfers between devices: none -> 8.57 us  [the longest x1 5.18 us: shards(): lax.all_to_all(jnp.broadcast_to(ints[None], (n, TABLE)), 'row', 0, 0, til...]
  transfers between devices with their start and end apart: 6 -> 7, of which waited for: 2 -> 3; matrix products, arithmetic and copies ran while one was open for 25% -> 9% of each run, Pallas kernels for 0% -> 7%
where the time goes in v1:
time: 51.4 us; the launch traced here: 50.8 us
  starting transfers between devices  18.4 us (36%)
  local copies, waits for them, and re-layouts  10.9 us (21%)
  waiting for transfers between devices  10.5 us (20%)
  Pallas kernels  9.33 us (18%)
  other arithmetic  0.78 us (2%)
  between operations  0.77 us (1%)
    pallas_call x5, Pallas kernels, call(): pl.pallas_call(kernel, out_shape=outs, in_specs=[pl.BlockSpec(memory_spac...  9.33 us
    unnamed x26, local copies, waits for them, and re-layouts  6.96 us
    all_to_all x1, starting transfers between devices, shards(): lax.all_to_all(jnp.broadcast_to(ints[None], (n, TABLE)), 'row', 0, 0, til...  5.18 us
    all_to_all x1, waiting for transfers between devices, shards(): lax.all_to_all(jnp.broadcast_to(ints[None], (n, TABLE)), 'row', 0, 0, til...  5.02 us
    ppermute x1, starting transfers between devices, shards(): feat_far = lax.ppermute(atom_feat, 'row', far)  4.63 us
    all_to_all x1, waiting for transfers between devices, shards(): lax.all_to_all(normed, 'row', 0, 0, tiled=True, axis_index_groups=same_core)  3.57 us
    all_to_all x1, starting transfers between devices, shards(): lax.all_to_all(normed, 'row', 0, 0, tiled=True, axis_index_groups=same_core)  3.39 us
    ppermute x1, starting transfers between devices, shards(): back_far = lax.ppermute(back, 'row', far)  2.96 us
  transfers between devices with their start and end apart: 7, of which 3 were waited for; matrix products, arithmetic and copies ran while one was open for 9% of the time, Pallas kernels for 7%

profile of v1, /device:TPU:1, one launch (start us, length us, event | category | flops | bytes accessed | tf_op | source)
XLA Modules:
  0.0 50.8 jit_solution(16730502913790726251)
XLA Ops:
  0.6 0.0 copy-start.1
  0.6 0.1 collective-permute-start
  0.8 4.6 %collective-permute-start.1 = (bf16[256,128]{1,0:T(8,128)(2,1)}, bf16[256,128]{1,0:T(8,128)(2,1)S(1)}, u32[]{:S(2)}, u32[]{:S(2)}) collective-permute-start(bf16[256,128]{1,0:T(8,128)(2,1)} %feat_ref.1), channel_id=1, source_target_pairs={{1,2},{3,4},{5,6},{7,8},{9,10},{11,12},{13,14},{2,1},{4,3},{6,5},{... | collective-permute-start | bytes 196616 | tf_op jit(solution)/shard_map/ppermute | solution.py:293
  5.4 0.8 %pad_add_fusion = s32[56]{0:T(128)S(1)} fusion(s32[8]{0:T(128)} %param.20, s32[16]{0:T(128)} %param.22, s32[16]{0:T(128)} %param.23, s32[16]{0:T(128)} %param.21), kind=kLoop, calls=%fused_computation | loop fusion | flops 168 | bytes 448 | tf_op jit(solution)/shard_map/concatenate | solution.py:295
  6.2 0.6 %broadcast_in_dim.18 = s32[16,1,128]{2,1,0:T(1,128)} broadcast(s32[128]{0:T(128)S(1)} %pad.4), dimensions={2} | broadcast | bytes 8704 | tf_op jit(solution)/shard_map/broadcast_in_dim | solution.py:297
  6.8 5.2 %all-to-all-start = ((s32[16,1,128]{2,1,0:T(1,128)}), s32[16,1,128]{2,1,0:T(1,128)S(1)}, u32[]{:S(2)}, u32[]{:S(2)}) async-start(s32[16,1,128]{2,1,0:T(1,128)} %broadcast_in_dim.18), calls=%async_computation | async-start | bytes 16384 | tf_op jit(solution)/shard_map/all_to_all | solution.py:297
  12.0 0.7 %broadcast_in_dim.20.token_gain_ref = f32[1,768]{1,0:T(1,128)S(1)} reshape(f32[768]{0:T(1024)} %param.31) | data formatting | bytes 6144 | tf_op jit(solution)/shard_map/broadcast_in_dim | solution.py:323
  12.7 5.0 %all-to-all-done = s32[16,1,128]{2,1,0:T(1,128)S(1)} async-done(((s32[16,1,128]{2,1,0:T(1,128)}), s32[16,1,128]{2,1,0:T(1,128)S(1)}, u32[]{:S(2)}, u32[]{:S(2)}) %all-to-all-start) | async-done | bytes 8224 | tf_op jit(solution)/shard_map/all_to_all | solution.py:297
  17.7 0.0 collective-permute-done.core_ref
  17.7 0.0 collective-permute-done.1.far_ref
  17.7 0.0 copy-start.3
  17.7 0.9 %copy-done.3 = bf16[128,768]{1,0:T(8,128)(2,1)S(1)} copy-done((bf16[128,768]{1,0:T(8,128)(2,1)S(1)}, bf16[128,768]{1,0:T(8,128)(2,1)}, u32[]{:S(2)}) %copy-start.3) | copy-done | bytes 196632
  18.6 0.0 copy-start.4
  18.6 0.9 %copy-done.4 = bf16[128,384]{1,0:T(8,128)(2,1)S(1)} copy-done((bf16[128,384]{1,0:T(8,128)(2,1)S(1)}, bf16[128,384]{1,0:T(8,128)(2,1)}, u32[]{:S(2)}) %copy-start.4) | copy-done | bytes 98328
  19.5 0.0 copy-start.5
  19.5 0.8 %copy-done.5 = bf16[256,128]{1,0:T(8,128)(2,1)S(1)} copy-done((bf16[256,128]{1,0:T(8,128)(2,1)S(1)}, bf16[256,128]{1,0:T(8,128)(2,1)}, u32[]{:S(2)}) %copy-start.5) | copy-done | bytes 65560
  20.4 0.0 copy-start.6
  20.4 0.8 %copy-done.6 = bf16[32,768]{1,0:T(8,128)(2,1)S(1)} copy-done((bf16[32,768]{1,0:T(8,128)(2,1)S(1)}, bf16[32,768]{1,0:T(8,128)(2,1)}, u32[]{:S(2)}) %copy-start.6) | copy-done | bytes 49176
  21.2 0.0 copy-start.7
  21.2 0.8 %copy-done.7 = bf16[128,128]{1,0:T(8,128)(2,1)S(1)} copy-done((bf16[128,128]{1,0:T(8,128)(2,1)S(1)}, bf16[128,128]{1,0:T(8,128)(2,1)}, u32[]{:S(2)}) %copy-start.7) | copy-done | bytes 32792
  21.9 0.0 copy-start.8
  21.9 0.7 %copy-done.8 = bf16[16,768]{1,0:T(8,128)(2,1)S(1)} copy-done((bf16[16,768]{1,0:T(8,128)(2,1)S(1)}, bf16[16,768]{1,0:T(8,128)(2,1)}, u32[]{:S(2)}) %copy-start.8) | copy-done | bytes 24600
  22.7 0.0 copy-start.12
  22.7 0.7 %copy-done.12 = f32[128]{0:T(128)S(1)} copy-done((f32[128]{0:T(128)S(1)}, f32[128]{0:T(128)}, u32[]{:S(2)}) %copy-start.12) | copy-done | bytes 536
  23.3 3.1 %shard_map.194 = (bf16[256,128]{1,0:T(8,128)(2,1)S(1)}, f32[16,768]{1,0:T(8,128)S(1)}, bf16[8,16,768]{2,1,0:T(8,128)(2,1)}) custom-call(bf16[256,128]{1,0:T(8,128)(2,1)S(1)} %copy-done.5, bf16[256,128]{1,0:T(8,128)(2,1)S(1)} %collective-permute-done.core_ref, bf16[256,128]{1,0:T(8,128)(2,1)S(1)} %collective-permute-done.1.far_ref, s32[16,128]{1,0:T(8,128)S(1)} %bitcast.5, ...), custom_call_target="tpu_custom_call" | custom-call | tf_op jit(solution)/shard_map/pallas_call | solution.py:253
  26.4 3.4 %all-to-all-start.1 = ((bf16[8,16,768]{2,1,0:T(8,128)(2,1)}), bf16[8,16,768]{2,1,0:T(8,128)(2,1)S(1)}, u32[]{:S(2)}, u32[]{:S(2)}) async-start(bf16[8,16,768]{2,1,0:T(8,128)(2,1)} %get-tuple-element.14.normed_ref), calls=%async_computation.1 | async-start | bytes 393216 | tf_op jit(solution)/shard_map/all_to_all | solution.py:325
  29.8 0.0 copy-done.1
  29.8 0.0 copy-start.9
  29.8 0.7 %copy-done.9 = bf16[128,16]{0,1:T(8,128)(2,1)S(1)} copy-done((bf16[128,16]{0,1:T(8,128)(2,1)S(1)}, bf16[128,16]{0,1:T(8,128)(2,1)}, u32[]{:S(2)}) %copy-start.9) | copy-done | bytes 4120
  30.5 0.0 copy-start.10
  30.5 0.7 %copy-done.10 = f32[128]{0:T(128)S(1)} copy-done((f32[128]{0:T(128)S(1)}, f32[128]{0:T(128)}, u32[]{:S(2)}) %copy-start.10) | copy-done | bytes 536
  31.1 1.8 %shard_map.195.bias_ref = f32[256,256]{1,0:T(8,128)S(1)} custom-call(bf16[16,256,128]{2,1,0:T(8,128)(2,1)S(1)} %copy-done.1, f32[1,128]{1,0:T(1,128)S(1)} %bitcast.8, bf16[16,128]{1,0:T(8,128)(2,1)S(1)} %bitcast.7), custom_call_target="tpu_custom_call" | custom-call | tf_op jit(solution)/shard_map/pallas_call | solution.py:253
  32.9 0.0 copy-start.11
  32.9 3.6 %all-to-all-done.1.mine_ref = bf16[8,16,768]{2,1,0:T(8,128)(2,1)S(1)} async-done(((bf16[8,16,768]{2,1,0:T(8,128)(2,1)}), bf16[8,16,768]{2,1,0:T(8,128)(2,1)S(1)}, u32[]{:S(2)}, u32[]{:S(2)}) %all-to-all-start.1) | async-done | bytes 196640 | tf_op jit(solution)/shard_map/all_to_all | solution.py:325
  36.5 2.1 %collective-permute-start.2 = (bf16[8,16,768]{2,1,0:T(8,128)(2,1)S(1)}, bf16[8,16,768]{2,1,0:T(8,128)(2,1)S(1)}, u32[]{:S(2)}, u32[]{:S(2)}) collective-permute-start(bf16[8,16,768]{2,1,0:T(8,128)(2,1)S(1)} %all-to-all-done.1.mine_ref), channel_id=1, source_target_pairs={{0,1},{1,0},{2,3},{3,2},{4,5},{5,4},{6,7},{7,6},{8,9},{9,8},{10,11... | collective-permute-start | bytes 589832 | tf_op jit(solution)/shard_map/ppermute | solution.py:326
  38.6 2.7 %fusion = (bf16[768,768]{1,0:T(8,128)(2,1)S(1)}, bf16[768,768]{1,0:T(8,128)(2,1)S(1)}, bf16[768,768]{1,0:T(8,128)(2,1)S(1)}, bf16[768,768]{1,0:T(8,128)(2,1)S(1)}) fusion(bf16[768,3072]{1,0:T(8,128)(2,1)} %param.32), kind=kLoop, calls=%fused_computation.1 | loop fusion | bytes 9437184 | tf_op jit(solution)/shard_map/slice | solution.py:355
  41.3 0.0 copy-done.11
  41.3 0.0 copy-start
  41.3 0.0 copy-start.2
  41.3 2.0 %shard_map.196 = (bf16[256,768]{1,0:T(8,128)(2,1)S(1)}, f32[16,768]{1,0:T(8,128)S(1)}, f32[256,256]{1,0:T(8,128)S(1)}, bf16[256,16]{1,0:T(8,128)(2,1)S(1)}, bf16...) custom-call(bf16[8,16,768]{2,1,0:T(8,128)(2,1)} %get-tuple-element.14.normed_ref, s32[16,128]{1,0:T(8,128)S(1)} %bitcast.6, ...), custom_call_target="tpu_custom_call" | custom-call | tf_op jit(solution)/shard_map/pallas_call | solution.py:253
  43.3 0.0 collective-permute-done.2.other_ref
  43.3 0.0 copy-done
  43.3 0.0 copy-done.2
  43.3 1.7 %shard_map.197 = (bf16[16,768]{1,0:T(8,128)(2,1)}, bf16[16,128]{1,0:T(8,128)(2,1)S(1)}) custom-call(bf16[8,16,768]{2,1,0:T(8,128)(2,1)S(1)} %all-to-all-done.1.mine_ref, bf16[8,16,768]{2,1,0:T(8,128)(2,1)S(1)} %collective-permute-done.2.other_ref, bf16[256,768]{1,0:T(8,128)(2,1)S(1)} %get-tuple-element.15.query_ref, ...), custom_call_target="tpu_custom_call" | custom-call | tf_op jit(solution)/shard_map/pallas_call | solution.py:253
  45.0 0.0 collective-permute-start.3
  45.0 3.0 %collective-permute-start.4 = (bf16[16,128]{1,0:T(8,128)(2,1)S(1)}, bf16[16,128]{1,0:T(8,128)(2,1)S(1)}, u32[]{:S(2)}, u32[]{:S(2)}) collective-permute-start(bf16[16,128]{1,0:T(8,128)(2,1)S(1)} %get-tuple-element.19.back_ref), channel_id=1, source_target_pairs={{1,2},{3,4},{5,6},{7,8},{9,10},{11,12},{13,14},{2,1},{4,3},{6,5},{... | collective-permute-start | bytes 12296 | tf_op jit(solution)/shard_map/ppermute | solution.py:359
  48.0 0.0 collective-permute-done.3.core_ref
  48.0 1.9 %collective-permute-done.4.far_ref = bf16[16,128]{1,0:T(8,128)(2,1)S(1)} collective-permute-done((bf16[16,128]{1,0:T(8,128)(2,1)S(1)}, bf16[16,128]{1,0:T(8,128)(2,1)S(1)}, u32[]{:S(2)}, u32[]{:S(2)}) %collective-permute-start.4) | collective-permute-done | bytes 4128 | tf_op jit(solution)/shard_map/ppermute | solution.py:359
  49.9 0.8 %shard_map.198 = bf16[256,128]{1,0:T(8,128)(2,1)} custom-call(bf16[256,128]{1,0:T(8,128)(2,1)S(1)} %get-tuple-element.13.mid_ref, bf16[16,128]{1,0:T(8,128)(2,1)S(1)} %get-tuple-element.19.back_ref, bf16[16,128]{1,0:T(8,128)(2,1)S(1)} %collective-permute-done.3.core_ref, bf16[16,128]{1,0:T(8,128)(2,1)S(1)} %collective-permute-done.4.far_ref, ...), custom_call_target="tpu_custom_call" | custom-call | tf_op jit(solution)/shard_map/pallas_call | solution.py:253
  (1 shorter events, 0.0 us)
Async XLA Ops:
  0.6 29.1 %copy-start.1 = (bf16[16,256,128]{2,1,0:T(8,128)(2,1)S(1)}, bf16[16,256,128]{2,1,0:T(8,128)(2,1)}, u32[]{:S(2)}) copy-start(bf16[16,256,128]{2,1,0:T(8,128)(2,1)} %pair_ref.1) | copy-start | bytes 3145732
  0.6 17.1 %collective-permute-start = (bf16[256,128]{1,0:T(8,128)(2,1)}, bf16[256,128]{1,0:T(8,128)(2,1)S(1)}, u32[]{:S(2)}, u32[]{:S(2)}) collective-permute-start(bf16[256,128]{1,0:T(8,128)(2,1)} %feat_ref.1), channel_id=1, source_target_pairs={{0,1},{1,0},{2,3},{3,2},{4,5},{5,4},{6,7},{7,6},{8,9},{9,8},{10,11... | collective-permute-start | bytes 196616 | tf_op jit(solution)/shard_map/ppermute | solution.py:294
  0.8 16.9 %collective-permute-start.1 = (bf16[256,128]{1,0:T(8,128)(2,1)}, bf16[256,128]{1,0:T(8,128)(2,1)S(1)}, u32[]{:S(2)}, u32[]{:S(2)}) collective-permute-start(bf16[256,128]{1,0:T(8,128)(2,1)} %feat_ref.1), channel_id=1, source_target_pairs={{1,2},{3,4},{5,6},{7,8},{9,10},{11,12},{13,14},{2,1},{4,3},{6,5},{... | collective-permute-start | bytes 196616 | tf_op jit(solution)/shard_map/ppermute | solution.py:293
  6.8 10.9 %all-to-all-start = ((s32[16,1,128]{2,1,0:T(1,128)}), s32[16,1,128]{2,1,0:T(1,128)S(1)}, u32[]{:S(2)}, u32[]{:S(2)}) async-start(s32[16,1,128]{2,1,0:T(1,128)} %broadcast_in_dim.18), calls=%async_computation | async-start | bytes 16384 | tf_op jit(solution)/shard_map/all_to_all | solution.py:297
  17.7 0.9 %copy-start.3 = (bf16[128,768]{1,0:T(8,128)(2,1)S(1)}, bf16[128,768]{1,0:T(8,128)(2,1)}, u32[]{:S(2)}) copy-start(bf16[128,768]{1,0:T(8,128)(2,1)} %pool_ref.1) | copy-start | bytes 589828
  18.6 0.9 %copy-start.4 = (bf16[128,384]{1,0:T(8,128)(2,1)S(1)}, bf16[128,384]{1,0:T(8,128)(2,1)}, u32[]{:S(2)}) copy-start(bf16[128,384]{1,0:T(8,128)(2,1)} %qkv_ref.1) | copy-start | bytes 294916
  19.5 0.8 %copy-start.5 = (bf16[256,128]{1,0:T(8,128)(2,1)S(1)}, bf16[256,128]{1,0:T(8,128)(2,1)}, u32[]{:S(2)}) copy-start(bf16[256,128]{1,0:T(8,128)(2,1)} %feat_ref.1) | copy-start | bytes 196612
  20.4 0.8 %copy-start.6 = (bf16[32,768]{1,0:T(8,128)(2,1)S(1)}, bf16[32,768]{1,0:T(8,128)(2,1)}, u32[]{:S(2)}) copy-start(bf16[32,768]{1,0:T(8,128)(2,1)} %restype_ref.1) | copy-start | bytes 147460
  21.2 0.8 %copy-start.7 = (bf16[128,128]{1,0:T(8,128)(2,1)S(1)}, bf16[128,128]{1,0:T(8,128)(2,1)}, u32[]{:S(2)}) copy-start(bf16[128,128]{1,0:T(8,128)(2,1)} %out_ref.2) | copy-start | bytes 98308
  21.9 0.7 %copy-start.8 = (bf16[16,768]{1,0:T(8,128)(2,1)S(1)}, bf16[16,768]{1,0:T(8,128)(2,1)}, u32[]{:S(2)}) copy-start(bf16[16,768]{1,0:T(8,128)(2,1)} %single_ref.1) | copy-start | bytes 73732
  22.7 0.7 %copy-start.12 = (f32[128]{0:T(128)S(1)}, f32[128]{0:T(128)}, u32[]{:S(2)}) copy-start(f32[128]{0:T(128)} %param.26) | copy-start | bytes 1540
  26.4 10.1 %all-to-all-start.1 = ((bf16[8,16,768]{2,1,0:T(8,128)(2,1)}), bf16[8,16,768]{2,1,0:T(8,128)(2,1)S(1)}, u32[]{:S(2)}, u32[]{:S(2)}) async-start(bf16[8,16,768]{2,1,0:T(8,128)(2,1)} %get-tuple-element.14.normed_ref), calls=%async_computation.1 | async-start | bytes 393216 | tf_op jit(solution)/shard_map/all_to_all | solution.py:325
  29.8 0.7 %copy-start.9 = (bf16[128,16]{0,1:T(8,128)(2,1)S(1)}, bf16[128,16]{0,1:T(8,128)(2,1)}, u32[]{:S(2)}) copy-start(bf16[128,16]{0,1:T(8,128)(2,1)} %param.35) | copy-start | bytes 12292
  30.5 0.7 %copy-start.10 = (f32[128]{0:T(128)S(1)}, f32[128]{0:T(128)}, u32[]{:S(2)}) copy-start(f32[128]{0:T(128)} %param.34) | copy-start | bytes 1540
  32.9 8.4 %copy-start.11 = (f32[16]{0:T(128)S(1)}, f32[16]{0:T(128)}, u32[]{:S(2)}) copy-start(f32[16]{0:T(128)} %param.36) | copy-start | bytes 196
  36.5 6.8 %collective-permute-start.2 = (bf16[8,16,768]{2,1,0:T(8,128)(2,1)S(1)}, bf16[8,16,768]{2,1,0:T(8,128)(2,1)S(1)}, u32[]{:S(2)}, u32[]{:S(2)}) collective-permute-start(bf16[8,16,768]{2,1,0:T(8,128)(2,1)S(1)} %all-to-all-done.1.mine_ref), channel_id=1, source_target_pairs={{0,1},{1,0},{2,3},{3,2},{4,5},{5,4},{6,7},{7,6},{8,9},{9,8},{10,11... | collective-permute-start | bytes 589832 | tf_op jit(solution)/shard_map/ppermute | solution.py:326
  41.3 2.0 %copy-start = (bf16[768,768]{1,0:T(8,128)(2,1)S(1)}, bf16[768,768]{1,0:T(8,128)(2,1)}, u32[]{:S(2)}) copy-start(bf16[768,768]{1,0:T(8,128)(2,1)} %out_ref.3) | copy-start | bytes 3538948
  41.3 2.0 %copy-start.2 = (bf16[768,128]{1,0:T(8,128)(2,1)S(1)}, bf16[768,128]{1,0:T(8,128)(2,1)}, u32[]{:S(2)}) copy-start(bf16[768,128]{1,0:T(8,128)(2,1)} %back_ref.1) | copy-start | bytes 589828
  45.0 3.0 %collective-permute-start.3 = (bf16[16,128]{1,0:T(8,128)(2,1)S(1)}, bf16[16,128]{1,0:T(8,128)(2,1)S(1)}, u32[]{:S(2)}, u32[]{:S(2)}) collective-permute-start(bf16[16,128]{1,0:T(8,128)(2,1)S(1)} %get-tuple-element.19.back_ref), channel_id=1, source_target_pairs={{0,1},{1,0},{2,3},{3,2},{4,5},{5,4},{6,7},{7,6},{8,9},{9,8},{10,11... | collective-permute-start | bytes 12296 | tf_op jit(solution)/shard_map/ppermute | solution.py:360
  45.0 4.9 %collective-permute-start.4 = (bf16[16,128]{1,0:T(8,128)(2,1)S(1)}, bf16[16,128]{1,0:T(8,128)(2,1)S(1)}, u32[]{:S(2)}, u32[]{:S(2)}) collective-permute-start(bf16[16,128]{1,0:T(8,128)(2,1)S(1)} %get-tuple-element.19.back_ref), channel_id=1, source_target_pairs={{1,2},{3,4},{5,6},{7,8},{9,10},{11,12},{13,14},{2,1},{4,3},{6,5},{... | collective-permute-start | bytes 12296 | tf_op jit(solution)/shard_map/ppermute | solution.py:359

commit v2 on v1

--- a/solution.py
+++ b/solution.py
@@ -19,12 +19,11 @@
 ADIM = 32
 HALF = 128
 REACH = 64
+COST = 2_000_000_000
 EPS = 1e-05
 NEG = -1e30
 F32 = jnp.float32
 BF16 = jnp.bfloat16
-VMEM_LIMIT = 24 * 1024 * 1024
-
 COUNT, CHAIN, RES, WIN = 0, 16, 32, 48
 TABLE = 128
 
@@ -59,6 +58,10 @@
 def atoms_before(table, row, tokens):
     keep = (iota(table.shape, 0) < row) & (iota(table.shape, 1) < COUNT + tokens)
     return jnp.sum(jnp.sum(jnp.where(keep, table, 0), axis=0, keepdims=True), axis=1, keepdims=True)
+
+
+def table_kernel(row_ref, table_ref):
+    table_ref[...] = jnp.broadcast_to(row_ref[...][None], table_ref.shape)
 
 
 def pair_kernel(pair_ref, gain_ref, weight_ref, bias_ref):
@@ -81,6 +84,7 @@
     pool_ref,
     restype_ref,
     token_gain_ref,
+    bias_ref,
     mid_ref,
     state_ref,
     normed_ref,
@@ -157,14 +161,13 @@
 
 
 def query_kernel(
-    normed_ref, table_ref, bias_ref, chain_weight_ref, wq_ref, wk_ref, wg_ref,
-    query_ref, gate_ref, biased_ref, before_ref, own_ref, after_ref,
+    normed_ref, table_ref, bias_ref, chain_weight_ref, proj_ref,
+    query_ref, gate_ref, biased_ref, pick_ref,
 ):
     me = lax.axis_index("row")
     normed = normed_ref[0]
     tokens = normed.shape[0]
-    query = dot(normed, wq_ref[...]).astype(BF16)
-    gate_ref[...] = jax.nn.sigmoid(dot(normed, wg_ref[...]))
+    query = dot(normed, proj_ref[:, :CS]).astype(BF16)
     head = iota((HEADS, CS), 1) // HDIM == iota((HEADS, CS), 0)
     spread = jnp.concatenate(
         [
@@ -173,7 +176,7 @@
         ],
         axis=0,
     ).astype(BF16)
-    query_ref[...] = dot_nt(spread, wk_ref[...]).astype(BF16)
+    query_ref[...] = dot_nt(spread, proj_ref[:, CS : 2 * CS]).astype(BF16)
     table = table_ref[...]
     n = table.shape[0]
     keys = n * tokens
@@ -192,24 +195,33 @@
     mine = iota(shape, 1) == iota(shape, 0) % HEADS
     weight = jnp.sum(jnp.where(mine, chain_weight_ref[...], 0.0), axis=1, keepdims=True)
     biased_ref[...] = bias_ref[...] + jnp.where(chain_rows == chain_keys, weight, 0.0)
-    rows = own_ref.shape[0]
-    counts = jnp.where(iota(table.shape, 1) < COUNT + tokens, table, 0).astype(F32)
-    shape = (TABLE, tokens)
-    ahead = jnp.where(iota(shape, 0) < COUNT + iota(shape, 1), 1.0, 0.0).astype(BF16)
-    starts = dot(counts.astype(BF16), ahead)
-    atom = (iota((rows, tokens), 0) + me * rows).astype(F32)
-    for step, ref in ((-1, before_ref), (0, own_ref), (1, after_ref)):
-        at = iota(starts.shape, 0) == me + step
-        begin = jnp.sum(jnp.where(at, starts, 0.0), axis=0, keepdims=True)
-        begin = begin + atoms_before(table, me + step, tokens).astype(F32)
-        size = jnp.sum(jnp.where(at, counts[:, COUNT : COUNT + tokens], 0.0), axis=0, keepdims=True)
-        ref[...] = jnp.where((atom >= begin) & (atom < begin + size), 1.0, 0.0).astype(BF16)
+    rows = pick_ref.shape[0]
+    counts = jnp.where(iota(table.shape, 1) < COUNT + tokens, table, 0).astype(F32).astype(BF16)
+    begin = jnp.zeros((1, TABLE), F32)
+    size = jnp.zeros((1, TABLE), F32)
+    for step in range(3):
+        shape = (TABLE, TABLE)
+        token = iota(shape, 1) - step * tokens
+        here = (token >= 0) & (token < tokens)
+        ahead = jnp.where(here & (iota(shape, 0) < COUNT + token), 1.0, 0.0).astype(BF16)
+        equal = jnp.where(here & (iota(shape, 0) == COUNT + token), 1.0, 0.0).astype(BF16)
+        at = iota(table.shape, 0) == me + step - 1
+        begin += jnp.sum(jnp.where(at, dot(counts, ahead), 0.0), axis=0, keepdims=True)
+        size += jnp.sum(jnp.where(at, dot(counts, equal), 0.0), axis=0, keepdims=True)
+        before = atoms_before(table, me + step - 1, tokens).astype(F32)
+        begin += jnp.where(here[:1], before, 0.0)
+    atom = (iota((rows, TABLE), 0) + me * rows).astype(F32)
+    pick_ref[...] = jnp.where((atom >= begin) & (atom < begin + size), 1.0, 0.0).astype(BF16)
+    gate_ref[...] = jax.nn.sigmoid(dot(normed, proj_ref[:, 3 * CS :]))
 
 
 def attend_kernel(
-    mine_ref, other_ref, query_ref, biased_ref, gate_ref, state_ref, wv_ref, out_ref, back_ref,
+    mine_ref, other_ref, query_ref, biased_ref, gate_ref, state_ref, out_ref, back_ref, proj_ref,
     tokens_ref, result_ref,
+    wv_ref, sem,
 ):
+    copy = pltpu.make_async_copy(proj_ref.at[:, pl.ds(2 * CS, CS)], wv_ref, sem)
+    copy.start()
     even = lax.rem(lax.axis_index("row"), 2) == 0
     tokens = state_ref.shape[0]
     chips = mine_ref.shape[0]
@@ -220,9 +232,10 @@
         [part[c] for c in range(chips) for part in (first, second)], axis=0
     )
     scores = dot_nt(query_ref[...], normed) * (1.0 / math.sqrt(HDIM)) + biased_ref[...]
-    values = dot(normed, wv_ref[...]).astype(BF16)
     weights = jnp.exp(scores - jnp.max(scores, axis=-1, keepdims=True))
     denom = jnp.sum(weights, axis=-1, keepdims=True)
+    copy.wait()
+    values = dot(normed, wv_ref[...]).astype(BF16)
     mixed = dot(weights.astype(BF16), values) / denom
     head = iota((HEADS, CS), 1) // HDIM == iota((HEADS, CS), 0)
     mixed = jnp.concatenate(
@@ -240,23 +253,26 @@
     result_ref[...] = dot(updated, back_ref[...]).astype(BF16)
 
 
-def spread_kernel(mid_ref, back_ref, core_ref, far_ref, before_ref, own_ref, after_ref, atoms_ref):
+def spread_kernel(mid_ref, back_ref, core_ref, far_ref, pick_ref, atoms_ref):
     even = lax.rem(lax.axis_index("row"), 2) == 0
-    core, far = core_ref[...], far_ref[...]
-    total = dot(before_ref[...], jnp.where(even, far, core))
-    total = total + dot(own_ref[...], back_ref[...])
-    total = total + dot(after_ref[...], jnp.where(even, core, far))
-    atoms_ref[...] = (mid_ref[...].astype(F32) + total).astype(BF16)
-
-
-def call(kernel, outs, *args):
+    core, far, own = core_ref[...], far_ref[...], back_ref[...]
+    rest = jnp.zeros((TABLE - 3 * own.shape[0], CA), BF16)
+    parts = [jnp.where(even, far, core), own, jnp.where(even, core, far), rest]
+    spread = dot(pick_ref[...], jnp.concatenate(parts, axis=0))
+    atoms_ref[...] = (mid_ref[...].astype(F32) + spread).astype(BF16)
+
+
+def call(kernel, outs, *args, hbm=(), limit=24, scratch=()):
+    spec = pl.BlockSpec(memory_space=pltpu.VMEM)
     return pl.pallas_call(
         kernel,
         out_shape=outs,
-        in_specs=[pl.BlockSpec(memory_space=pltpu.VMEM)] * len(args),
-        out_specs=jax.tree.map(lambda _: pl.BlockSpec(memory_space=pltpu.VMEM), outs),
-        compiler_params=pltpu.CompilerParams(vmem_limit_bytes=VMEM_LIMIT),
-    )(*args)
+        in_specs=[spec] * len(args) + [pl.BlockSpec(memory_space=pltpu.HBM)] * len(hbm),
+        out_specs=jax.tree.map(lambda _: spec, outs),
+        scratch_shapes=list(scratch),
+        compiler_params=pltpu.CompilerParams(vmem_limit_bytes=limit * 1024 * 1024),
+        cost_estimate=pl.CostEstimate(flops=COST, bytes_accessed=COST // 200, transcendentals=0),
+    )(*args, *hbm)
 
 
 def shape_of(shape, dtype):
@@ -293,15 +309,12 @@
     feat_far = lax.ppermute(atom_feat, "row", far)
     feat_core = lax.ppermute(atom_feat, "row", cores)
     ints = jnp.concatenate([atom_count, chain_id, residue_type, window_start])
-    ints = jnp.pad(ints, (0, TABLE - ints.shape[0]))
-    table = lax.all_to_all(jnp.broadcast_to(ints[None], (n, TABLE)), "row", 0, 0, tiled=True)
+    ints = jnp.pad(ints, (0, TABLE - ints.shape[0]))[None]
+    table = call(table_kernel, shape_of((n, 1, TABLE), jnp.int32), ints)
+    table = lax.all_to_all(table, "row", 0, 0, tiled=True).reshape(n, TABLE)
 
     bias = call(
-        pair_kernel,
-        shape_of((tokens * HEADS, extent), F32),
-        pair,
-        pair_gain[None],
-        pair_bias_weight.T,
+        pair_kernel, shape_of((tokens * HEADS, extent), F32), pair, pair_gain, pair_bias_weight.T
     )
     mid, state, normed = call(
         functools.partial(atom_kernel, n),
@@ -315,34 +328,31 @@
         feat_far,
         table,
         token_single,
-        atom_gain[None],
+        atom_gain,
         atom_qkv,
         atom_out,
         pool_weight,
         restype_table,
-        token_gain[None],
+        token_gain,
+        bias,
     )
     mine = lax.all_to_all(normed, "row", 0, 0, tiled=True, axis_index_groups=same_core)
-    other = lax.ppermute(mine, "row", cores)
-    pick = shape_of((rows, tokens), BF16)
-    query, gate, biased, before, own, after = call(
+    query, gate, biased, pick = call(
         query_kernel,
         (
             shape_of((tokens * HEADS, CS), BF16),
             shape_of((tokens, CS), F32),
             shape_of((tokens * HEADS, extent), F32),
-            pick,
-            pick,
-            pick,
+            shape_of((rows, TABLE), BF16),
         ),
         normed,
         table,
         bias,
-        chain_weight[None],
-        token_proj[:, :CS],
-        token_proj[:, CS : 2 * CS],
-        token_proj[:, 3 * CS :],
-    )
+        chain_weight,
+        token_proj,
+    )
+    mine, query = lax.optimization_barrier((mine, query))
+    other = lax.ppermute(mine, "row", cores)
     tokens_out, back = call(
         attend_kernel,
         (shape_of((tokens, CS), BF16), shape_of((tokens, CA), BF16)),
@@ -352,15 +362,22 @@
         biased,
         gate,
         state,
-        token_proj[:, 2 * CS : 3 * CS],
         token_out,
         back_weight,
+        hbm=(token_proj,),
+        limit=50,
+        scratch=(pltpu.VMEM((CS, CS), BF16), pltpu.SemaphoreType.DMA),
     )
     back_far = lax.ppermute(back, "row", far)
     back_core = lax.ppermute(back, "row", cores)
     atoms_out = call(
-        spread_kernel, shape_of((rows, CA), BF16),
-        mid, back, back_core, back_far, before, own, after,
+        spread_kernel,
+        shape_of((rows, CA), BF16),
+        mid,
+        back,
+        back_core,
+        back_far,
+        pick,
     )
     return (atoms_out, tokens_out)
 

time: 51.4 us -> 44.4 us (0.86)
  local copies, waits for them, and re-layouts: 10.9 us -> 2.4 us
  Pallas kernels: 9.33 us -> 11.5 us
  waiting for transfers between devices: 10.5 us -> 9.69 us
    unnamed x26 -> x30, local copies, waits for them, and re-layouts: 6.96 us -> 2.4 us
    slice x1 -> x0, local copies, waits for them, and re-layouts: 2.66 us -> none  [shards(): token_proj[:, 2 * CS:3 * CS]]
    pallas_call x5 -> x6, Pallas kernels: 9.33 us -> 11.5 us  [call(): pl.pallas_call(kernel, out_shape=outs, in_specs=[spec] * len(args) + [pl....]
    broadcast_in_dim x2 -> x1, local copies, waits for them, and re-layouts: 1.3 us -> 0.01 us  [shards(): ints = jnp.pad(ints, (0, TABLE - ints.shape[0]))[None]]
    all_to_all x1, waiting for transfers between devices: 5.02 us -> 3.88 us  [shards(): table = lax.all_to_all(table, 'row', 0, 0, tiled=True).reshape(n, TABLE)]
    all_to_all x1, waiting for transfers between devices: 3.57 us -> 2.43 us  [shards(): lax.all_to_all(normed, 'row', 0, 0, tiled=True, axis_index_groups=same_core)]
    ppermute x1, waiting for transfers between devices: 0.01 us -> 1.07 us  [shards(): other = lax.ppermute(mine, 'row', cores)]
  transfers between devices with their start and end apart: 7 -> 7, of which waited for: 3 -> 4; matrix products, arithmetic and copies ran while one was open for 9% -> 2% of each run, Pallas kernels for 7% -> 10%
where the time goes in v2:
time: 44.4 us; the launch traced here: 43.9 us
  starting transfers between devices  18.8 us (42%)
  Pallas kernels  11.5 us (26%)
  waiting for transfers between devices  9.69 us (22%)
  local copies, waits for them, and re-layouts  2.4 us (5%)
  between operations  0.84 us (2%)
  other arithmetic  0.78 us (2%)
    pallas_call x6, Pallas kernels, call(): pl.pallas_call(kernel, out_shape=outs, in_specs=[spec] * len(args) + [pl....  11.5 us
    all_to_all x1, starting transfers between devices, shards(): table = lax.all_to_all(table, 'row', 0, 0, tiled=True).reshape(n, TABLE)  5.33 us
    ppermute x1, starting transfers between devices, shards(): feat_far = lax.ppermute(atom_feat, 'row', far)  4.63 us
    all_to_all x1, waiting for transfers between devices, shards(): table = lax.all_to_all(table, 'row', 0, 0, tiled=True).reshape(n, TABLE)  3.88 us
    all_to_all x1, starting transfers between devices, shards(): lax.all_to_all(normed, 'row', 0, 0, tiled=True, axis_index_groups=same_core)  3.52 us
    ppermute x1, starting transfers between devices, shards(): back_far = lax.ppermute(back, 'row', far)  2.6 us
    all_to_all x1, waiting for transfers between devices, shards(): lax.all_to_all(normed, 'row', 0, 0, tiled=True, axis_index_groups=same_core)  2.43 us
    unnamed x30, local copies, waits for them, and re-layouts  2.4 us
  transfers between devices with their start and end apart: 7, of which 4 were waited for; matrix products, arithmetic and copies ran while one was open for 2% of the time, Pallas kernels for 10%

profile of v2, /device:TPU:1, one launch (start us, length us, event | category | flops | bytes accessed | tf_op | source)
XLA Modules:
  0.0 43.9 jit_solution(17109741800193244572)
XLA Ops:
  0.6 0.0 copy-start.10
  0.6 0.0 copy-start.2
  0.7 0.0 copy-start.12
  0.7 0.1 collective-permute-start
  0.8 4.6 %collective-permute-start.1 = (bf16[256,128]{1,0:T(8,128)(2,1)}, bf16[256,128]{1,0:T(8,128)(2,1)S(1)}, u32[]{:S(2)}, u32[]{:S(2)}) collective-permute-start(bf16[256,128]{1,0:T(8,128)(2,1)} %feat_ref.1), channel_id=1, source_target_pairs={{1,2},{3,4},{5,6},{7,8},{9,10},{11,12},{13,14},{2,1},{4,3},{6,5},{... | collective-permute-start | bytes 196616 | tf_op jit(solution)/shard_map/ppermute | solution.py:309
  5.4 0.8 %pad_add_fusion = s32[56]{0:T(128)S(1)} fusion(s32[8]{0:T(128)} %param.20, s32[16]{0:T(128)} %param.22, s32[16]{0:T(128)} %param.23, s32[16]{0:T(128)} %param.21), kind=kLoop, calls=%fused_computation | loop fusion | flops 168 | bytes 448 | tf_op jit(solution)/shard_map/concatenate | solution.py:311
  6.2 0.6 %shard_map.194 = s32[16,1,128]{2,1,0:T(1,128)} custom-call(s32[1,128]{1,0:T(1,128)S(1)} %pad_bitcast_fusion.row_ref), custom_call_target="tpu_custom_call" | custom-call | flops 2000000000 | bytes 10000000 | tf_op jit(solution)/shard_map/pallas_call | solution.py:267
  6.8 0.0 copy-start.3
  6.8 0.0 copy-start.5
  6.8 0.0 copy-start.6
  6.8 0.0 copy-start.7
  6.8 0.0 copy-start.8
  6.8 0.0 copy-start.9
  6.9 0.0 copy-start.11
  6.9 0.0 copy-start.13
  6.9 5.3 %all-to-all-start = ((s32[16,1,128]{2,1,0:T(1,128)}), s32[16,1,128]{2,1,0:T(1,128)S(1)}, u32[]{:S(2)}, u32[]{:S(2)}) async-start(s32[16,1,128]{2,1,0:T(1,128)} %shard_map.194), calls=%async_computation | async-start | bytes 16384 | tf_op jit(solution)/shard_map/all_to_all | solution.py:314
  12.2 0.0 copy-done.10
  12.2 0.0 copy-done.2
  12.2 0.0 copy-done.12
  12.2 1.8 %shard_map.195.bias_ref = f32[256,256]{1,0:T(8,128)S(1)} custom-call(bf16[16,256,128]{2,1,0:T(8,128)(2,1)S(1)} %copy-done.2, f32[128]{0:T(128)S(1)} %copy-done.12, bf16[16,128]{1,0:T(8,128)(2,1)S(1)} %bitcast.6), custom_call_target="tpu_custom_call" | custom-call | flops 2000000000 | bytes 10000000 | tf_op jit(solution)/shard_map/pallas_call | solution.py:267
  14.0 0.0 copy-start.14
  14.0 3.9 %all-to-all-done = s32[16,1,128]{2,1,0:T(1,128)S(1)} async-done(((s32[16,1,128]{2,1,0:T(1,128)}), s32[16,1,128]{2,1,0:T(1,128)S(1)}, u32[]{:S(2)}, u32[]{:S(2)}) %all-to-all-start) | async-done | bytes 8224 | tf_op jit(solution)/shard_map/all_to_all | solution.py:314
  17.9 0.0 collective-permute-done.core_ref
  17.9 0.0 collective-permute-done.1.far_ref
  17.9 0.0 copy-done.3
  17.9 0.0 copy-done.5
  17.9 0.0 copy-done.6
  17.9 0.0 copy-done.7
  18.0 0.0 copy-done.8
  18.0 0.0 copy-done.9
  18.0 0.0 copy-done.11
  18.0 0.0 copy-done.13
  18.0 0.0 copy-start.1
  18.0 3.1 %shard_map.196 = (bf16[256,128]{1,0:T(8,128)(2,1)S(1)}, f32[16,768]{1,0:T(8,128)S(1)}, bf16[8,16,768]{2,1,0:T(8,128)(2,1)}) custom-call(bf16[256,128]{1,0:T(8,128)(2,1)S(1)} %copy-done.6, bf16[256,128]{1,0:T(8,128)(2,1)S(1)} %collective-permute-done.core_ref, bf16[256,128]{1,0:T(8,128)(2,1)S(1)} %collective-permute-done.1.far_ref, s32[16,128]{1,0:T(8,128)S(1)} %bitcast.4, ...), custom_call_target="tpu_custom_call" | custom-call | flops 2000000000 | bytes 10000000 | tf_op jit(solution)/shard_map/pallas_call | solution.py:267
  21.1 0.0 copy-start.4
  21.1 3.5 %all-to-all-start.1 = ((bf16[8,16,768]{2,1,0:T(8,128)(2,1)}), bf16[8,16,768]{2,1,0:T(8,128)(2,1)S(1)}, u32[]{:S(2)}, u32[]{:S(2)}) async-start(bf16[8,16,768]{2,1,0:T(8,128)(2,1)} %get-tuple-element.14.normed_ref), calls=%async_computation.1 | async-start | bytes 393216 | tf_op jit(solution)/shard_map/all_to_all | solution.py:339
  24.6 0.0 copy-done.14
  24.6 0.0 copy-start
  24.6 2.3 %copy-done = bf16[768,3072]{1,0:T(8,128)(2,1)S(1)} copy-done((bf16[768,3072]{1,0:T(8,128)(2,1)S(1)}, bf16[768,3072]{1,0:T(8,128)(2,1)}, u32[]{:S(2)}) %copy-start) | copy-done | bytes 4718616
  27.0 1.9 %shard_map.197 = (bf16[256,768]{1,0:T(8,128)(2,1)S(1)}, f32[16,768]{1,0:T(8,128)S(1)}, f32[256,256]{1,0:T(8,128)S(1)}, bf16[256,128]{1,0:T(8,128)(2,1)S(1)}) custom-call(bf16[8,16,768]{2,1,0:T(8,128)(2,1)} %get-tuple-element.14.normed_ref, s32[16,128]{1,0:T(8,128)S(1)} %bitcast.5, f32[256,256]{1,0:T(8,128)S(1)} %shard_map.195.bias_ref, f32[16]{0:T(128)S(1)} %copy-done.14, ...), custom_call_target="tpu_custom_call" | custom-call | flops 2000000000 | bytes 10000000 | tf_op jit(solution)/shard_map/pallas_call | solution.py:267
  28.9 2.4 %all-to-all-done.1.mine_ref = bf16[8,16,768]{2,1,0:T(8,128)(2,1)S(1)} async-done(((bf16[8,16,768]{2,1,0:T(8,128)(2,1)}), bf16[8,16,768]{2,1,0:T(8,128)(2,1)S(1)}, u32[]{:S(2)}, u32[]{:S(2)}) %all-to-all-start.1) | async-done | bytes 196640 | tf_op jit(solution)/shard_map/all_to_all | solution.py:339
  31.3 2.1 %collective-permute-start.2 = (bf16[8,16,768]{2,1,0:T(8,128)(2,1)S(1)}, bf16[8,16,768]{2,1,0:T(8,128)(2,1)S(1)}, u32[]{:S(2)}, u32[]{:S(2)}) collective-permute-start(bf16[8,16,768]{2,1,0:T(8,128)(2,1)S(1)} %all-to-all-done.1.mine_ref), channel_id=1, source_target_pairs={{0,1},{1,0},{2,3},{3,2},{4,5},{5,4},{6,7},{7,6},{8,9},{9,8},{10,11... | collective-permute-start | bytes 589832 | tf_op jit(solution)/shard_map/ppermute | solution.py:355
  33.4 1.1 %collective-permute-done.2.other_ref = bf16[8,16,768]{2,1,0:T(8,128)(2,1)S(1)} collective-permute-done((bf16[8,16,768]{2,1,0:T(8,128)(2,1)S(1)}, bf16[8,16,768]{2,1,0:T(8,128)(2,1)S(1)}, u32[]{:S(2)}, u32[]{:S(2)}) %collective-permute-start.2) | collective-permute-done | bytes 196640 | tf_op jit(solution)/shard_map/ppermute | solution.py:355
  34.5 0.0 copy-done.1
  34.5 0.0 copy-done.4
  34.5 3.3 %shard_map.198 = (bf16[16,768]{1,0:T(8,128)(2,1)}, bf16[16,128]{1,0:T(8,128)(2,1)S(1)}) custom-call(bf16[8,16,768]{2,1,0:T(8,128)(2,1)S(1)} %all-to-all-done.1.mine_ref, bf16[8,16,768]{2,1,0:T(8,128)(2,1)S(1)} %collective-permute-done.2.other_ref, bf16[256,768]{1,0:T(8,128)(2,1)S(1)} %get-tuple-element.17.query_ref, ...), custom_call_target="tpu_custom_call" | custom-call | flops 2000000000 | bytes 10000000 | tf_op jit(solution)/shard_map/pallas_call | solution.py:267
  37.8 0.4 collective-permute-start.3
  38.3 2.6 %collective-permute-start.4 = (bf16[16,128]{1,0:T(8,128)(2,1)S(1)}, bf16[16,128]{1,0:T(8,128)(2,1)S(1)}, u32[]{:S(2)}, u32[]{:S(2)}) collective-permute-start(bf16[16,128]{1,0:T(8,128)(2,1)S(1)} %get-tuple-element.21.back_ref), channel_id=1, source_target_pairs={{1,2},{3,4},{5,6},{7,8},{9,10},{11,12},{13,14},{2,1},{4,3},{6,5},{... | collective-permute-start | bytes 12296 | tf_op jit(solution)/shard_map/ppermute | solution.py:371
  40.9 0.0 collective-permute-done.3.core_ref
  40.9 2.3 %collective-permute-done.4.far_ref = bf16[16,128]{1,0:T(8,128)(2,1)S(1)} collective-permute-done((bf16[16,128]{1,0:T(8,128)(2,1)S(1)}, bf16[16,128]{1,0:T(8,128)(2,1)S(1)}, u32[]{:S(2)}, u32[]{:S(2)}) %collective-permute-start.4) | collective-permute-done | bytes 4128 | tf_op jit(solution)/shard_map/ppermute | solution.py:371
  43.2 0.8 %shard_map.199 = bf16[256,128]{1,0:T(8,128)(2,1)} custom-call(bf16[256,128]{1,0:T(8,128)(2,1)S(1)} %get-tuple-element.13.mid_ref, bf16[16,128]{1,0:T(8,128)(2,1)S(1)} %get-tuple-element.21.back_ref, bf16[16,128]{1,0:T(8,128)(2,1)S(1)} %collective-permute-done.3.core_ref, bf16[16,128]{1,0:T(8,128)(2,1)S(1)} %collective-permute-done.4.far_ref, ...), custom_call_target="tpu_custom_call" | custom-call | flops 2000000000 | bytes 10000000 | tf_op jit(solution)/shard_map/pallas_call | solution.py:267
  (1 shorter events, 0.0 us)
Async XLA Ops:
  0.6 11.6 %copy-start.10 = (bf16[128,16]{0,1:T(8,128)(2,1)S(1)}, bf16[128,16]{0,1:T(8,128)(2,1)}, u32[]{:S(2)}) copy-start(bf16[128,16]{0,1:T(8,128)(2,1)} %param.35) | copy-start | bytes 12292
  0.6 11.6 %copy-start.2 = (bf16[16,256,128]{2,1,0:T(8,128)(2,1)S(1)}, bf16[16,256,128]{2,1,0:T(8,128)(2,1)}, u32[]{:S(2)}) copy-start(bf16[16,256,128]{2,1,0:T(8,128)(2,1)} %pair_ref.1) | copy-start | bytes 3145732
  0.7 11.6 %copy-start.12 = (f32[128]{0:T(128)S(1)}, f32[128]{0:T(128)}, u32[]{:S(2)}) copy-start(f32[128]{0:T(128)} %gain_ref.2) | copy-start | bytes 1540
  0.7 17.3 %collective-permute-start = (bf16[256,128]{1,0:T(8,128)(2,1)}, bf16[256,128]{1,0:T(8,128)(2,1)S(1)}, u32[]{:S(2)}, u32[]{:S(2)}) collective-permute-start(bf16[256,128]{1,0:T(8,128)(2,1)} %feat_ref.1), channel_id=1, source_target_pairs={{0,1},{1,0},{2,3},{3,2},{4,5},{5,4},{6,7},{7,6},{8,9},{9,8},{10,11... | collective-permute-start | bytes 196616 | tf_op jit(solution)/shard_map/ppermute | solution.py:310
  0.8 17.1 %collective-permute-start.1 = (bf16[256,128]{1,0:T(8,128)(2,1)}, bf16[256,128]{1,0:T(8,128)(2,1)S(1)}, u32[]{:S(2)}, u32[]{:S(2)}) collective-permute-start(bf16[256,128]{1,0:T(8,128)(2,1)} %feat_ref.1), channel_id=1, source_target_pairs={{1,2},{3,4},{5,6},{7,8},{9,10},{11,12},{13,14},{2,1},{4,3},{6,5},{... | collective-permute-start | bytes 196616 | tf_op jit(solution)/shard_map/ppermute | solution.py:309
  6.8 11.1 %copy-start.3 = (bf16[128,768]{1,0:T(8,128)(2,1)S(1)}, bf16[128,768]{1,0:T(8,128)(2,1)}, u32[]{:S(2)}) copy-start(bf16[128,768]{1,0:T(8,128)(2,1)} %pool_ref.1) | copy-start | bytes 589828
  6.8 11.1 %copy-start.5 = (bf16[128,384]{1,0:T(8,128)(2,1)S(1)}, bf16[128,384]{1,0:T(8,128)(2,1)}, u32[]{:S(2)}) copy-start(bf16[128,384]{1,0:T(8,128)(2,1)} %qkv_ref.1) | copy-start | bytes 294916
  6.8 11.1 %copy-start.6 = (bf16[256,128]{1,0:T(8,128)(2,1)S(1)}, bf16[256,128]{1,0:T(8,128)(2,1)}, u32[]{:S(2)}) copy-start(bf16[256,128]{1,0:T(8,128)(2,1)} %feat_ref.1) | copy-start | bytes 196612
  6.8 11.1 %copy-start.7 = (bf16[32,768]{1,0:T(8,128)(2,1)S(1)}, bf16[32,768]{1,0:T(8,128)(2,1)}, u32[]{:S(2)}) copy-start(bf16[32,768]{1,0:T(8,128)(2,1)} %restype_ref.1) | copy-start | bytes 147460
  6.8 11.1 %copy-start.8 = (bf16[128,128]{1,0:T(8,128)(2,1)S(1)}, bf16[128,128]{1,0:T(8,128)(2,1)}, u32[]{:S(2)}) copy-start(bf16[128,128]{1,0:T(8,128)(2,1)} %out_ref.2) | copy-start | bytes 98308
  6.8 11.1 %copy-start.9 = (bf16[16,768]{1,0:T(8,128)(2,1)S(1)}, bf16[16,768]{1,0:T(8,128)(2,1)}, u32[]{:S(2)}) copy-start(bf16[16,768]{1,0:T(8,128)(2,1)} %single_ref.1) | copy-start | bytes 73732
  6.9 11.1 %copy-start.11 = (f32[768]{0:T(1024)S(1)}, f32[768]{0:T(1024)}, u32[]{:S(2)}) copy-start(f32[768]{0:T(1024)} %token_gain_ref.1) | copy-start | bytes 9220
  6.9 11.1 %copy-start.13 = (f32[128]{0:T(128)S(1)}, f32[128]{0:T(128)}, u32[]{:S(2)}) copy-start(f32[128]{0:T(128)} %gain_ref.3) | copy-start | bytes 1540
  6.9 11.0 %all-to-all-start = ((s32[16,1,128]{2,1,0:T(1,128)}), s32[16,1,128]{2,1,0:T(1,128)S(1)}, u32[]{:S(2)}, u32[]{:S(2)}) async-start(s32[16,1,128]{2,1,0:T(1,128)} %shard_map.194), calls=%async_computation | async-start | bytes 16384 | tf_op jit(solution)/shard_map/all_to_all | solution.py:314
  14.0 10.6 %copy-start.14 = (f32[16]{0:T(128)S(1)}, f32[16]{0:T(128)}, u32[]{:S(2)}) copy-start(f32[16]{0:T(128)} %chain_weight_ref.1) | copy-start | bytes 196
  18.0 16.5 %copy-start.1 = (bf16[768,768]{1,0:T(8,128)(2,1)S(1)}, bf16[768,768]{1,0:T(8,128)(2,1)}, u32[]{:S(2)}) copy-start(bf16[768,768]{1,0:T(8,128)(2,1)} %out_ref.3) | copy-start | bytes 3538948
  21.1 13.5 %copy-start.4 = (bf16[768,128]{1,0:T(8,128)(2,1)S(1)}, bf16[768,128]{1,0:T(8,128)(2,1)}, u32[]{:S(2)}) copy-start(bf16[768,128]{1,0:T(8,128)(2,1)} %back_ref.1) | copy-start | bytes 589828
  21.1 10.2 %all-to-all-start.1 = ((bf16[8,16,768]{2,1,0:T(8,128)(2,1)}), bf16[8,16,768]{2,1,0:T(8,128)(2,1)S(1)}, u32[]{:S(2)}, u32[]{:S(2)}) async-start(bf16[8,16,768]{2,1,0:T(8,128)(2,1)} %get-tuple-element.14.normed_ref), calls=%async_computation.1 | async-start | bytes 393216 | tf_op jit(solution)/shard_map/all_to_all | solution.py:339
  24.6 2.3 %copy-start = (bf16[768,3072]{1,0:T(8,128)(2,1)S(1)}, bf16[768,3072]{1,0:T(8,128)(2,1)}, u32[]{:S(2)}) copy-start(bf16[768,3072]{1,0:T(8,128)(2,1)} %proj_ref.3) | copy-start | bytes 14155780
  31.3 3.2 %collective-permute-start.2 = (bf16[8,16,768]{2,1,0:T(8,128)(2,1)S(1)}, bf16[8,16,768]{2,1,0:T(8,128)(2,1)S(1)}, u32[]{:S(2)}, u32[]{:S(2)}) collective-permute-start(bf16[8,16,768]{2,1,0:T(8,128)(2,1)S(1)} %all-to-all-done.1.mine_ref), channel_id=1, source_target_pairs={{0,1},{1,0},{2,3},{3,2},{4,5},{5,4},{6,7},{7,6},{8,9},{9,8},{10,11... | collective-permute-start | bytes 589832 | tf_op jit(solution)/shard_map/ppermute | solution.py:355
  37.8 3.1 %collective-permute-start.3 = (bf16[16,128]{1,0:T(8,128)(2,1)S(1)}, bf16[16,128]{1,0:T(8,128)(2,1)S(1)}, u32[]{:S(2)}, u32[]{:S(2)}) collective-permute-start(bf16[16,128]{1,0:T(8,128)(2,1)S(1)} %get-tuple-element.21.back_ref), channel_id=1, source_target_pairs={{0,1},{1,0},{2,3},{3,2},{4,5},{5,4},{6,7},{7,6},{8,9},{9,8},{10,11... | collective-permute-start | bytes 12296 | tf_op jit(solution)/shard_map/ppermute | solution.py:372
  38.3 4.9 %collective-permute-start.4 = (bf16[16,128]{1,0:T(8,128)(2,1)S(1)}, bf16[16,128]{1,0:T(8,128)(2,1)S(1)}, u32[]{:S(2)}, u32[]{:S(2)}) collective-permute-start(bf16[16,128]{1,0:T(8,128)(2,1)S(1)} %get-tuple-element.21.back_ref), channel_id=1, source_target_pairs={{1,2},{3,4},{5,6},{7,8},{9,10},{11,12},{13,14},{2,1},{4,3},{6,5},{... | collective-permute-start | bytes 12296 | tf_op jit(solution)/shard_map/ppermute | solution.py:371

commit v3 on v2

--- a/solution.py
+++ b/solution.py
@@ -19,6 +19,7 @@
 ADIM = 32
 HALF = 128
 REACH = 64
+VMEM_LIMIT = 24 * 1024 * 1024
 COST = 2_000_000_000
 EPS = 1e-05
 NEG = -1e30
@@ -71,99 +72,125 @@
         bias_ref[t * HEADS : (t + 1) * HEADS, :] = dot_nt(weight, normed)
 
 
+def attend_window(queries, keys, values, start, begin, atoms):
+    count, extent = queries.shape[0], keys.shape[0]
+    head = iota((count, CA), 1) // ADIM
+    stacked = jnp.concatenate(
+        [jnp.where(head == h, queries, jnp.zeros_like(queries)) for h in range(AHEADS)], axis=0
+    )
+    scores = dot_nt(stacked, keys) * (1.0 / math.sqrt(ADIM))
+    place = iota((count, extent), 1) + begin
+    inside = (place >= start) & (place < start + KWIN) & (place >= 0) & (place < atoms)
+    inside = jnp.concatenate([inside.astype(F32)] * AHEADS, axis=0) > 0.5
+    scores = jnp.where(inside, scores, NEG)
+    weights = jnp.exp(scores - jnp.max(scores, axis=-1, keepdims=True))
+    denom = jnp.sum(weights, axis=-1, keepdims=True)
+    mixed = dot(weights.astype(BF16), values) / denom
+    total = jnp.zeros((count, CA), F32)
+    for h in range(AHEADS):
+        total = total + jnp.where(head == h, mixed[h * count : (h + 1) * count], 0.0)
+    return total.astype(BF16)
+
+
+def block_starts(row, count, first):
+    shape = (count, row.shape[1])
+    lane = iota(shape, 1) - first
+    return jnp.sum(jnp.where(lane == iota(shape, 0) // QBLK, row, 0), axis=1, keepdims=True)
+
+
+def edges(feat_core, feat_far, rows):
+    even = lax.rem(lax.axis_index("row"), 2) == 0
+    left = jnp.where(even, feat_far[rows - HALF :, :], feat_core[rows - HALF :, :])
+    right = jnp.where(even, feat_core[:HALF, :], feat_far[:HALF, :])
+    return left, right
+
+
 def atom_kernel(
-    n,
-    feat_ref,
-    core_ref,
-    far_ref,
-    table_ref,
-    single_ref,
-    gain_ref,
-    qkv_ref,
-    out_ref,
-    pool_ref,
-    restype_ref,
-    token_gain_ref,
-    bias_ref,
-    mid_ref,
-    state_ref,
-    normed_ref,
+    n, feat_ref, core_ref, far_ref, window_ref, gain_ref, qkv_ref, out_ref, pool_ref, bias_ref,
+    proj_ref, mid_ref, lifted_ref,
 ):
     me = lax.axis_index("row")
-    even = lax.rem(me, 2) == 0
     rows = feat_ref.shape[0]
+    left, right = edges(core_ref[...], far_ref[...], rows)
+    feat = jnp.concatenate([left, feat_ref[...], right], axis=0).astype(F32)
+    proj = dot(norm(feat, gain_ref[...]).astype(BF16), qkv_ref[...]).astype(BF16)
+    proj_ref[...] = proj
+    for s in range(rows // HALF):
+        own = slice(HALF * s, HALF * s + HALF)
+        ext = slice(HALF * s + HALF, HALF * s + 2 * HALF)
+        near = slice(HALF * s + HALF - REACH, HALF * s + 3 * HALF - REACH)
+        mixed = attend_window(
+            proj[ext, :CA],
+            proj[near, CA : 2 * CA],
+            proj[near, 2 * CA :],
+            block_starts(window_ref[...], HALF, s * HALF // QBLK),
+            me * rows + HALF * s - REACH,
+            n * rows,
+        )
+        mid = (feat[ext] + dot(mixed, out_ref[...])).astype(BF16)
+        mid_ref[own, :] = mid
+        lifted_ref[own, :] = jnp.maximum(dot(mid, pool_ref[...]), 0.0).astype(BF16)
+
+
+def state_kernel(
+    n, proj_ref, lifted_ref, core_ref, far_ref, table_ref, single_ref, out_ref, pool_ref, restype_ref, gain_ref,
+    state_ref, normed_ref,
+):
+    me = lax.axis_index("row")
+    rows = lifted_ref.shape[0]
     tokens = single_ref.shape[0]
     table = table_ref[...]
     own_row = table_row(table, me)
-    left = jnp.where(even, far_ref[rows - HALF :, :], core_ref[rows - HALF :, :])
-    right = jnp.where(even, core_ref[:HALF, :], far_ref[:HALF, :])
-    feat = jnp.concatenate([left, feat_ref[...], right], axis=0)
-    normed = norm(feat.astype(F32), gain_ref[...]).astype(BF16)
-    proj = dot(normed, qkv_ref[...]).astype(BF16)
-    span = rows + 2 * REACH
     windows = rows // QBLK
-    edge = REACH // QBLK
-    win_left = table_row(table, me - 1)
-    win_right = table_row(table, me + 1)
-    mids = []
-    for s in range(span // HALF):
-        begin = REACH + HALF * s
-        queries = proj[begin : begin + HALF, :CA]
-        keys = proj[HALF * s : HALF * s + 2 * HALF, CA : 2 * CA]
-        values = proj[HALF * s : HALF * s + 2 * HALF, 2 * CA :]
-        head = iota((HALF, CA), 1) // ADIM
-        stacked = jnp.concatenate(
-            [jnp.where(head == h, queries, jnp.zeros_like(queries)) for h in range(AHEADS)], axis=0
+    size = 2 * HALF
+    mixed = []
+    for at, base, row, first in (
+        (HALF - REACH, 0, me - 1, windows - REACH // QBLK),
+        (HALF + rows, rows + 2 * HALF - size, me + 1, 0),
+    ):
+        mixed.append(
+            attend_window(
+                proj_ref[at : at + REACH, :CA],
+                proj_ref[base : base + size, CA : 2 * CA],
+                proj_ref[base : base + size, 2 * CA :],
+                block_starts(table_row(table, row), REACH, WIN + first),
+                me * rows - HALF + base,
+                n * rows,
+            )
         )
-        scores = dot_nt(stacked, keys) * (1.0 / math.sqrt(ADIM))
-        shape = (HALF, TABLE)
-        block = iota(shape, 0) // QBLK + (HALF // QBLK) * s - edge
-        lane = iota(shape, 1) - WIN
-        begins = jnp.where((block >= 0) & (block < windows) & (lane == block), own_row, 0)
-        if s == 0:
-            begins += jnp.where((block < 0) & (lane == block + windows), win_left, 0)
-        if s == span // HALF - 1:
-            begins += jnp.where((block >= windows) & (lane == block - windows), win_right, 0)
-        start = jnp.sum(begins, axis=1, keepdims=True)
-        shape = (HALF, 2 * HALF)
-        place = iota(shape, 1) + (me * rows - HALF + HALF * s)
-        inside = (place >= start) & (place < start + KWIN) & (place >= 0) & (place < n * rows)
-        inside = jnp.concatenate([inside.astype(F32)] * AHEADS, axis=0) > 0.5
-        scores = jnp.where(inside, scores, NEG)
-        weights = jnp.exp(scores - jnp.max(scores, axis=-1, keepdims=True))
-        denom = jnp.sum(weights, axis=-1, keepdims=True)
-        mixed = dot(weights.astype(BF16), values) / denom
-        total = jnp.zeros((HALF, CA), F32)
-        for h in range(AHEADS):
-            total = total + jnp.where(head == h, mixed[h * HALF : (h + 1) * HALF], 0.0)
-        added = dot(total.astype(BF16), out_ref[...])
-        mids.append((feat[begin : begin + HALF].astype(F32) + added).astype(BF16))
-    mid = jnp.concatenate(mids, axis=0)
-    mid_ref[...] = mid[REACH : REACH + rows]
-    lifted = jnp.maximum(dot(mid, pool_ref[...]), 0.0).astype(BF16)
+    left, right = edges(core_ref[...], far_ref[...], rows)
+    feat = jnp.concatenate([left[HALF - REACH :], right[:REACH]], axis=0).astype(F32)
+    mid = (feat + dot(jnp.concatenate(mixed, axis=0), out_ref[...])).astype(BF16)
+    beside = jnp.maximum(dot(mid, pool_ref[...]), 0.0).astype(BF16)
     count = column(own_row, COUNT, tokens)
     shape = (tokens, TABLE)
     ahead = (iota(shape, 1) >= COUNT) & (iota(shape, 1) < COUNT + iota(shape, 0))
-    begin = atoms_before(table, me, tokens) + jnp.sum(
-        jnp.where(ahead, own_row, 0), axis=1, keepdims=True
-    )
-    atom = iota((tokens, span), 1) + (me * rows - REACH)
+    begin = atoms_before(table, me, tokens) - me * rows
+    begin = begin + jnp.sum(jnp.where(ahead, own_row, 0), axis=1, keepdims=True)
+    atom = iota((tokens, rows), 1)
     chosen = (atom >= begin) & (atom < begin + count)
-    pooled = dot(jnp.where(chosen, 1.0, 0.0).astype(BF16), lifted)
+    pooled = dot(jnp.where(chosen, 1.0, 0.0).astype(BF16), lifted_ref[...])
+    lane = iota((tokens, 2 * REACH), 1)
+    atom = jnp.where(lane < REACH, lane - REACH, lane - REACH + rows)
+    chosen = (atom >= begin) & (atom < begin + count)
+    pooled = pooled + dot(jnp.where(chosen, 1.0, 0.0).astype(BF16), beside)
     kind = column(own_row, RES, tokens)
     onehot = jnp.where(iota((tokens, RESTYPES), 1) == kind, 1.0, 0.0).astype(BF16)
     state = single_ref[...].astype(F32) + pooled / count.astype(F32)
     state = state + dot(onehot, restype_ref[...])
     state_ref[...] = state
-    token_normed = norm(state, token_gain_ref[...]).astype(BF16)
+    token_normed = norm(state, gain_ref[...]).astype(BF16)
     for i in range(normed_ref.shape[0]):
         normed_ref[i] = token_normed
 
 
 def query_kernel(
     normed_ref, table_ref, bias_ref, chain_weight_ref, proj_ref,
-    query_ref, gate_ref, biased_ref, pick_ref,
+    query_ref, gate_ref, biased_ref, pick_ref, wv_ref,
+    sem,
 ):
+    copy = pltpu.make_async_copy(proj_ref.at[:, pl.ds(2 * CS, CS)], wv_ref, sem)
+    copy.start()
     me = lax.axis_index("row")
     normed = normed_ref[0]
     tokens = normed.shape[0]
@@ -213,15 +240,12 @@
     atom = (iota((rows, TABLE), 0) + me * rows).astype(F32)
     pick_ref[...] = jnp.where((atom >= begin) & (atom < begin + size), 1.0, 0.0).astype(BF16)
     gate_ref[...] = jax.nn.sigmoid(dot(normed, proj_ref[:, 3 * CS :]))
+    copy.wait()
 
 
 def attend_kernel(
-    mine_ref, other_ref, query_ref, biased_ref, gate_ref, state_ref, out_ref, back_ref, proj_ref,
-    tokens_ref, result_ref,
-    wv_ref, sem,
+    mine_ref, other_ref, query_ref, biased_ref, gate_ref, state_ref, wv_ref, out_ref, tokens_ref, copy_ref
 ):
-    copy = pltpu.make_async_copy(proj_ref.at[:, pl.ds(2 * CS, CS)], wv_ref, sem)
-    copy.start()
     even = lax.rem(lax.axis_index("row"), 2) == 0
     tokens = state_ref.shape[0]
     chips = mine_ref.shape[0]
@@ -234,7 +258,6 @@
     scores = dot_nt(query_ref[...], normed) * (1.0 / math.sqrt(HDIM)) + biased_ref[...]
     weights = jnp.exp(scores - jnp.max(scores, axis=-1, keepdims=True))
     denom = jnp.sum(weights, axis=-1, keepdims=True)
-    copy.wait()
     values = dot(normed, wv_ref[...]).astype(BF16)
     mixed = dot(weights.astype(BF16), values) / denom
     head = iota((HEADS, CS), 1) // HDIM == iota((HEADS, CS), 0)
@@ -250,29 +273,31 @@
     gated = (mixed * gate_ref[...]).astype(BF16)
     updated = (state_ref[...] + dot(gated, out_ref[...])).astype(BF16)
     tokens_ref[...] = updated
-    result_ref[...] = dot(updated, back_ref[...]).astype(BF16)
-
-
-def spread_kernel(mid_ref, back_ref, core_ref, far_ref, pick_ref, atoms_ref):
+    copy_ref[...] = updated
+
+
+def spread_kernel(mid_ref, own_ref, core_ref, far_ref, pick_ref, weight_ref, atoms_ref):
     even = lax.rem(lax.axis_index("row"), 2) == 0
-    core, far, own = core_ref[...], far_ref[...], back_ref[...]
-    rest = jnp.zeros((TABLE - 3 * own.shape[0], CA), BF16)
-    parts = [jnp.where(even, far, core), own, jnp.where(even, core, far), rest]
-    spread = dot(pick_ref[...], jnp.concatenate(parts, axis=0))
+    core, far, own = core_ref[...], far_ref[...], own_ref[...]
+    parts = [jnp.where(even, far, core), own, jnp.where(even, core, far)]
+    back = dot(jnp.concatenate(parts, axis=0), weight_ref[...]).astype(BF16)
+    rest = jnp.zeros((TABLE - back.shape[0], CA), BF16)
+    spread = dot(pick_ref[...], jnp.concatenate([back, rest], axis=0))
     atoms_ref[...] = (mid_ref[...].astype(F32) + spread).astype(BF16)
 
 
-def call(kernel, outs, *args, hbm=(), limit=24, scratch=()):
+def call(kernel, outs, *args, scratch=(), aliases=None):
     spec = pl.BlockSpec(memory_space=pltpu.VMEM)
     return pl.pallas_call(
         kernel,
         out_shape=outs,
-        in_specs=[spec] * len(args) + [pl.BlockSpec(memory_space=pltpu.HBM)] * len(hbm),
+        in_specs=[spec] * len(args),
         out_specs=jax.tree.map(lambda _: spec, outs),
         scratch_shapes=list(scratch),
-        compiler_params=pltpu.CompilerParams(vmem_limit_bytes=limit * 1024 * 1024),
+        input_output_aliases=aliases or {},
+        compiler_params=pltpu.CompilerParams(vmem_limit_bytes=VMEM_LIMIT),
         cost_estimate=pl.CostEstimate(flops=COST, bytes_accessed=COST // 200, transcendentals=0),
-    )(*args, *hbm)
+    )(*args)
 
 
 def shape_of(shape, dtype):
@@ -316,68 +341,80 @@
     bias = call(
         pair_kernel, shape_of((tokens * HEADS, extent), F32), pair, pair_gain, pair_bias_weight.T
     )
-    mid, state, normed = call(
+    proj, mid, lifted = call(
         functools.partial(atom_kernel, n),
         (
+            shape_of((rows + 2 * HALF, 3 * CA), BF16),
             shape_of((rows, CA), BF16),
-            shape_of((tokens, CS), F32),
-            shape_of((n // 2, tokens, CS), BF16),
+            shape_of((rows, CS), BF16),
         ),
         atom_feat,
         feat_core,
         feat_far,
-        table,
-        token_single,
+        window_start[None],
         atom_gain,
         atom_qkv,
         atom_out,
         pool_weight,
+        bias,
+    )
+    state, normed = call(
+        functools.partial(state_kernel, n),
+        (shape_of((tokens, CS), F32), shape_of((n // 2, tokens, CS), BF16)),
+        proj,
+        lifted,
+        feat_core,
+        feat_far,
+        table,
+        token_single,
+        atom_out,
+        pool_weight,
         restype_table,
         token_gain,
-        bias,
     )
     mine = lax.all_to_all(normed, "row", 0, 0, tiled=True, axis_index_groups=same_core)
-    query, gate, biased, pick = call(
+    query, gate, biased, pick, wv = call(
         query_kernel,
         (
             shape_of((tokens * HEADS, CS), BF16),
             shape_of((tokens, CS), F32),
             shape_of((tokens * HEADS, extent), F32),
             shape_of((rows, TABLE), BF16),
+            shape_of((CS, CS), BF16),
         ),
         normed,
         table,
         bias,
         chain_weight,
         token_proj,
+        scratch=(pltpu.SemaphoreType.DMA,),
+        aliases={2: 2},
     )
     mine, query = lax.optimization_barrier((mine, query))
     other = lax.ppermute(mine, "row", cores)
-    tokens_out, back = call(
+    tokens_out, updated = call(
         attend_kernel,
-        (shape_of((tokens, CS), BF16), shape_of((tokens, CA), BF16)),
+        (shape_of((tokens, CS), BF16), shape_of((tokens, CS), BF16)),
         mine,
         other,
         query,
         biased,
         gate,
         state,
+        wv,
         token_out,
-        back_weight,
-        hbm=(token_proj,),
-        limit=50,
-        scratch=(pltpu.VMEM((CS, CS), BF16), pltpu.SemaphoreType.DMA),
-    )
-    back_far = lax.ppermute(back, "row", far)
-    back_core = lax.ppermute(back, "row", cores)
+    )
+    tokens_far = lax.ppermute(updated, "row", far)
+    tokens_core = lax.ppermute(updated, "row", cores)
     atoms_out = call(
         spread_kernel,
         shape_of((rows, CA), BF16),
         mid,
-        back,
-        back_core,
-        back_far,
+        updated,
+        tokens_core,
+        tokens_far,
         pick,
+        back_weight,
     )
     return (atoms_out, tokens_out)
 

time: 44.4 us -> 41.8 us (0.941)
  waiting for transfers between devices: 9.69 us -> 7.7 us
    all_to_all x1, waiting for transfers between devices: 3.88 us -> 1.81 us  [shards(): table = lax.all_to_all(table, 'row', 0, 0, tiled=True).reshape(n, TABLE)]
    pallas_call x6 -> x7, Pallas kernels: 11.5 us -> 11.1 us  [call(): pl.pallas_call(kernel, out_shape=outs, in_specs=[spec] * len(args), out_s...]
    unnamed x30 -> x32, local copies, waits for them, and re-layouts: 2.4 us -> 2.42 us
  transfers between devices with their start and end apart: 7 -> 7, of which waited for: 4 -> 4; matrix products, arithmetic and copies ran while one was open for 2% -> 2% of each run, Pallas kernels for 10% -> 16%
where the time goes in v3:
time: 41.8 us; the launch traced here: 41.4 us
  starting transfers between devices  18.5 us (44%)
  Pallas kernels  11.1 us (27%)
  waiting for transfers between devices  7.7 us (18%)
  local copies, waits for them, and re-layouts  2.42 us (6%)
  between operations  0.87 us (2%)
  other arithmetic  0.78 us (2%)
    pallas_call x7, Pallas kernels, call(): pl.pallas_call(kernel, out_shape=outs, in_specs=[spec] * len(args), out_s...  11.1 us
    all_to_all x1, starting transfers between devices, shards(): table = lax.all_to_all(table, 'row', 0, 0, tiled=True).reshape(n, TABLE)  5.31 us
    ppermute x1, starting transfers between devices, shards(): feat_far = lax.ppermute(atom_feat, 'row', far)  4.5 us
    all_to_all x1, starting transfers between devices, shards(): lax.all_to_all(normed, 'row', 0, 0, tiled=True, axis_index_groups=same_core)  3.59 us
    ppermute x1, starting transfers between devices, shards(): tokens_far = lax.ppermute(updated, 'row', far)  2.62 us
    ppermute x1, waiting for transfers between devices, shards(): tokens_far = lax.ppermute(updated, 'row', far)  2.5 us
    unnamed x32, local copies, waits for them, and re-layouts  2.42 us
    all_to_all x1, waiting for transfers between devices, shards(): lax.all_to_all(normed, 'row', 0, 0, tiled=True, axis_index_groups=same_core)  2.32 us
  transfers between devices with their start and end apart: 7, of which 4 were waited for; matrix products, arithmetic and copies ran while one was open for 2% of the time, Pallas kernels for 16%

profile of v3, /device:TPU:1, one launch (start us, length us, event | category | flops | bytes accessed | tf_op | source)
XLA Modules:
  0.0 41.4 jit_solution(14054455798449589750)
XLA Ops:
  0.6 0.1 collective-permute-start
  0.8 4.5 %collective-permute-start.1 = (bf16[256,128]{1,0:T(8,128)(2,1)}, bf16[256,128]{1,0:T(8,128)(2,1)S(1)}, u32[]{:S(2)}, u32[]{:S(2)}) collective-permute-start(bf16[256,128]{1,0:T(8,128)(2,1)} %feat_ref.1), channel_id=1, source_target_pairs={{1,2},{3,4},{5,6},{7,8},{9,10},{11,12},{13,14},{2,1},{4,3},{6,5},{... | collective-permute-start | bytes 196616 | tf_op jit(solution)/shard_map/ppermute | solution.py:334
  5.3 0.8 %pad_add_fusion = s32[56]{0:T(128)S(1)} fusion(s32[8]{0:T(128)} %param.20, s32[16]{0:T(128)} %param.22, s32[16]{0:T(128)} %param.23, s32[16]{0:T(128)} %param.21), kind=kLoop, calls=%fused_computation | loop fusion | flops 168 | bytes 448 | tf_op jit(solution)/shard_map/concatenate | solution.py:336
  6.0 0.0 copy-start.3
  6.0 0.0 copy-start.11
  6.1 0.0 copy-start.13
  6.1 0.6 %shard_map.196 = s32[16,1,128]{2,1,0:T(1,128)} custom-call(s32[1,128]{1,0:T(1,128)S(1)} %pad_bitcast_fusion.row_ref), custom_call_target="tpu_custom_call" | custom-call | flops 2000000000 | bytes 10000000 | tf_op jit(solution)/shard_map/pallas_call | solution.py:291
  6.7 5.3 %all-to-all-start = ((s32[16,1,128]{2,1,0:T(1,128)}), s32[16,1,128]{2,1,0:T(1,128)S(1)}, u32[]{:S(2)}, u32[]{:S(2)}) async-start(s32[16,1,128]{2,1,0:T(1,128)} %shard_map.196), calls=%async_computation | async-start | bytes 16384 | tf_op jit(solution)/shard_map/all_to_all | solution.py:339
  12.0 0.0 copy-done.3
  12.0 0.0 copy-done.11
  12.0 0.0 copy-done.13
  12.0 0.0 copy-start
  12.0 0.0 copy-start.4
  12.0 0.0 copy-start.6
  12.1 0.0 copy-start.7
  12.1 0.0 copy-start.9
  12.1 0.0 copy-start.14
  12.1 1.8 %shard_map.194.bias_ref = f32[256,256]{1,0:T(8,128)S(1)} custom-call(bf16[16,256,128]{2,1,0:T(8,128)(2,1)S(1)} %copy-done.3, f32[128]{0:T(128)S(1)} %copy-done.13, bf16[16,128]{1,0:T(8,128)(2,1)S(1)} %bitcast.8), custom_call_target="tpu_custom_call" | custom-call | flops 2000000000 | bytes 10000000 | tf_op jit(solution)/shard_map/pallas_call | solution.py:291
  13.9 0.0 collective-permute-done.core_ref
  13.9 0.0 collective-permute-done.1.far_ref
  13.9 0.0 copy-done
  13.9 0.0 copy-done.4
  13.9 0.0 copy-done.6
  13.9 0.0 copy-done.7
  13.9 0.0 copy-done.9
  14.0 0.0 copy-done.14
  14.0 0.0 copy-start.8
  14.0 0.0 copy-start.10
  14.0 0.0 copy-start.12
  14.0 1.9 %shard_map.195 = (bf16[512,384]{1,0:T(8,128)(2,1)S(1)}, bf16[256,128]{1,0:T(8,128)(2,1)S(1)}, bf16[256,768]{1,0:T(8,128)(2,1)S(1)}) custom-call(bf16[256,128]{1,0:T(8,128)(2,1)S(1)} %copy-done.7, bf16[256,128]{1,0:T(8,128)(2,1)S(1)} %collective-permute-done.core_ref, bf16[256,128]{1,0:T(8,128)(2,1)S(1)} %collective-permute-done.1.far_ref, ...), custom_call_target="tpu_custom_call" | custom-call | flops 2000000000 | bytes 10000000 | tf_op jit(solution)/shard_map/pallas_call | solution.py:291
  15.9 1.8 %all-to-all-done = s32[16,1,128]{2,1,0:T(1,128)S(1)} async-done(((s32[16,1,128]{2,1,0:T(1,128)}), s32[16,1,128]{2,1,0:T(1,128)S(1)}, u32[]{:S(2)}, u32[]{:S(2)}) %all-to-all-start) | async-done | bytes 8224 | tf_op jit(solution)/shard_map/all_to_all | solution.py:339
  17.7 0.0 copy-done.8
  17.7 0.0 copy-done.10
  17.7 0.0 copy-done.12
  17.7 0.0 copy-start.15
  17.7 2.0 %shard_map.197 = (f32[16,768]{1,0:T(8,128)S(1)}, bf16[8,16,768]{2,1,0:T(8,128)(2,1)}) custom-call(bf16[512,384]{1,0:T(8,128)(2,1)S(1)} %get-tuple-element.17.proj_ref, bf16[256,768]{1,0:T(8,128)(2,1)S(1)} %get-tuple-element.18.lifted_ref, bf16[256,128]{1,0:T(8,128)(2,1)S(1)} %collective-permute-done.core_ref, ...), custom_call_target="tpu_custom_call" | custom-call | flops 2000000000 | bytes 10000000 | tf_op jit(solution)/shard_map/pallas_call | solution.py:291
  19.8 3.6 %all-to-all-start.1 = ((bf16[8,16,768]{2,1,0:T(8,128)(2,1)}), bf16[8,16,768]{2,1,0:T(8,128)(2,1)S(1)}, u32[]{:S(2)}, u32[]{:S(2)}) async-start(bf16[8,16,768]{2,1,0:T(8,128)(2,1)} %get-tuple-element.19.normed_ref), calls=%async_computation.1 | async-start | bytes 393216 | tf_op jit(solution)/shard_map/all_to_all | solution.py:375
  23.4 0.0 copy-done.15
  23.4 0.0 copy-start.1
  23.4 2.3 %copy-done.1 = bf16[768,3072]{1,0:T(8,128)(2,1)S(1)} copy-done((bf16[768,3072]{1,0:T(8,128)(2,1)S(1)}, bf16[768,3072]{1,0:T(8,128)(2,1)}, u32[]{:S(2)}) %copy-start.1) | copy-done | bytes 4718616
  25.7 0.0 copy-start.2
  25.7 2.2 %shard_map.198 = (bf16[256,768]{1,0:T(8,128)(2,1)S(1)}, f32[16,768]{1,0:T(8,128)S(1)}, f32[256,256]{1,0:T(8,128)S(1)}, bf16[256,128]{1,0:T(8,128)(2,1)S(1)}, bf16[768,768]{1,0:T(8,128)(2,1)S(1)}) custom-call(bf16[8,16,768]{2,1,0:T(8,128)(2,1)} %get-tuple-element.19.normed_ref, s32[16,128]{1,0:T(8,128)S(1)} %bitcast.6, ...), custom_call_target="tpu_custom_call", output_to_operand_aliasing={{2}: (2, {})} | custom-call | flops 2000000000 | bytes 10000000 | tf_op jit(solution)/shard_map/pallas_call | solution.py:291
  27.9 2.3 %all-to-all-done.1.mine_ref = bf16[8,16,768]{2,1,0:T(8,128)(2,1)S(1)} async-done(((bf16[8,16,768]{2,1,0:T(8,128)(2,1)}), bf16[8,16,768]{2,1,0:T(8,128)(2,1)S(1)}, u32[]{:S(2)}, u32[]{:S(2)}) %all-to-all-start.1) | async-done | bytes 196640 | tf_op jit(solution)/shard_map/all_to_all | solution.py:375
  30.2 2.0 %collective-permute-start.2 = (bf16[8,16,768]{2,1,0:T(8,128)(2,1)S(1)}, bf16[8,16,768]{2,1,0:T(8,128)(2,1)S(1)}, u32[]{:S(2)}, u32[]{:S(2)}) collective-permute-start(bf16[8,16,768]{2,1,0:T(8,128)(2,1)S(1)} %all-to-all-done.1.mine_ref), channel_id=1, source_target_pairs={{0,1},{1,0},{2,3},{3,2},{4,5},{5,4},{6,7},{7,6},{8,9},{9,8},{10,11... | collective-permute-start | bytes 589832 | tf_op jit(solution)/shard_map/ppermute | solution.py:394
  32.3 1.1 %collective-permute-done.2.other_ref = bf16[8,16,768]{2,1,0:T(8,128)(2,1)S(1)} collective-permute-done((bf16[8,16,768]{2,1,0:T(8,128)(2,1)S(1)}, bf16[8,16,768]{2,1,0:T(8,128)(2,1)S(1)}, u32[]{:S(2)}, u32[]{:S(2)}) %collective-permute-start.2) | collective-permute-done | bytes 196640 | tf_op jit(solution)/shard_map/ppermute | solution.py:394
  33.3 0.0 copy-done.2
  33.3 0.0 copy-start.5
  33.3 1.6 %shard_map.199 = (bf16[16,768]{1,0:T(8,128)(2,1)}, bf16[16,768]{1,0:T(8,128)(2,1)S(1)}) custom-call(bf16[8,16,768]{2,1,0:T(8,128)(2,1)S(1)} %all-to-all-done.1.mine_ref, bf16[8,16,768]{2,1,0:T(8,128)(2,1)S(1)} %collective-permute-done.2.other_ref, bf16[256,768]{1,0:T(8,128)(2,1)S(1)} %get-tuple-element.22.query_ref, ...), custom_call_target="tpu_custom_call" | custom-call | flops 2000000000 | bytes 10000000 | tf_op jit(solution)/shard_map/pallas_call | solution.py:291
  35.0 0.4 collective-permute-start.3
  35.4 2.6 %collective-permute-start.4 = (bf16[16,768]{1,0:T(8,128)(2,1)S(1)}, bf16[16,768]{1,0:T(8,128)(2,1)S(1)}, u32[]{:S(2)}, u32[]{:S(2)}) collective-permute-start(bf16[16,768]{1,0:T(8,128)(2,1)S(1)} %get-tuple-element.27.own_ref), channel_id=1, source_target_pairs={{1,2},{3,4},{5,6},{7,8},{9,10},{11,12},{13,14},{2,1},{4,3},{6,5},{... | collective-permute-start | bytes 73736 | tf_op jit(solution)/shard_map/ppermute | solution.py:407
  38.0 0.0 collective-permute-done.3.core_ref
  38.0 2.5 %collective-permute-done.4.far_ref = bf16[16,768]{1,0:T(8,128)(2,1)S(1)} collective-permute-done((bf16[16,768]{1,0:T(8,128)(2,1)S(1)}, bf16[16,768]{1,0:T(8,128)(2,1)S(1)}, u32[]{:S(2)}, u32[]{:S(2)}) %collective-permute-start.4) | collective-permute-done | bytes 24608 | tf_op jit(solution)/shard_map/ppermute | solution.py:407
  40.5 0.0 copy-done.5
  40.5 0.9 %shard_map.200 = bf16[256,128]{1,0:T(8,128)(2,1)} custom-call(bf16[256,128]{1,0:T(8,128)(2,1)S(1)} %get-tuple-element.16.mid_ref, bf16[16,768]{1,0:T(8,128)(2,1)S(1)} %get-tuple-element.27.own_ref, bf16[16,768]{1,0:T(8,128)(2,1)S(1)} %collective-permute-done.3.core_ref, bf16[16,768]{1,0:T(8,128)(2,1)S(1)} %collective-permute-done.4.far_ref, ...), custom_call_target="tpu_custom_call" | custom-call | flops 2000000000 | bytes 10000000 | tf_op jit(solution)/shard_map/pallas_call | solution.py:291
  (1 shorter events, 0.0 us)
Async XLA Ops:
  0.6 13.3 %collective-permute-start = (bf16[256,128]{1,0:T(8,128)(2,1)}, bf16[256,128]{1,0:T(8,128)(2,1)S(1)}, u32[]{:S(2)}, u32[]{:S(2)}) collective-permute-start(bf16[256,128]{1,0:T(8,128)(2,1)} %feat_ref.1), channel_id=1, source_target_pairs={{0,1},{1,0},{2,3},{3,2},{4,5},{5,4},{6,7},{7,6},{8,9},{9,8},{10,11... | collective-permute-start | bytes 196616 | tf_op jit(solution)/shard_map/ppermute | solution.py:335
  0.8 13.1 %collective-permute-start.1 = (bf16[256,128]{1,0:T(8,128)(2,1)}, bf16[256,128]{1,0:T(8,128)(2,1)S(1)}, u32[]{:S(2)}, u32[]{:S(2)}) collective-permute-start(bf16[256,128]{1,0:T(8,128)(2,1)} %feat_ref.1), channel_id=1, source_target_pairs={{1,2},{3,4},{5,6},{7,8},{9,10},{11,12},{13,14},{2,1},{4,3},{6,5},{... | collective-permute-start | bytes 196616 | tf_op jit(solution)/shard_map/ppermute | solution.py:334
  6.0 5.9 %copy-start.3 = (bf16[16,256,128]{2,1,0:T(8,128)(2,1)S(1)}, bf16[16,256,128]{2,1,0:T(8,128)(2,1)}, u32[]{:S(2)}) copy-start(bf16[16,256,128]{2,1,0:T(8,128)(2,1)} %pair_ref.1) | copy-start | bytes 3145732
  6.0 6.0 %copy-start.11 = (bf16[128,16]{0,1:T(8,128)(2,1)S(1)}, bf16[128,16]{0,1:T(8,128)(2,1)}, u32[]{:S(2)}) copy-start(bf16[128,16]{0,1:T(8,128)(2,1)} %param.35) | copy-start | bytes 12292
  6.1 5.9 %copy-start.13 = (f32[128]{0:T(128)S(1)}, f32[128]{0:T(128)}, u32[]{:S(2)}) copy-start(f32[128]{0:T(128)} %gain_ref.3) | copy-start | bytes 1540
  6.7 11.0 %all-to-all-start = ((s32[16,1,128]{2,1,0:T(1,128)}), s32[16,1,128]{2,1,0:T(1,128)S(1)}, u32[]{:S(2)}, u32[]{:S(2)}) async-start(s32[16,1,128]{2,1,0:T(1,128)} %shard_map.196), calls=%async_computation | async-start | bytes 16384 | tf_op jit(solution)/shard_map/all_to_all | solution.py:339
  12.0 1.9 %copy-start = (s32[8]{0:T(128)S(1)}, s32[8]{0:T(128)}, u32[]{:S(2)}) copy-start(s32[8]{0:T(128)} %param.20) | copy-start | bytes 100
  12.0 1.9 %copy-start.4 = (bf16[128,768]{1,0:T(8,128)(2,1)S(1)}, bf16[128,768]{1,0:T(8,128)(2,1)}, u32[]{:S(2)}) copy-start(bf16[128,768]{1,0:T(8,128)(2,1)} %pool_ref.3) | copy-start | bytes 589828
  12.0 1.9 %copy-start.6 = (bf16[128,384]{1,0:T(8,128)(2,1)S(1)}, bf16[128,384]{1,0:T(8,128)(2,1)}, u32[]{:S(2)}) copy-start(bf16[128,384]{1,0:T(8,128)(2,1)} %qkv_ref.1) | copy-start | bytes 294916
  12.1 1.9 %copy-start.7 = (bf16[256,128]{1,0:T(8,128)(2,1)S(1)}, bf16[256,128]{1,0:T(8,128)(2,1)}, u32[]{:S(2)}) copy-start(bf16[256,128]{1,0:T(8,128)(2,1)} %feat_ref.1) | copy-start | bytes 196612
  12.1 1.9 %copy-start.9 = (bf16[128,128]{1,0:T(8,128)(2,1)S(1)}, bf16[128,128]{1,0:T(8,128)(2,1)}, u32[]{:S(2)}) copy-start(bf16[128,128]{1,0:T(8,128)(2,1)} %out_ref.4) | copy-start | bytes 98308
  12.1 1.9 %copy-start.14 = (f32[128]{0:T(128)S(1)}, f32[128]{0:T(128)}, u32[]{:S(2)}) copy-start(f32[128]{0:T(128)} %gain_ref.4) | copy-start | bytes 1540
  14.0 3.7 %copy-start.8 = (bf16[32,768]{1,0:T(8,128)(2,1)S(1)}, bf16[32,768]{1,0:T(8,128)(2,1)}, u32[]{:S(2)}) copy-start(bf16[32,768]{1,0:T(8,128)(2,1)} %restype_ref.1) | copy-start | bytes 147460
  14.0 3.7 %copy-start.10 = (bf16[16,768]{1,0:T(8,128)(2,1)S(1)}, bf16[16,768]{1,0:T(8,128)(2,1)}, u32[]{:S(2)}) copy-start(bf16[16,768]{1,0:T(8,128)(2,1)} %single_ref.1) | copy-start | bytes 73732
  14.0 3.7 %copy-start.12 = (f32[768]{0:T(1024)S(1)}, f32[768]{0:T(1024)}, u32[]{:S(2)}) copy-start(f32[768]{0:T(1024)} %gain_ref.5) | copy-start | bytes 9220
  17.7 5.6 %copy-start.15 = (f32[16]{0:T(128)S(1)}, f32[16]{0:T(128)}, u32[]{:S(2)}) copy-start(f32[16]{0:T(128)} %chain_weight_ref.1) | copy-start | bytes 196
  19.8 10.5 %all-to-all-start.1 = ((bf16[8,16,768]{2,1,0:T(8,128)(2,1)}), bf16[8,16,768]{2,1,0:T(8,128)(2,1)S(1)}, u32[]{:S(2)}, u32[]{:S(2)}) async-start(bf16[8,16,768]{2,1,0:T(8,128)(2,1)} %get-tuple-element.19.normed_ref), calls=%async_computation.1 | async-start | bytes 393216 | tf_op jit(solution)/shard_map/all_to_all | solution.py:375
  23.4 2.3 %copy-start.1 = (bf16[768,3072]{1,0:T(8,128)(2,1)S(1)}, bf16[768,3072]{1,0:T(8,128)(2,1)}, u32[]{:S(2)}) copy-start(bf16[768,3072]{1,0:T(8,128)(2,1)} %proj_ref.1) | copy-start | bytes 14155780
  25.7 7.6 %copy-start.2 = (bf16[768,768]{1,0:T(8,128)(2,1)S(1)}, bf16[768,768]{1,0:T(8,128)(2,1)}, u32[]{:S(2)}) copy-start(bf16[768,768]{1,0:T(8,128)(2,1)} %out_ref.5) | copy-start | bytes 3538948
  30.2 3.1 %collective-permute-start.2 = (bf16[8,16,768]{2,1,0:T(8,128)(2,1)S(1)}, bf16[8,16,768]{2,1,0:T(8,128)(2,1)S(1)}, u32[]{:S(2)}, u32[]{:S(2)}) collective-permute-start(bf16[8,16,768]{2,1,0:T(8,128)(2,1)S(1)} %all-to-all-done.1.mine_ref), channel_id=1, source_target_pairs={{0,1},{1,0},{2,3},{3,2},{4,5},{5,4},{6,7},{7,6},{8,9},{9,8},{10,11... | collective-permute-start | bytes 589832 | tf_op jit(solution)/shard_map/ppermute | solution.py:394
  33.3 7.2 %copy-start.5 = (bf16[768,128]{1,0:T(8,128)(2,1)S(1)}, bf16[768,128]{1,0:T(8,128)(2,1)}, u32[]{:S(2)}) copy-start(bf16[768,128]{1,0:T(8,128)(2,1)} %weight_ref.1) | copy-start | bytes 589828
  35.0 3.0 %collective-permute-start.3 = (bf16[16,768]{1,0:T(8,128)(2,1)S(1)}, bf16[16,768]{1,0:T(8,128)(2,1)S(1)}, u32[]{:S(2)}, u32[]{:S(2)}) collective-permute-start(bf16[16,768]{1,0:T(8,128)(2,1)S(1)} %get-tuple-element.27.own_ref), channel_id=1, source_target_pairs={{0,1},{1,0},{2,3},{3,2},{4,5},{5,4},{6,7},{7,6},{8,9},{9,8},{10,11... | collective-permute-start | bytes 73736 | tf_op jit(solution)/shard_map/ppermute | solution.py:408
  35.4 5.1 %collective-permute-start.4 = (bf16[16,768]{1,0:T(8,128)(2,1)S(1)}, bf16[16,768]{1,0:T(8,128)(2,1)S(1)}, u32[]{:S(2)}, u32[]{:S(2)}) collective-permute-start(bf16[16,768]{1,0:T(8,128)(2,1)S(1)} %get-tuple-element.27.own_ref), channel_id=1, source_target_pairs={{1,2},{3,4},{5,6},{7,8},{9,10},{11,12},{13,14},{2,1},{4,3},{6,5},{... | collective-permute-start | bytes 73736 | tf_op jit(solution)/shard_map/ppermute | solution.py:407

commit v4 on v3

--- a/solution.py
+++ b/solution.py
@@ -61,8 +61,21 @@
     return jnp.sum(jnp.sum(jnp.where(keep, table, 0), axis=0, keepdims=True), axis=1, keepdims=True)
 
 
-def table_kernel(row_ref, table_ref):
-    table_ref[...] = jnp.broadcast_to(row_ref[...][None], table_ref.shape)
+def first_kernel(out_ref):
+    out_ref[...] = jnp.zeros_like(out_ref)
+
+
+def table_kernel(zero_ref, count_ref, chain_ref, kind_ref, window_ref, table_ref):
+    row = zero_ref[:1]
+    pieces = ((COUNT, count_ref), (CHAIN, chain_ref), (RES, kind_ref), (WIN, window_ref))
+    for base, ref in pieces:
+        size = ref.shape[1]
+        shape = (size, TABLE)
+        at = iota(shape, 1) == iota(shape, 0) + base
+        eye = iota((size, size), 0) == iota((size, size), 1)
+        values = jnp.sum(jnp.where(eye, ref[...], 0), axis=1, keepdims=True)
+        row = row + jnp.sum(jnp.where(at, values, 0), axis=0, keepdims=True)
+    table_ref[...] = jnp.broadcast_to(row[None], table_ref.shape)
 
 
 def pair_kernel(pair_ref, gain_ref, weight_ref, bias_ref):
@@ -244,7 +257,7 @@
 
 
 def attend_kernel(
-    mine_ref, other_ref, query_ref, biased_ref, gate_ref, state_ref, wv_ref, out_ref, tokens_ref, copy_ref
+    mine_ref, other_ref, query_ref, biased_ref, gate_ref, state_ref, wv_ref, out_ref, tokens_ref
 ):
     even = lax.rem(lax.axis_index("row"), 2) == 0
     tokens = state_ref.shape[0]
@@ -271,19 +284,27 @@
         axis=0,
     )
     gated = (mixed * gate_ref[...]).astype(BF16)
-    updated = (state_ref[...] + dot(gated, out_ref[...])).astype(BF16)
-    tokens_ref[...] = updated
-    copy_ref[...] = updated
-
-
-def spread_kernel(mid_ref, own_ref, core_ref, far_ref, pick_ref, weight_ref, atoms_ref):
+    tokens_ref[...] = (state_ref[...] + dot(gated, out_ref[...])).astype(BF16)
+
+
+def own_kernel(mid_ref, own_ref, pick_ref, weight_ref, back_ref, partial_ref, tokens_ref):
+    own = own_ref[...]
+    tokens_ref[...] = own
+    back = dot(own, weight_ref[...]).astype(BF16)
+    back_ref[...] = back
+    count = back.shape[0]
+    rest = jnp.zeros((TABLE - 2 * count, CA), BF16)
+    spread = dot(pick_ref[...], jnp.concatenate([jnp.zeros_like(back), back, rest], axis=0))
+    partial_ref[...] = mid_ref[...].astype(F32) + spread
+
+
+def beside_kernel(partial_ref, core_ref, far_ref, pick_ref, weight_ref, atoms_ref):
     even = lax.rem(lax.axis_index("row"), 2) == 0
-    core, far, own = core_ref[...], far_ref[...], own_ref[...]
-    parts = [jnp.where(even, far, core), own, jnp.where(even, core, far)]
-    back = dot(jnp.concatenate(parts, axis=0), weight_ref[...]).astype(BF16)
-    rest = jnp.zeros((TABLE - back.shape[0], CA), BF16)
-    spread = dot(pick_ref[...], jnp.concatenate([back, rest], axis=0))
-    atoms_ref[...] = (mid_ref[...].astype(F32) + spread).astype(BF16)
+    core, far = core_ref[...], dot(far_ref[...], weight_ref[...]).astype(BF16)
+    parts = [jnp.where(even, far, core), jnp.zeros_like(core), jnp.where(even, core, far)]
+    rest = jnp.zeros((TABLE - 3 * core.shape[0], CA), BF16)
+    spread = dot(pick_ref[...], jnp.concatenate([*parts, rest], axis=0))
+    atoms_ref[...] = (partial_ref[...] + spread).astype(BF16)
 
 
 def call(kernel, outs, *args, scratch=(), aliases=None):
@@ -333,9 +354,15 @@
 
     feat_far = lax.ppermute(atom_feat, "row", far)
     feat_core = lax.ppermute(atom_feat, "row", cores)
-    ints = jnp.concatenate([atom_count, chain_id, residue_type, window_start])
-    ints = jnp.pad(ints, (0, TABLE - ints.shape[0]))[None]
-    table = call(table_kernel, shape_of((n, 1, TABLE), jnp.int32), ints)
+    table = call(
+        table_kernel,
+        shape_of((n, 1, TABLE), jnp.int32),
+        call(first_kernel, shape_of((8, TABLE), jnp.int32)),
+        atom_count[None],
+        chain_id[None],
+        residue_type[None],
+        window_start[None],
+    )
     table = lax.all_to_all(table, "row", 0, 0, tiled=True).reshape(n, TABLE)
 
     bias = call(
@@ -392,9 +419,9 @@
     )
     mine, query = lax.optimization_barrier((mine, query))
     other = lax.ppermute(mine, "row", cores)
-    tokens_out, updated = call(
+    updated = call(
         attend_kernel,
-        (shape_of((tokens, CS), BF16), shape_of((tokens, CS), BF16)),
+        shape_of((tokens, CS), BF16),
         mine,
         other,
         query,
@@ -405,13 +432,20 @@
         token_out,
     )
     tokens_far = lax.ppermute(updated, "row", far)
-    tokens_core = lax.ppermute(updated, "row", cores)
-    atoms_out = call(
-        spread_kernel,
-        shape_of((rows, CA), BF16),
+    back, partial, tokens_out = call(
+        own_kernel,
+        (shape_of((tokens, CA), BF16), shape_of((rows, CA), F32), shape_of((tokens, CS), BF16)),
         mid,
         updated,
-        tokens_core,
+        pick,
+        back_weight,
+    )
+    back_core = lax.ppermute(back, "row", cores)
+    atoms_out = call(
+        beside_kernel,
+        shape_of((rows, CA), BF16),
+        partial,
+        back_core,
         tokens_far,
         pick,
         back_weight,

time: 41.8 us -> 40.1 us (0.959)
  waiting for transfers between devices: 7.7 us -> 6.84 us
  other arithmetic: 0.78 us -> 0 us
    ppermute x1, waiting for transfers between devices: 2.5 us -> 0.46 us  [shards(): tokens_far = lax.ppermute(updated, 'row', far)]
    ppermute x1, waiting for transfers between devices: 0.01 us -> 1.16 us  [shards(): back_core = lax.ppermute(back, 'row', cores)]
    concatenate x1 -> x0, other arithmetic: 0.78 us -> none  [shards(): ints = jnp.concatenate([atom_count, chain_id, residue_type, window_start])]
    pallas_call x7 -> x9, Pallas kernels: 11.1 us -> 11.2 us  [call(): pl.pallas_call(kernel, out_shape=outs, in_specs=[spec] * len(args), out_s...]
    unnamed x32 -> x38, local copies, waits for them, and re-layouts: 2.42 us -> 2.43 us
  transfers between devices with their start and end apart: 7 -> 7, of which waited for: 4 -> 5; matrix products, arithmetic and copies ran while one was open for 2% -> 0% of each run, Pallas kernels for 16% -> 18%
where the time goes in v4:
time: 40.1 us; the launch traced here: 39.8 us
  starting transfers between devices  18.4 us (46%)
  Pallas kernels  11.2 us (28%)
  waiting for transfers between devices  6.84 us (17%)
  local copies, waits for them, and re-layouts  2.43 us (6%)
  between operations  0.92 us (2%)
    pallas_call x9, Pallas kernels, call(): pl.pallas_call(kernel, out_shape=outs, in_specs=[spec] * len(args), out_s...  11.2 us
    all_to_all x1, starting transfers between devices, shards(): table = lax.all_to_all(table, 'row', 0, 0, tiled=True).reshape(n, TABLE)  5.31 us
    ppermute x1, starting transfers between devices, shards(): feat_far = lax.ppermute(atom_feat, 'row', far)  4.5 us
    all_to_all x1, starting transfers between devices, shards(): lax.all_to_all(normed, 'row', 0, 0, tiled=True, axis_index_groups=same_core)  3.56 us
    ppermute x1, starting transfers between devices, shards(): tokens_far = lax.ppermute(updated, 'row', far)  2.86 us
    unnamed x38, local copies, waits for them, and re-layouts  2.43 us
    all_to_all x1, waiting for transfers between devices, shards(): lax.all_to_all(normed, 'row', 0, 0, tiled=True, axis_index_groups=same_core)  2.31 us
    ppermute x1, starting transfers between devices, shards(): other = lax.ppermute(mine, 'row', cores)  2.02 us
  transfers between devices with their start and end apart: 7, of which 5 were waited for; matrix products, arithmetic and copies ran while one was open for 0% of the time, Pallas kernels for 18%

profile of v4, /device:TPU:1, one launch (start us, length us, event | category | flops | bytes accessed | tf_op | source)
XLA Modules:
  0.0 39.8 jit_solution(11527628667385708356)
XLA Ops:
  0.6 0.0 copy-start.16
  0.6 0.0 copy-start.12
  0.7 0.0 copy-start.13
  0.7 0.0 copy-start.14
  0.7 0.1 collective-permute-start
  0.8 4.5 %collective-permute-start.1 = (bf16[256,128]{1,0:T(8,128)(2,1)}, bf16[256,128]{1,0:T(8,128)(2,1)S(1)}, u32[]{:S(2)}, u32[]{:S(2)}) collective-permute-start(bf16[256,128]{1,0:T(8,128)(2,1)} %feat_ref.1), channel_id=1, source_target_pairs={{1,2},{3,4},{5,6},{7,8},{9,10},{11,12},{13,14},{2,1},{4,3},{6,5},{... | collective-permute-start | bytes 196616 | tf_op jit(solution)/shard_map/ppermute | solution.py:355
  5.3 0.0 copy-done.16
  5.3 0.0 copy-done.12
  5.3 0.0 copy-done.13
  5.3 0.0 copy-done.14
  5.3 0.0 copy-start.2
  5.4 0.0 copy-start.10
  5.4 0.0 copy-start.15
  5.4 0.7 %shard_map.197 = s32[16,1,128]{2,1,0:T(1,128)} custom-call(s32[8,128]{1,0:T(8,128)S(1)} %shard_map.196.zero_ref, s32[1,16]{1,0:T(1,128)S(1)} %bitcast.9, s32[1,16]{1,0:T(1,128)S(1)} %bitcast.10, s32[1,16]{1,0:T(1,128)S(1)} %bitcast.11, s32[1,8]{1,0:T(1,128)S(1)} %bitcast.12), custom_call_target="tpu_custom_call" | custom-call | flops 2000000000 | bytes 10000000 | tf_op jit(solution)/shard_map/pallas_call | solution.py:312
  6.1 5.3 %all-to-all-start = ((s32[16,1,128]{2,1,0:T(1,128)}), s32[16,1,128]{2,1,0:T(1,128)S(1)}, u32[]{:S(2)}, u32[]{:S(2)}) async-start(s32[16,1,128]{2,1,0:T(1,128)} %shard_map.197), calls=%async_computation | async-start | bytes 16384 | tf_op jit(solution)/shard_map/all_to_all | solution.py:366
  11.4 0.0 copy-done.2
  11.4 0.0 copy-done.10
  11.4 0.0 copy-done.15
  11.4 0.0 copy-start.3
  11.4 0.0 copy-start.5
  11.5 0.0 copy-start.6
  11.5 0.0 copy-start.8
  11.5 0.0 copy-start.17
  11.5 1.8 %shard_map.194.bias_ref = f32[256,256]{1,0:T(8,128)S(1)} custom-call(bf16[16,256,128]{2,1,0:T(8,128)(2,1)S(1)} %copy-done.2, f32[128]{0:T(128)S(1)} %copy-done.15, bf16[16,128]{1,0:T(8,128)(2,1)S(1)} %bitcast.8), custom_call_target="tpu_custom_call" | custom-call | flops 2000000000 | bytes 10000000 | tf_op jit(solution)/shard_map/pallas_call | solution.py:312
  13.3 0.0 copy-start.7
  13.3 0.0 copy-start.9
  13.3 0.0 copy-start.11
  13.3 0.0 collective-permute-done.core_ref
  13.3 0.0 collective-permute-done.1.far_ref
  13.3 0.0 copy-done.3
  13.3 0.0 copy-done.5
  13.4 0.0 copy-done.6
  13.4 0.0 copy-done.8
  13.4 0.0 copy-done.17
  13.4 1.9 %shard_map.195 = (bf16[512,384]{1,0:T(8,128)(2,1)S(1)}, bf16[256,128]{1,0:T(8,128)(2,1)S(1)}, bf16[256,768]{1,0:T(8,128)(2,1)S(1)}) custom-call(bf16[256,128]{1,0:T(8,128)(2,1)S(1)} %copy-done.6, bf16[256,128]{1,0:T(8,128)(2,1)S(1)} %collective-permute-done.core_ref, bf16[256,128]{1,0:T(8,128)(2,1)S(1)} %collective-permute-done.1.far_ref, ...), custom_call_target="tpu_custom_call" | custom-call | flops 2000000000 | bytes 10000000 | tf_op jit(solution)/shard_map/pallas_call | solution.py:312
  15.3 1.8 %all-to-all-done = s32[16,1,128]{2,1,0:T(1,128)S(1)} async-done(((s32[16,1,128]{2,1,0:T(1,128)}), s32[16,1,128]{2,1,0:T(1,128)S(1)}, u32[]{:S(2)}, u32[]{:S(2)}) %all-to-all-start) | async-done | bytes 8224 | tf_op jit(solution)/shard_map/all_to_all | solution.py:366
  17.1 0.0 copy-done.7
  17.1 0.0 copy-done.9
  17.1 0.0 copy-done.11
  17.1 0.0 copy-start.18
  17.1 2.0 %shard_map.198 = (f32[16,768]{1,0:T(8,128)S(1)}, bf16[8,16,768]{2,1,0:T(8,128)(2,1)}) custom-call(bf16[512,384]{1,0:T(8,128)(2,1)S(1)} %get-tuple-element.18.proj_ref, bf16[256,768]{1,0:T(8,128)(2,1)S(1)} %get-tuple-element.19.lifted_ref, bf16[256,128]{1,0:T(8,128)(2,1)S(1)} %collective-permute-done.core_ref, ...), custom_call_target="tpu_custom_call" | custom-call | flops 2000000000 | bytes 10000000 | tf_op jit(solution)/shard_map/pallas_call | solution.py:312
  19.2 3.6 %all-to-all-start.1 = ((bf16[8,16,768]{2,1,0:T(8,128)(2,1)}), bf16[8,16,768]{2,1,0:T(8,128)(2,1)S(1)}, u32[]{:S(2)}, u32[]{:S(2)}) async-start(bf16[8,16,768]{2,1,0:T(8,128)(2,1)} %get-tuple-element.20.normed_ref), calls=%async_computation.1 | async-start | bytes 393216 | tf_op jit(solution)/shard_map/all_to_all | solution.py:402
  22.7 0.0 copy-done.18
  22.7 0.0 copy-start
  22.7 2.3 %copy-done = bf16[768,3072]{1,0:T(8,128)(2,1)S(1)} copy-done((bf16[768,3072]{1,0:T(8,128)(2,1)S(1)}, bf16[768,3072]{1,0:T(8,128)(2,1)}, u32[]{:S(2)}) %copy-start) | copy-done | bytes 4718616
  25.1 0.0 copy-start.1
  25.1 2.2 %shard_map.199 = (bf16[256,768]{1,0:T(8,128)(2,1)S(1)}, f32[16,768]{1,0:T(8,128)S(1)}, f32[256,256]{1,0:T(8,128)S(1)}, bf16[256,128]{1,0:T(8,128)(2,1)S(1)}, bf16[768,768]{1,0:T(8,128)(2,1)S(1)}) custom-call(bf16[8,16,768]{2,1,0:T(8,128)(2,1)} %get-tuple-element.20.normed_ref, s32[16,128]{1,0:T(8,128)S(1)} %bitcast.7, ...), custom_call_target="tpu_custom_call", output_to_operand_aliasing={{2}: (2, {})} | custom-call | flops 2000000000 | bytes 10000000 | tf_op jit(solution)/shard_map/pallas_call | solution.py:312
  27.3 2.3 %all-to-all-done.1.mine_ref = bf16[8,16,768]{2,1,0:T(8,128)(2,1)S(1)} async-done(((bf16[8,16,768]{2,1,0:T(8,128)(2,1)}), bf16[8,16,768]{2,1,0:T(8,128)(2,1)S(1)}, u32[]{:S(2)}, u32[]{:S(2)}) %all-to-all-start.1) | async-done | bytes 196640 | tf_op jit(solution)/shard_map/all_to_all | solution.py:402
  29.6 2.0 %collective-permute-start.2 = (bf16[8,16,768]{2,1,0:T(8,128)(2,1)S(1)}, bf16[8,16,768]{2,1,0:T(8,128)(2,1)S(1)}, u32[]{:S(2)}, u32[]{:S(2)}) collective-permute-start(bf16[8,16,768]{2,1,0:T(8,128)(2,1)S(1)} %all-to-all-done.1.mine_ref), channel_id=1, source_target_pairs={{0,1},{1,0},{2,3},{3,2},{4,5},{5,4},{6,7},{7,6},{8,9},{9,8},{10,11... | collective-permute-start | bytes 589832 | tf_op jit(solution)/shard_map/ppermute | solution.py:421
  31.6 1.1 %collective-permute-done.2.other_ref = bf16[8,16,768]{2,1,0:T(8,128)(2,1)S(1)} collective-permute-done((bf16[8,16,768]{2,1,0:T(8,128)(2,1)S(1)}, bf16[8,16,768]{2,1,0:T(8,128)(2,1)S(1)}, u32[]{:S(2)}, u32[]{:S(2)}) %collective-permute-start.2) | collective-permute-done | bytes 196640 | tf_op jit(solution)/shard_map/ppermute | solution.py:421
  32.7 0.0 copy-done.1
  32.7 0.0 copy-start.4
  32.7 1.0 %shard_map.200.own_ref = bf16[16,768]{1,0:T(8,128)(2,1)S(1)} custom-call(bf16[8,16,768]{2,1,0:T(8,128)(2,1)S(1)} %all-to-all-done.1.mine_ref, bf16[8,16,768]{2,1,0:T(8,128)(2,1)S(1)} %collective-permute-done.2.other_ref, bf16[256,768]{1,0:T(8,128)(2,1)S(1)} %get-tuple-element.23.query_ref, f32[256,256]{1,0:T(8,128)S(1)} %get-tuple-element.24.biased_ref, ...), custom_call_target="tpu_custom_call" | custom-call | flops 2000000000 | bytes 10000000 | tf_op jit(solution)/shard_map/pallas_call | solution.py:312
  33.7 2.9 %collective-permute-start.4 = (bf16[16,768]{1,0:T(8,128)(2,1)S(1)}, bf16[16,768]{1,0:T(8,128)(2,1)S(1)}, u32[]{:S(2)}, u32[]{:S(2)}) collective-permute-start(bf16[16,768]{1,0:T(8,128)(2,1)S(1)} %shard_map.200.own_ref), channel_id=1, source_target_pairs={{1,2},{3,4},{5,6},{7,8},{9,10},{11,12},{13,14},{2,1},{4,3},{6,5},{... | collective-permute-start | bytes 73736 | tf_op jit(solution)/shard_map/ppermute | solution.py:434
  36.6 0.0 copy-done.4
  36.6 0.6 %shard_map.201 = (bf16[16,128]{1,0:T(8,128)(2,1)S(1)}, f32[256,128]{1,0:T(8,128)S(1)}, bf16[16,768]{1,0:T(8,128)(2,1)}) custom-call(bf16[256,128]{1,0:T(8,128)(2,1)S(1)} %get-tuple-element.17.mid_ref, bf16[16,768]{1,0:T(8,128)(2,1)S(1)} %shard_map.200.own_ref, bf16[256,128]{1,0:T(8,128)(2,1)S(1)} %get-tuple-element.28.pick_ref, bf16[768,128]{1,0:T(8,128)(2,1)S(1)} %copy-done.4), custom_call_target="tpu_custom_call" | custom-call | flops 2000000000 | bytes 10000000 | tf_op jit(solution)/shard_map/pallas_call | solution.py:312
  37.2 0.0 collective-permute-start.3
  37.2 1.2 %collective-permute-done.3.core_ref = bf16[16,128]{1,0:T(8,128)(2,1)S(1)} collective-permute-done((bf16[16,128]{1,0:T(8,128)(2,1)S(1)}, bf16[16,128]{1,0:T(8,128)(2,1)S(1)}, u32[]{:S(2)}, u32[]{:S(2)}) %collective-permute-start.3) | collective-permute-done | bytes 4128 | tf_op jit(solution)/shard_map/ppermute | solution.py:443
  38.4 0.5 %collective-permute-done.4.far_ref = bf16[16,768]{1,0:T(8,128)(2,1)S(1)} collective-permute-done((bf16[16,768]{1,0:T(8,128)(2,1)S(1)}, bf16[16,768]{1,0:T(8,128)(2,1)S(1)}, u32[]{:S(2)}, u32[]{:S(2)}) %collective-permute-start.4) | collective-permute-done | bytes 24608 | tf_op jit(solution)/shard_map/ppermute | solution.py:434
  38.9 0.9 %shard_map.202 = bf16[256,128]{1,0:T(8,128)(2,1)} custom-call(f32[256,128]{1,0:T(8,128)S(1)} %get-tuple-element.29.partial_ref, bf16[16,128]{1,0:T(8,128)(2,1)S(1)} %collective-permute-done.3.core_ref, bf16[16,768]{1,0:T(8,128)(2,1)S(1)} %collective-permute-done.4.far_ref, bf16[256,128]{1,0:T(8,128)(2,1)S(1)} %get-tuple-element.28.pick_ref, ...), custom_call_target="tpu_custom_call" | custom-call | flops 2000000000 | bytes 10000000 | tf_op jit(solution)/shard_map/pallas_call | solution.py:312
  (1 shorter events, 0.0 us)
Async XLA Ops:
  0.6 4.7 %copy-start.16 = (s32[8]{0:T(128)S(1)}, s32[8]{0:T(128)}, u32[]{:S(2)}) copy-start(s32[8]{0:T(128)} %param.20) | copy-start | bytes 100
  0.6 4.7 %copy-start.12 = (s32[16]{0:T(128)S(1)}, s32[16]{0:T(128)}, u32[]{:S(2)}) copy-start(s32[16]{0:T(128)} %param.21) | copy-start | bytes 196
  0.7 4.7 %copy-start.13 = (s32[16]{0:T(128)S(1)}, s32[16]{0:T(128)}, u32[]{:S(2)}) copy-start(s32[16]{0:T(128)} %param.23) | copy-start | bytes 196
  0.7 4.7 %copy-start.14 = (s32[16]{0:T(128)S(1)}, s32[16]{0:T(128)}, u32[]{:S(2)}) copy-start(s32[16]{0:T(128)} %param.22) | copy-start | bytes 196
  0.7 12.6 %collective-permute-start = (bf16[256,128]{1,0:T(8,128)(2,1)}, bf16[256,128]{1,0:T(8,128)(2,1)S(1)}, u32[]{:S(2)}, u32[]{:S(2)}) collective-permute-start(bf16[256,128]{1,0:T(8,128)(2,1)} %feat_ref.1), channel_id=1, source_target_pairs={{0,1},{1,0},{2,3},{3,2},{4,5},{5,4},{6,7},{7,6},{8,9},{9,8},{10,11... | collective-permute-start | bytes 196616 | tf_op jit(solution)/shard_map/ppermute | solution.py:356
  0.8 12.5 %collective-permute-start.1 = (bf16[256,128]{1,0:T(8,128)(2,1)}, bf16[256,128]{1,0:T(8,128)(2,1)S(1)}, u32[]{:S(2)}, u32[]{:S(2)}) collective-permute-start(bf16[256,128]{1,0:T(8,128)(2,1)} %feat_ref.1), channel_id=1, source_target_pairs={{1,2},{3,4},{5,6},{7,8},{9,10},{11,12},{13,14},{2,1},{4,3},{6,5},{... | collective-permute-start | bytes 196616 | tf_op jit(solution)/shard_map/ppermute | solution.py:355
  5.3 6.1 %copy-start.2 = (bf16[16,256,128]{2,1,0:T(8,128)(2,1)S(1)}, bf16[16,256,128]{2,1,0:T(8,128)(2,1)}, u32[]{:S(2)}) copy-start(bf16[16,256,128]{2,1,0:T(8,128)(2,1)} %pair_ref.1) | copy-start | bytes 3145732
  5.4 6.1 %copy-start.10 = (bf16[128,16]{0,1:T(8,128)(2,1)S(1)}, bf16[128,16]{0,1:T(8,128)(2,1)}, u32[]{:S(2)}) copy-start(bf16[128,16]{0,1:T(8,128)(2,1)} %param.35) | copy-start | bytes 12292
  5.4 6.1 %copy-start.15 = (f32[128]{0:T(128)S(1)}, f32[128]{0:T(128)}, u32[]{:S(2)}) copy-start(f32[128]{0:T(128)} %gain_ref.3) | copy-start | bytes 1540
  6.1 11.0 %all-to-all-start = ((s32[16,1,128]{2,1,0:T(1,128)}), s32[16,1,128]{2,1,0:T(1,128)S(1)}, u32[]{:S(2)}, u32[]{:S(2)}) async-start(s32[16,1,128]{2,1,0:T(1,128)} %shard_map.197), calls=%async_computation | async-start | bytes 16384 | tf_op jit(solution)/shard_map/all_to_all | solution.py:366
  11.4 1.9 %copy-start.3 = (bf16[128,768]{1,0:T(8,128)(2,1)S(1)}, bf16[128,768]{1,0:T(8,128)(2,1)}, u32[]{:S(2)}) copy-start(bf16[128,768]{1,0:T(8,128)(2,1)} %pool_ref.3) | copy-start | bytes 589828
  11.4 1.9 %copy-start.5 = (bf16[128,384]{1,0:T(8,128)(2,1)S(1)}, bf16[128,384]{1,0:T(8,128)(2,1)}, u32[]{:S(2)}) copy-start(bf16[128,384]{1,0:T(8,128)(2,1)} %qkv_ref.1) | copy-start | bytes 294916
  11.5 1.9 %copy-start.6 = (bf16[256,128]{1,0:T(8,128)(2,1)S(1)}, bf16[256,128]{1,0:T(8,128)(2,1)}, u32[]{:S(2)}) copy-start(bf16[256,128]{1,0:T(8,128)(2,1)} %feat_ref.1) | copy-start | bytes 196612
  11.5 1.9 %copy-start.8 = (bf16[128,128]{1,0:T(8,128)(2,1)S(1)}, bf16[128,128]{1,0:T(8,128)(2,1)}, u32[]{:S(2)}) copy-start(bf16[128,128]{1,0:T(8,128)(2,1)} %out_ref.4) | copy-start | bytes 98308
  11.5 1.9 %copy-start.17 = (f32[128]{0:T(128)S(1)}, f32[128]{0:T(128)}, u32[]{:S(2)}) copy-start(f32[128]{0:T(128)} %gain_ref.4) | copy-start | bytes 1540
  13.3 3.8 %copy-start.7 = (bf16[32,768]{1,0:T(8,128)(2,1)S(1)}, bf16[32,768]{1,0:T(8,128)(2,1)}, u32[]{:S(2)}) copy-start(bf16[32,768]{1,0:T(8,128)(2,1)} %restype_ref.1) | copy-start | bytes 147460
  13.3 3.8 %copy-start.9 = (bf16[16,768]{1,0:T(8,128)(2,1)S(1)}, bf16[16,768]{1,0:T(8,128)(2,1)}, u32[]{:S(2)}) copy-start(bf16[16,768]{1,0:T(8,128)(2,1)} %single_ref.1) | copy-start | bytes 73732
  13.3 3.8 %copy-start.11 = (f32[768]{0:T(1024)S(1)}, f32[768]{0:T(1024)}, u32[]{:S(2)}) copy-start(f32[768]{0:T(1024)} %gain_ref.5) | copy-start | bytes 9220
  17.1 5.6 %copy-start.18 = (f32[16]{0:T(128)S(1)}, f32[16]{0:T(128)}, u32[]{:S(2)}) copy-start(f32[16]{0:T(128)} %chain_weight_ref.1) | copy-start | bytes 196
  19.2 10.4 %all-to-all-start.1 = ((bf16[8,16,768]{2,1,0:T(8,128)(2,1)}), bf16[8,16,768]{2,1,0:T(8,128)(2,1)S(1)}, u32[]{:S(2)}, u32[]{:S(2)}) async-start(bf16[8,16,768]{2,1,0:T(8,128)(2,1)} %get-tuple-element.20.normed_ref), calls=%async_computation.1 | async-start | bytes 393216 | tf_op jit(solution)/shard_map/all_to_all | solution.py:402
  22.7 2.3 %copy-start = (bf16[768,3072]{1,0:T(8,128)(2,1)S(1)}, bf16[768,3072]{1,0:T(8,128)(2,1)}, u32[]{:S(2)}) copy-start(bf16[768,3072]{1,0:T(8,128)(2,1)} %proj_ref.1) | copy-start | bytes 14155780
  25.1 7.6 %copy-start.1 = (bf16[768,768]{1,0:T(8,128)(2,1)S(1)}, bf16[768,768]{1,0:T(8,128)(2,1)}, u32[]{:S(2)}) copy-start(bf16[768,768]{1,0:T(8,128)(2,1)} %out_ref.5) | copy-start | bytes 3538948
  29.6 3.1 %collective-permute-start.2 = (bf16[8,16,768]{2,1,0:T(8,128)(2,1)S(1)}, bf16[8,16,768]{2,1,0:T(8,128)(2,1)S(1)}, u32[]{:S(2)}, u32[]{:S(2)}) collective-permute-start(bf16[8,16,768]{2,1,0:T(8,128)(2,1)S(1)} %all-to-all-done.1.mine_ref), channel_id=1, source_target_pairs={{0,1},{1,0},{2,3},{3,2},{4,5},{5,4},{6,7},{7,6},{8,9},{9,8},{10,11... | collective-permute-start | bytes 589832 | tf_op jit(solution)/shard_map/ppermute | solution.py:421
  32.7 3.9 %copy-start.4 = (bf16[768,128]{1,0:T(8,128)(2,1)S(1)}, bf16[768,128]{1,0:T(8,128)(2,1)}, u32[]{:S(2)}) copy-start(bf16[768,128]{1,0:T(8,128)(2,1)} %weight_ref.3) | copy-start | bytes 589828
  33.7 5.1 %collective-permute-start.4 = (bf16[16,768]{1,0:T(8,128)(2,1)S(1)}, bf16[16,768]{1,0:T(8,128)(2,1)S(1)}, u32[]{:S(2)}, u32[]{:S(2)}) collective-permute-start(bf16[16,768]{1,0:T(8,128)(2,1)S(1)} %shard_map.200.own_ref), channel_id=1, source_target_pairs={{1,2},{3,4},{5,6},{7,8},{9,10},{11,12},{13,14},{2,1},{4,3},{6,5},{... | collective-permute-start | bytes 73736 | tf_op jit(solution)/shard_map/ppermute | solution.py:434
  37.2 1.2 %collective-permute-start.3 = (bf16[16,128]{1,0:T(8,128)(2,1)S(1)}, bf16[16,128]{1,0:T(8,128)(2,1)S(1)}, u32[]{:S(2)}, u32[]{:S(2)}) collective-permute-start(bf16[16,128]{1,0:T(8,128)(2,1)S(1)} %get-tuple-element.30), channel_id=1, source_target_pairs={{0,1},{1,0},{2,3},{3,2},{4,5},{5,4},{6,7},{7,6},{8,9},{9,8},{10,11... | collective-permute-start | bytes 12296 | tf_op jit(solution)/shard_map/ppermute | solution.py:443

commit v5 on v4

--- a/solution.py
+++ b/solution.py
@@ -25,7 +25,6 @@
 NEG = -1e30
 F32 = jnp.float32
 BF16 = jnp.bfloat16
-COUNT, CHAIN, RES, WIN = 0, 16, 32, 48
 TABLE = 128
 
 
@@ -57,7 +56,7 @@
 
 
 def atoms_before(table, row, tokens):
-    keep = (iota(table.shape, 0) < row) & (iota(table.shape, 1) < COUNT + tokens)
+    keep = (iota(table.shape, 0) < row) & (iota(table.shape, 1) < tokens)
     return jnp.sum(jnp.sum(jnp.where(keep, table, 0), axis=0, keepdims=True), axis=1, keepdims=True)
 
 
@@ -67,14 +66,16 @@
 
 def table_kernel(zero_ref, count_ref, chain_ref, kind_ref, window_ref, table_ref):
     row = zero_ref[:1]
-    pieces = ((COUNT, count_ref), (CHAIN, chain_ref), (RES, kind_ref), (WIN, window_ref))
-    for base, ref in pieces:
+    pieces = (count_ref, chain_ref, kind_ref, window_ref)
+    base = 0
+    for ref in pieces:
         size = ref.shape[1]
         shape = (size, TABLE)
         at = iota(shape, 1) == iota(shape, 0) + base
         eye = iota((size, size), 0) == iota((size, size), 1)
         values = jnp.sum(jnp.where(eye, ref[...], 0), axis=1, keepdims=True)
         row = row + jnp.sum(jnp.where(at, values, 0), axis=0, keepdims=True)
+        base += size
     table_ref[...] = jnp.broadcast_to(row[None], table_ref.shape)
 
 
@@ -85,13 +86,17 @@
         bias_ref[t * HEADS : (t + 1) * HEADS, :] = dot_nt(weight, normed)
 
 
-def attend_window(queries, keys, values, start, begin, atoms):
-    count, extent = queries.shape[0], keys.shape[0]
-    head = iota((count, CA), 1) // ADIM
+def window_scores(queries, keys):
+    head = iota(queries.shape, 1) // ADIM
     stacked = jnp.concatenate(
         [jnp.where(head == h, queries, jnp.zeros_like(queries)) for h in range(AHEADS)], axis=0
     )
-    scores = dot_nt(stacked, keys) * (1.0 / math.sqrt(ADIM))
+    return dot_nt(stacked, keys) * (1.0 / math.sqrt(ADIM))
+
+
+def attend_window(scores, values, start, begin, atoms):
+    count, extent = scores.shape[0] // AHEADS, scores.shape[1]
+    head = iota((count, CA), 1) // ADIM
     place = iota((count, extent), 1) + begin
     inside = (place >= start) & (place < start + KWIN) & (place >= 0) & (place < atoms)
     inside = jnp.concatenate([inside.astype(F32)] * AHEADS, axis=0) > 0.5
@@ -120,21 +125,25 @@
 
 def atom_kernel(
     n, feat_ref, core_ref, far_ref, window_ref, gain_ref, qkv_ref, out_ref, pool_ref, bias_ref,
-    proj_ref, mid_ref, lifted_ref,
+    values_ref, scores_ref, mid_ref, lifted_ref,
 ):
     me = lax.axis_index("row")
     rows = feat_ref.shape[0]
     left, right = edges(core_ref[...], far_ref[...], rows)
     feat = jnp.concatenate([left, feat_ref[...], right], axis=0).astype(F32)
     proj = dot(norm(feat, gain_ref[...]).astype(BF16), qkv_ref[...]).astype(BF16)
-    proj_ref[...] = proj
+    values_ref[...] = proj[:, 2 * CA :]
+    for i, (at, base) in enumerate(((HALF - REACH, 0), (HALF + rows, rows))):
+        part = window_scores(
+            proj[at : at + REACH, :CA], proj[base : base + 2 * HALF, CA : 2 * CA]
+        )
+        scores_ref[i] = part
     for s in range(rows // HALF):
         own = slice(HALF * s, HALF * s + HALF)
         ext = slice(HALF * s + HALF, HALF * s + 2 * HALF)
         near = slice(HALF * s + HALF - REACH, HALF * s + 3 * HALF - REACH)
         mixed = attend_window(
-            proj[ext, :CA],
-            proj[near, CA : 2 * CA],
+            window_scores(proj[ext, :CA], proj[near, CA : 2 * CA]),
             proj[near, 2 * CA :],
             block_starts(window_ref[...], HALF, s * HALF // QBLK),
             me * rows + HALF * s - REACH,
@@ -146,7 +155,7 @@
 
 
 def state_kernel(
-    n, proj_ref, lifted_ref, core_ref, far_ref, table_ref, single_ref, out_ref, pool_ref, restype_ref, gain_ref,
+    n, values_ref, scores_ref, lifted_ref, core_ref, far_ref, table_ref, single_ref, out_ref, pool_ref, restype_ref, gain_ref,
     state_ref, normed_ref,
 ):
     me = lax.axis_index("row")
@@ -155,18 +164,15 @@
     table = table_ref[...]
     own_row = table_row(table, me)
     windows = rows // QBLK
-    size = 2 * HALF
     mixed = []
-    for at, base, row, first in (
-        (HALF - REACH, 0, me - 1, windows - REACH // QBLK),
-        (HALF + rows, rows + 2 * HALF - size, me + 1, 0),
+    for i, (base, row, first) in enumerate(
+        ((0, me - 1, windows - REACH // QBLK), (rows, me + 1, 0))
     ):
         mixed.append(
             attend_window(
-                proj_ref[at : at + REACH, :CA],
-                proj_ref[base : base + size, CA : 2 * CA],
-                proj_ref[base : base + size, 2 * CA :],
-                block_starts(table_row(table, row), REACH, WIN + first),
+                scores_ref[i],
+                values_ref[base : base + 2 * HALF, :],
+                block_starts(table_row(table, row), REACH, 3 * tokens + first),
                 me * rows - HALF + base,
                 n * rows,
             )
@@ -175,9 +181,9 @@
     feat = jnp.concatenate([left[HALF - REACH :], right[:REACH]], axis=0).astype(F32)
     mid = (feat + dot(jnp.concatenate(mixed, axis=0), out_ref[...])).astype(BF16)
     beside = jnp.maximum(dot(mid, pool_ref[...]), 0.0).astype(BF16)
-    count = column(own_row, COUNT, tokens)
+    count = column(own_row, 0, tokens)
     shape = (tokens, TABLE)
-    ahead = (iota(shape, 1) >= COUNT) & (iota(shape, 1) < COUNT + iota(shape, 0))
+    ahead = iota(shape, 1) < iota(shape, 0)
     begin = atoms_before(table, me, tokens) - me * rows
     begin = begin + jnp.sum(jnp.where(ahead, own_row, 0), axis=1, keepdims=True)
     atom = iota((tokens, rows), 1)
@@ -187,7 +193,7 @@
     atom = jnp.where(lane < REACH, lane - REACH, lane - REACH + rows)
     chosen = (atom >= begin) & (atom < begin + count)
     pooled = pooled + dot(jnp.where(chosen, 1.0, 0.0).astype(BF16), beside)
-    kind = column(own_row, RES, tokens)
+    kind = column(own_row, 2 * tokens, tokens)
     onehot = jnp.where(iota((tokens, RESTYPES), 1) == kind, 1.0, 0.0).astype(BF16)
     state = single_ref[...].astype(F32) + pooled / count.astype(F32)
     state = state + dot(onehot, restype_ref[...])
@@ -207,11 +213,11 @@
     me = lax.axis_index("row")
     normed = normed_ref[0]
     tokens = normed.shape[0]
-    query = dot(normed, proj_ref[:, :CS]).astype(BF16)
+    query = dot(normed, proj_ref[:, :CS]).astype(BF16).astype(F32)
     head = iota((HEADS, CS), 1) // HDIM == iota((HEADS, CS), 0)
     spread = jnp.concatenate(
         [
-            jnp.where(head, jnp.broadcast_to(query[t : t + 1].astype(F32), (HEADS, CS)), 0.0)
+            jnp.where(head, jnp.broadcast_to(query[t : t + 1], (HEADS, CS)), 0.0)
             for t in range(tokens)
         ],
         axis=0,
@@ -221,7 +227,7 @@
     n = table.shape[0]
     keys = n * tokens
     shape = (TABLE, keys)
-    pick = jnp.where(iota(shape, 0) == CHAIN + iota(shape, 1) % tokens, 1.0, 0.0).astype(BF16)
+    pick = jnp.where(iota(shape, 0) == tokens + iota(shape, 1) % tokens, 1.0, 0.0).astype(BF16)
     each = dot(table.astype(F32).astype(BF16), pick)
     shape = (n, keys)
     chain_keys = jnp.sum(
@@ -229,22 +235,22 @@
     )
     own_row = table_row(table, me)
     shape = (tokens * HEADS, TABLE)
-    mine = iota(shape, 1) == CHAIN + iota(shape, 0) // HEADS
+    mine = iota(shape, 1) == tokens + iota(shape, 0) // HEADS
     chain_rows = jnp.sum(jnp.where(mine, own_row, 0), axis=1, keepdims=True).astype(F32)
     shape = (tokens * HEADS, HEADS)
     mine = iota(shape, 1) == iota(shape, 0) % HEADS
     weight = jnp.sum(jnp.where(mine, chain_weight_ref[...], 0.0), axis=1, keepdims=True)
     biased_ref[...] = bias_ref[...] + jnp.where(chain_rows == chain_keys, weight, 0.0)
     rows = pick_ref.shape[0]
-    counts = jnp.where(iota(table.shape, 1) < COUNT + tokens, table, 0).astype(F32).astype(BF16)
+    counts = jnp.where(iota(table.shape, 1) < tokens, table, 0).astype(F32).astype(BF16)
     begin = jnp.zeros((1, TABLE), F32)
     size = jnp.zeros((1, TABLE), F32)
     for step in range(3):
         shape = (TABLE, TABLE)
         token = iota(shape, 1) - step * tokens
         here = (token >= 0) & (token < tokens)
-        ahead = jnp.where(here & (iota(shape, 0) < COUNT + token), 1.0, 0.0).astype(BF16)
-        equal = jnp.where(here & (iota(shape, 0) == COUNT + token), 1.0, 0.0).astype(BF16)
+        ahead = jnp.where(here & (iota(shape, 0) < token), 1.0, 0.0).astype(BF16)
+        equal = jnp.where(here & (iota(shape, 0) == token), 1.0, 0.0).astype(BF16)
         at = iota(table.shape, 0) == me + step - 1
         begin += jnp.sum(jnp.where(at, dot(counts, ahead), 0.0), axis=0, keepdims=True)
         size += jnp.sum(jnp.where(at, dot(counts, equal), 0.0), axis=0, keepdims=True)
@@ -368,10 +374,11 @@
     bias = call(
         pair_kernel, shape_of((tokens * HEADS, extent), F32), pair, pair_gain, pair_bias_weight.T
     )
-    proj, mid, lifted = call(
+    values, scores, mid, lifted = call(
         functools.partial(atom_kernel, n),
         (
-            shape_of((rows + 2 * HALF, 3 * CA), BF16),
+            shape_of((rows + 2 * HALF, CA), BF16),
+            shape_of((2, AHEADS * REACH, 2 * HALF), F32),
             shape_of((rows, CA), BF16),
             shape_of((rows, CS), BF16),
         ),
@@ -388,7 +395,8 @@
     state, normed = call(
         functools.partial(state_kernel, n),
         (shape_of((tokens, CS), F32), shape_of((n // 2, tokens, CS), BF16)),
-        proj,
+        values,
+        scores,
         lifted,
         feat_core,
         feat_far,

time: 40.1 us -> 39.9 us (level)
  transfers between devices with their start and end apart: 7 -> 7, of which waited for: 5 -> 5; matrix products, arithmetic and copies ran while one was open for 0% -> 0% of each run, Pallas kernels for 18% -> 19%
where the time goes in v5:
time: 39.9 us; the launch traced here: 39.6 us
  starting transfers between devices  18.4 us (46%)
  Pallas kernels  11 us (28%)
  waiting for transfers between devices  6.78 us (17%)
  local copies, waits for them, and re-layouts  2.43 us (6%)
  between operations  0.92 us (2%)
    pallas_call x9, Pallas kernels, call(): pl.pallas_call(kernel, out_shape=outs, in_specs=[spec] * len(args), out_s...  11 us
    all_to_all x1, starting transfers between devices, shards(): table = lax.all_to_all(table, 'row', 0, 0, tiled=True).reshape(n, TABLE)  5.31 us
    ppermute x1, starting transfers between devices, shards(): feat_far = lax.ppermute(atom_feat, 'row', far)  4.5 us
    all_to_all x1, starting transfers between devices, shards(): lax.all_to_all(normed, 'row', 0, 0, tiled=True, axis_index_groups=same_core)  3.62 us
    ppermute x1, starting transfers between devices, shards(): tokens_far = lax.ppermute(updated, 'row', far)  2.86 us
    unnamed x38, local copies, waits for them, and re-layouts  2.43 us
    all_to_all x1, waiting for transfers between devices, shards(): lax.all_to_all(normed, 'row', 0, 0, tiled=True, axis_index_groups=same_core)  2.31 us
    ppermute x1, starting transfers between devices, shards(): other = lax.ppermute(mine, 'row', cores)  2.02 us
  transfers between devices with their start and end apart: 7, of which 5 were waited for; matrix products, arithmetic and copies ran while one was open for 0% of the time, Pallas kernels for 19%

profile of v5, /device:TPU:1, one launch (start us, length us, event | category | flops | bytes accessed | tf_op | source)
XLA Modules:
  0.0 39.6 jit_solution(7860640714260206452)
XLA Ops:
  0.6 0.0 copy-start.16
  0.6 0.0 copy-start.12
  0.7 0.0 copy-start.13
  0.7 0.0 copy-start.14
  0.7 0.1 collective-permute-start
  0.8 4.5 %collective-permute-start.1 = (bf16[256,128]{1,0:T(8,128)(2,1)}, bf16[256,128]{1,0:T(8,128)(2,1)S(1)}, u32[]{:S(2)}, u32[]{:S(2)}) collective-permute-start(bf16[256,128]{1,0:T(8,128)(2,1)} %feat_ref.1), channel_id=1, source_target_pairs={{1,2},{3,4},{5,6},{7,8},{9,10},{11,12},{13,14},{2,1},{4,3},{6,5},{... | collective-permute-start | bytes 196616 | tf_op jit(solution)/shard_map/ppermute | solution.py:361
  5.3 0.0 copy-done.16
  5.3 0.0 copy-done.12
  5.3 0.0 copy-done.13
  5.3 0.0 copy-done.14
  5.3 0.0 copy-start.2
  5.4 0.0 copy-start.10
  5.4 0.0 copy-start.15
  5.4 0.7 %shard_map.197 = s32[16,1,128]{2,1,0:T(1,128)} custom-call(s32[8,128]{1,0:T(8,128)S(1)} %shard_map.196.zero_ref, s32[1,16]{1,0:T(1,128)S(1)} %bitcast.9, s32[1,16]{1,0:T(1,128)S(1)} %bitcast.10, s32[1,16]{1,0:T(1,128)S(1)} %bitcast.11, s32[1,8]{1,0:T(1,128)S(1)} %bitcast.12), custom_call_target="tpu_custom_call" | custom-call | flops 2000000000 | bytes 10000000 | tf_op jit(solution)/shard_map/pallas_call | solution.py:318
  6.1 5.3 %all-to-all-start = ((s32[16,1,128]{2,1,0:T(1,128)}), s32[16,1,128]{2,1,0:T(1,128)S(1)}, u32[]{:S(2)}, u32[]{:S(2)}) async-start(s32[16,1,128]{2,1,0:T(1,128)} %shard_map.197), calls=%async_computation | async-start | bytes 16384 | tf_op jit(solution)/shard_map/all_to_all | solution.py:372
  11.4 0.0 copy-done.2
  11.4 0.0 copy-done.10
  11.4 0.0 copy-done.15
  11.4 0.0 copy-start.3
  11.4 0.0 copy-start.5
  11.5 0.0 copy-start.6
  11.5 0.0 copy-start.8
  11.5 0.0 copy-start.17
  11.5 1.8 %shard_map.194.bias_ref = f32[256,256]{1,0:T(8,128)S(1)} custom-call(bf16[16,256,128]{2,1,0:T(8,128)(2,1)S(1)} %copy-done.2, f32[128]{0:T(128)S(1)} %copy-done.15, bf16[16,128]{1,0:T(8,128)(2,1)S(1)} %bitcast.8), custom_call_target="tpu_custom_call" | custom-call | flops 2000000000 | bytes 10000000 | tf_op jit(solution)/shard_map/pallas_call | solution.py:318
  13.3 0.0 copy-start.7
  13.3 0.0 copy-start.9
  13.3 0.0 copy-start.11
  13.3 0.0 collective-permute-done.core_ref
  13.3 0.0 collective-permute-done.1.far_ref
  13.3 0.0 copy-done.3
  13.3 0.0 copy-done.5
  13.4 0.0 copy-done.6
  13.4 0.0 copy-done.8
  13.4 0.0 copy-done.17
  13.4 2.0 %shard_map.195 = (bf16[512,128]{1,0:T(8,128)(2,1)S(1)}, f32[2,256,256]{2,1,0:T(8,128)S(1)}, bf16[256,128]{1,0:T(8,128)(2,1)S(1)}, bf16[256,768]{1,0:T(8,128)(2,1)S(1)}) custom-call(bf16[256,128]{1,0:T(8,128)(2,1)S(1)} %copy-done.6, bf16[256,128]{1,0:T(8,128)(2,1)S(1)} %collective-permute-done.core_ref, bf16[256,128]{1,0:T(8,128)(2,1)S(1)} %collective-permute-done.1.far_ref, ...), custom_call_target="tpu_custom_call" | custom-call | flops 2000000000 | bytes 10000000 | tf_op jit(solution)/shard_map/pallas_call | solution.py:318
  15.3 1.8 %all-to-all-done = s32[16,1,128]{2,1,0:T(1,128)S(1)} async-done(((s32[16,1,128]{2,1,0:T(1,128)}), s32[16,1,128]{2,1,0:T(1,128)S(1)}, u32[]{:S(2)}, u32[]{:S(2)}) %all-to-all-start) | async-done | bytes 8224 | tf_op jit(solution)/shard_map/all_to_all | solution.py:372
  17.1 0.0 copy-done.7
  17.1 0.0 copy-done.9
  17.1 0.0 copy-done.11
  17.1 0.0 copy-start.18
  17.1 1.7 %shard_map.198 = (f32[16,768]{1,0:T(8,128)S(1)}, bf16[8,16,768]{2,1,0:T(8,128)(2,1)}) custom-call(bf16[512,128]{1,0:T(8,128)(2,1)S(1)} %get-tuple-element.19.values_ref, f32[2,256,256]{2,1,0:T(8,128)S(1)} %get-tuple-element.20.scores_ref, bf16[256,768]{1,0:T(8,128)(2,1)S(1)} %get-tuple-element.21.lifted_ref, ...), custom_call_target="tpu_custom_call" | custom-call | flops 2000000000 | bytes 10000000 | tf_op jit(solution)/shard_map/pallas_call | solution.py:318
  18.9 3.6 %all-to-all-start.1 = ((bf16[8,16,768]{2,1,0:T(8,128)(2,1)}), bf16[8,16,768]{2,1,0:T(8,128)(2,1)S(1)}, u32[]{:S(2)}, u32[]{:S(2)}) async-start(bf16[8,16,768]{2,1,0:T(8,128)(2,1)} %get-tuple-element.22.normed_ref), calls=%async_computation.1 | async-start | bytes 393216 | tf_op jit(solution)/shard_map/all_to_all | solution.py:410
  22.5 0.0 copy-done.18
  22.5 0.0 copy-start
  22.5 2.3 %copy-done = bf16[768,3072]{1,0:T(8,128)(2,1)S(1)} copy-done((bf16[768,3072]{1,0:T(8,128)(2,1)S(1)}, bf16[768,3072]{1,0:T(8,128)(2,1)}, u32[]{:S(2)}) %copy-start) | copy-done | bytes 4718616
  24.8 0.0 copy-start.1
  24.8 2.2 %shard_map.199 = (bf16[256,768]{1,0:T(8,128)(2,1)S(1)}, f32[16,768]{1,0:T(8,128)S(1)}, f32[256,256]{1,0:T(8,128)S(1)}, bf16[256,128]{1,0:T(8,128)(2,1)S(1)}, bf16[768,768]{1,0:T(8,128)(2,1)S(1)}) custom-call(bf16[8,16,768]{2,1,0:T(8,128)(2,1)} %get-tuple-element.22.normed_ref, s32[16,128]{1,0:T(8,128)S(1)} %bitcast.7, ...), custom_call_target="tpu_custom_call", output_to_operand_aliasing={{2}: (2, {})} | custom-call | flops 2000000000 | bytes 10000000 | tf_op jit(solution)/shard_map/pallas_call | solution.py:318
  27.1 2.3 %all-to-all-done.1.mine_ref = bf16[8,16,768]{2,1,0:T(8,128)(2,1)S(1)} async-done(((bf16[8,16,768]{2,1,0:T(8,128)(2,1)}), bf16[8,16,768]{2,1,0:T(8,128)(2,1)S(1)}, u32[]{:S(2)}, u32[]{:S(2)}) %all-to-all-start.1) | async-done | bytes 196640 | tf_op jit(solution)/shard_map/all_to_all | solution.py:410
  29.4 2.0 %collective-permute-start.2 = (bf16[8,16,768]{2,1,0:T(8,128)(2,1)S(1)}, bf16[8,16,768]{2,1,0:T(8,128)(2,1)S(1)}, u32[]{:S(2)}, u32[]{:S(2)}) collective-permute-start(bf16[8,16,768]{2,1,0:T(8,128)(2,1)S(1)} %all-to-all-done.1.mine_ref), channel_id=1, source_target_pairs={{0,1},{1,0},{2,3},{3,2},{4,5},{5,4},{6,7},{7,6},{8,9},{9,8},{10,11... | collective-permute-start | bytes 589832 | tf_op jit(solution)/shard_map/ppermute | solution.py:429
  31.4 1.1 %collective-permute-done.2.other_ref = bf16[8,16,768]{2,1,0:T(8,128)(2,1)S(1)} collective-permute-done((bf16[8,16,768]{2,1,0:T(8,128)(2,1)S(1)}, bf16[8,16,768]{2,1,0:T(8,128)(2,1)S(1)}, u32[]{:S(2)}, u32[]{:S(2)}) %collective-permute-start.2) | collective-permute-done | bytes 196640 | tf_op jit(solution)/shard_map/ppermute | solution.py:429
  32.5 0.0 copy-done.1
  32.5 0.0 copy-start.4
  32.5 1.0 %shard_map.200.own_ref = bf16[16,768]{1,0:T(8,128)(2,1)S(1)} custom-call(bf16[8,16,768]{2,1,0:T(8,128)(2,1)S(1)} %all-to-all-done.1.mine_ref, bf16[8,16,768]{2,1,0:T(8,128)(2,1)S(1)} %collective-permute-done.2.other_ref, bf16[256,768]{1,0:T(8,128)(2,1)S(1)} %get-tuple-element.25.query_ref, f32[256,256]{1,0:T(8,128)S(1)} %get-tuple-element.26.biased_ref, ...), custom_call_target="tpu_custom_call" | custom-call | flops 2000000000 | bytes 10000000 | tf_op jit(solution)/shard_map/pallas_call | solution.py:318
  33.5 2.9 %collective-permute-start.4 = (bf16[16,768]{1,0:T(8,128)(2,1)S(1)}, bf16[16,768]{1,0:T(8,128)(2,1)S(1)}, u32[]{:S(2)}, u32[]{:S(2)}) collective-permute-start(bf16[16,768]{1,0:T(8,128)(2,1)S(1)} %shard_map.200.own_ref), channel_id=1, source_target_pairs={{1,2},{3,4},{5,6},{7,8},{9,10},{11,12},{13,14},{2,1},{4,3},{6,5},{... | collective-permute-start | bytes 73736 | tf_op jit(solution)/shard_map/ppermute | solution.py:442
  36.4 0.0 copy-done.4
  36.4 0.6 %shard_map.201 = (bf16[16,128]{1,0:T(8,128)(2,1)S(1)}, f32[256,128]{1,0:T(8,128)S(1)}, bf16[16,768]{1,0:T(8,128)(2,1)}) custom-call(bf16[256,128]{1,0:T(8,128)(2,1)S(1)} %get-tuple-element.18.mid_ref, bf16[16,768]{1,0:T(8,128)(2,1)S(1)} %shard_map.200.own_ref, bf16[256,128]{1,0:T(8,128)(2,1)S(1)} %get-tuple-element.30.pick_ref, bf16[768,128]{1,0:T(8,128)(2,1)S(1)} %copy-done.4), custom_call_target="tpu_custom_call" | custom-call | flops 2000000000 | bytes 10000000 | tf_op jit(solution)/shard_map/pallas_call | solution.py:318
  37.0 0.0 collective-permute-start.3
  37.0 1.2 %collective-permute-done.3.core_ref = bf16[16,128]{1,0:T(8,128)(2,1)S(1)} collective-permute-done((bf16[16,128]{1,0:T(8,128)(2,1)S(1)}, bf16[16,128]{1,0:T(8,128)(2,1)S(1)}, u32[]{:S(2)}, u32[]{:S(2)}) %collective-permute-start.3) | collective-permute-done | bytes 4128 | tf_op jit(solution)/shard_map/ppermute | solution.py:451
  38.2 0.5 %collective-permute-done.4.far_ref = bf16[16,768]{1,0:T(8,128)(2,1)S(1)} collective-permute-done((bf16[16,768]{1,0:T(8,128)(2,1)S(1)}, bf16[16,768]{1,0:T(8,128)(2,1)S(1)}, u32[]{:S(2)}, u32[]{:S(2)}) %collective-permute-start.4) | collective-permute-done | bytes 24608 | tf_op jit(solution)/shard_map/ppermute | solution.py:442
  38.7 0.9 %shard_map.202 = bf16[256,128]{1,0:T(8,128)(2,1)} custom-call(f32[256,128]{1,0:T(8,128)S(1)} %get-tuple-element.31.partial_ref, bf16[16,128]{1,0:T(8,128)(2,1)S(1)} %collective-permute-done.3.core_ref, bf16[16,768]{1,0:T(8,128)(2,1)S(1)} %collective-permute-done.4.far_ref, bf16[256,128]{1,0:T(8,128)(2,1)S(1)} %get-tuple-element.30.pick_ref, ...), custom_call_target="tpu_custom_call" | custom-call | flops 2000000000 | bytes 10000000 | tf_op jit(solution)/shard_map/pallas_call | solution.py:318
  (1 shorter events, 0.0 us)
Async XLA Ops:
  0.6 4.7 %copy-start.16 = (s32[8]{0:T(128)S(1)}, s32[8]{0:T(128)}, u32[]{:S(2)}) copy-start(s32[8]{0:T(128)} %param.20) | copy-start | bytes 100
  0.6 4.7 %copy-start.12 = (s32[16]{0:T(128)S(1)}, s32[16]{0:T(128)}, u32[]{:S(2)}) copy-start(s32[16]{0:T(128)} %param.21) | copy-start | bytes 196
  0.7 4.7 %copy-start.13 = (s32[16]{0:T(128)S(1)}, s32[16]{0:T(128)}, u32[]{:S(2)}) copy-start(s32[16]{0:T(128)} %param.23) | copy-start | bytes 196
  0.7 4.7 %copy-start.14 = (s32[16]{0:T(128)S(1)}, s32[16]{0:T(128)}, u32[]{:S(2)}) copy-start(s32[16]{0:T(128)} %param.22) | copy-start | bytes 196
  0.7 12.6 %collective-permute-start = (bf16[256,128]{1,0:T(8,128)(2,1)}, bf16[256,128]{1,0:T(8,128)(2,1)S(1)}, u32[]{:S(2)}, u32[]{:S(2)}) collective-permute-start(bf16[256,128]{1,0:T(8,128)(2,1)} %feat_ref.1), channel_id=1, source_target_pairs={{0,1},{1,0},{2,3},{3,2},{4,5},{5,4},{6,7},{7,6},{8,9},{9,8},{10,11... | collective-permute-start | bytes 196616 | tf_op jit(solution)/shard_map/ppermute | solution.py:362
  0.8 12.5 %collective-permute-start.1 = (bf16[256,128]{1,0:T(8,128)(2,1)}, bf16[256,128]{1,0:T(8,128)(2,1)S(1)}, u32[]{:S(2)}, u32[]{:S(2)}) collective-permute-start(bf16[256,128]{1,0:T(8,128)(2,1)} %feat_ref.1), channel_id=1, source_target_pairs={{1,2},{3,4},{5,6},{7,8},{9,10},{11,12},{13,14},{2,1},{4,3},{6,5},{... | collective-permute-start | bytes 196616 | tf_op jit(solution)/shard_map/ppermute | solution.py:361
  5.3 6.1 %copy-start.2 = (bf16[16,256,128]{2,1,0:T(8,128)(2,1)S(1)}, bf16[16,256,128]{2,1,0:T(8,128)(2,1)}, u32[]{:S(2)}) copy-start(bf16[16,256,128]{2,1,0:T(8,128)(2,1)} %pair_ref.1) | copy-start | bytes 3145732
  5.4 6.1 %copy-start.10 = (bf16[128,16]{0,1:T(8,128)(2,1)S(1)}, bf16[128,16]{0,1:T(8,128)(2,1)}, u32[]{:S(2)}) copy-start(bf16[128,16]{0,1:T(8,128)(2,1)} %param.35) | copy-start | bytes 12292
  5.4 6.1 %copy-start.15 = (f32[128]{0:T(128)S(1)}, f32[128]{0:T(128)}, u32[]{:S(2)}) copy-start(f32[128]{0:T(128)} %gain_ref.3) | copy-start | bytes 1540
  6.1 11.0 %all-to-all-start = ((s32[16,1,128]{2,1,0:T(1,128)}), s32[16,1,128]{2,1,0:T(1,128)S(1)}, u32[]{:S(2)}, u32[]{:S(2)}) async-start(s32[16,1,128]{2,1,0:T(1,128)} %shard_map.197), calls=%async_computation | async-start | bytes 16384 | tf_op jit(solution)/shard_map/all_to_all | solution.py:372
  11.4 1.9 %copy-start.3 = (bf16[128,768]{1,0:T(8,128)(2,1)S(1)}, bf16[128,768]{1,0:T(8,128)(2,1)}, u32[]{:S(2)}) copy-start(bf16[128,768]{1,0:T(8,128)(2,1)} %pool_ref.3) | copy-start | bytes 589828
  11.4 1.9 %copy-start.5 = (bf16[128,384]{1,0:T(8,128)(2,1)S(1)}, bf16[128,384]{1,0:T(8,128)(2,1)}, u32[]{:S(2)}) copy-start(bf16[128,384]{1,0:T(8,128)(2,1)} %qkv_ref.1) | copy-start | bytes 294916
  11.5 1.9 %copy-start.6 = (bf16[256,128]{1,0:T(8,128)(2,1)S(1)}, bf16[256,128]{1,0:T(8,128)(2,1)}, u32[]{:S(2)}) copy-start(bf16[256,128]{1,0:T(8,128)(2,1)} %feat_ref.1) | copy-start | bytes 196612
  11.5 1.9 %copy-start.8 = (bf16[128,128]{1,0:T(8,128)(2,1)S(1)}, bf16[128,128]{1,0:T(8,128)(2,1)}, u32[]{:S(2)}) copy-start(bf16[128,128]{1,0:T(8,128)(2,1)} %out_ref.4) | copy-start | bytes 98308
  11.5 1.9 %copy-start.17 = (f32[128]{0:T(128)S(1)}, f32[128]{0:T(128)}, u32[]{:S(2)}) copy-start(f32[128]{0:T(128)} %gain_ref.4) | copy-start | bytes 1540
  13.3 3.8 %copy-start.7 = (bf16[32,768]{1,0:T(8,128)(2,1)S(1)}, bf16[32,768]{1,0:T(8,128)(2,1)}, u32[]{:S(2)}) copy-start(bf16[32,768]{1,0:T(8,128)(2,1)} %restype_ref.1) | copy-start | bytes 147460
  13.3 3.8 %copy-start.9 = (bf16[16,768]{1,0:T(8,128)(2,1)S(1)}, bf16[16,768]{1,0:T(8,128)(2,1)}, u32[]{:S(2)}) copy-start(bf16[16,768]{1,0:T(8,128)(2,1)} %single_ref.1) | copy-start | bytes 73732
  13.3 3.8 %copy-start.11 = (f32[768]{0:T(1024)S(1)}, f32[768]{0:T(1024)}, u32[]{:S(2)}) copy-start(f32[768]{0:T(1024)} %gain_ref.5) | copy-start | bytes 9220
  17.1 5.4 %copy-start.18 = (f32[16]{0:T(128)S(1)}, f32[16]{0:T(128)}, u32[]{:S(2)}) copy-start(f32[16]{0:T(128)} %chain_weight_ref.1) | copy-start | bytes 196
  18.9 10.5 %all-to-all-start.1 = ((bf16[8,16,768]{2,1,0:T(8,128)(2,1)}), bf16[8,16,768]{2,1,0:T(8,128)(2,1)S(1)}, u32[]{:S(2)}, u32[]{:S(2)}) async-start(bf16[8,16,768]{2,1,0:T(8,128)(2,1)} %get-tuple-element.22.normed_ref), calls=%async_computation.1 | async-start | bytes 393216 | tf_op jit(solution)/shard_map/all_to_all | solution.py:410
  22.5 2.3 %copy-start = (bf16[768,3072]{1,0:T(8,128)(2,1)S(1)}, bf16[768,3072]{1,0:T(8,128)(2,1)}, u32[]{:S(2)}) copy-start(bf16[768,3072]{1,0:T(8,128)(2,1)} %proj_ref.1) | copy-start | bytes 14155780
  24.8 7.6 %copy-start.1 = (bf16[768,768]{1,0:T(8,128)(2,1)S(1)}, bf16[768,768]{1,0:T(8,128)(2,1)}, u32[]{:S(2)}) copy-start(bf16[768,768]{1,0:T(8,128)(2,1)} %out_ref.5) | copy-start | bytes 3538948
  29.4 3.1 %collective-permute-start.2 = (bf16[8,16,768]{2,1,0:T(8,128)(2,1)S(1)}, bf16[8,16,768]{2,1,0:T(8,128)(2,1)S(1)}, u32[]{:S(2)}, u32[]{:S(2)}) collective-permute-start(bf16[8,16,768]{2,1,0:T(8,128)(2,1)S(1)} %all-to-all-done.1.mine_ref), channel_id=1, source_target_pairs={{0,1},{1,0},{2,3},{3,2},{4,5},{5,4},{6,7},{7,6},{8,9},{9,8},{10,11... | collective-permute-start | bytes 589832 | tf_op jit(solution)/shard_map/ppermute | solution.py:429
  32.5 3.9 %copy-start.4 = (bf16[768,128]{1,0:T(8,128)(2,1)S(1)}, bf16[768,128]{1,0:T(8,128)(2,1)}, u32[]{:S(2)}) copy-start(bf16[768,128]{1,0:T(8,128)(2,1)} %weight_ref.3) | copy-start | bytes 589828
  33.5 5.1 %collective-permute-start.4 = (bf16[16,768]{1,0:T(8,128)(2,1)S(1)}, bf16[16,768]{1,0:T(8,128)(2,1)S(1)}, u32[]{:S(2)}, u32[]{:S(2)}) collective-permute-start(bf16[16,768]{1,0:T(8,128)(2,1)S(1)} %shard_map.200.own_ref), channel_id=1, source_target_pairs={{1,2},{3,4},{5,6},{7,8},{9,10},{11,12},{13,14},{2,1},{4,3},{6,5},{... | collective-permute-start | bytes 73736 | tf_op jit(solution)/shard_map/ppermute | solution.py:442
  37.0 1.2 %collective-permute-start.3 = (bf16[16,128]{1,0:T(8,128)(2,1)S(1)}, bf16[16,128]{1,0:T(8,128)(2,1)S(1)}, u32[]{:S(2)}, u32[]{:S(2)}) collective-permute-start(bf16[16,128]{1,0:T(8,128)(2,1)S(1)} %get-tuple-element.32), channel_id=1, source_target_pairs={{0,1},{1,0},{2,3},{3,2},{4,5},{5,4},{6,7},{7,6},{8,9},{9,8},{10,11... | collective-permute-start | bytes 12296 | tf_op jit(solution)/shard_map/ppermute | solution.py:451

commit v6 on v5

--- a/solution.py
+++ b/solution.py
@@ -46,8 +46,12 @@
     return lax.broadcasted_iota(jnp.int32, shape, axis)
 
 
-def table_row(table, row):
-    return jnp.sum(jnp.where(iota(table.shape, 0) == row, table, 0), axis=0, keepdims=True)
+def owner(shape):
+    return shape[0] - 1 - iota(shape, 0)
+
+
+def table_row(table, device):
+    return jnp.sum(jnp.where(owner(table.shape) == device, table, 0), axis=0, keepdims=True)
 
 
 def column(row, base, size):
@@ -55,8 +59,8 @@
     return jnp.sum(jnp.where(iota(shape, 1) == iota(shape, 0) + base, row, 0), axis=1, keepdims=True)
 
 
-def atoms_before(table, row, tokens):
-    keep = (iota(table.shape, 0) < row) & (iota(table.shape, 1) < tokens)
+def atoms_before(table, device, tokens):
+    keep = (owner(table.shape) < device) & (iota(table.shape, 1) < tokens)
     return jnp.sum(jnp.sum(jnp.where(keep, table, 0), axis=0, keepdims=True), axis=1, keepdims=True)
 
 
@@ -231,7 +235,7 @@
     each = dot(table.astype(F32).astype(BF16), pick)
     shape = (n, keys)
     chain_keys = jnp.sum(
-        jnp.where(iota(shape, 1) // tokens == iota(shape, 0), each, 0.0), axis=0, keepdims=True
+        jnp.where(iota(shape, 1) // tokens == owner(shape), each, 0.0), axis=0, keepdims=True
     )
     own_row = table_row(table, me)
     shape = (tokens * HEADS, TABLE)
@@ -251,7 +255,7 @@
         here = (token >= 0) & (token < tokens)
         ahead = jnp.where(here & (iota(shape, 0) < token), 1.0, 0.0).astype(BF16)
         equal = jnp.where(here & (iota(shape, 0) == token), 1.0, 0.0).astype(BF16)
-        at = iota(table.shape, 0) == me + step - 1
+        at = owner(table.shape) == me + step - 1
         begin += jnp.sum(jnp.where(at, dot(counts, ahead), 0.0), axis=0, keepdims=True)
         size += jnp.sum(jnp.where(at, dot(counts, equal), 0.0), axis=0, keepdims=True)
         before = atoms_before(table, me + step - 1, tokens).astype(F32)
@@ -272,7 +276,7 @@
     first = jnp.where(even, mine, other)
     second = jnp.where(even, other, mine)
     normed = jnp.concatenate(
-        [part[c] for c in range(chips) for part in (first, second)], axis=0
+        [part[(c - chips // 2) % chips] for c in range(chips) for part in (first, second)], axis=0
     )
     scores = dot_nt(query_ref[...], normed) * (1.0 / math.sqrt(HDIM)) + biased_ref[...]
     weights = jnp.exp(scores - jnp.max(scores, axis=-1, keepdims=True))
@@ -356,7 +360,9 @@
     rows, tokens, extent = atom_feat.shape[0], token_single.shape[0], pair.shape[1]
     cores = [(i, i ^ 1) for i in range(n)]
     far = [(i, i + 1) for i in range(1, n - 1, 2)] + [(i + 1, i) for i in range(1, n - 1, 2)]
-    same_core = [[2 * c + core for c in range(n // 2)] for core in range(2)]
+    chips = n // 2
+    same_core = [[2 * ((c + chips // 2) % chips) + core for c in range(chips)] for core in range(2)]
+    backwards = [list(reversed(range(n)))]
 
     feat_far = lax.ppermute(atom_feat, "row", far)
     feat_core = lax.ppermute(atom_feat, "row", cores)
@@ -369,7 +375,7 @@
         residue_type[None],
         window_start[None],
     )
-    table = lax.all_to_all(table, "row", 0, 0, tiled=True).reshape(n, TABLE)
+    table = lax.all_to_all(table, "row", 0, 0, tiled=True, axis_index_groups=backwards).reshape(n, TABLE)
 
     bias = call(
         pair_kernel, shape_of((tokens * HEADS, extent), F32), pair, pair_gain, pair_bias_weight.T

time: 39.9 us -> 36.9 us (0.925)
  waiting for transfers between devices: 6.78 us -> 2.72 us
  starting transfers between devices: 18.4 us -> 19.4 us
    all_to_all x1, waiting for transfers between devices: 2.31 us -> 0.02 us  [shards(): lax.all_to_all(normed, 'row', 0, 0, tiled=True, axis_index_groups=same_core)]
    all_to_all x1, waiting for transfers between devices: 1.77 us -> 0.01 us  [shards(): lax.all_to_all(table, 'row', 0, 0, tiled=True, axis_index_groups=backwards)]
    all_to_all x1, starting transfers between devices: 5.31 us -> 6.05 us  [shards(): lax.all_to_all(table, 'row', 0, 0, tiled=True, axis_index_groups=backwards)]
  transfers between devices with their start and end apart: 7 -> 7, of which waited for: 5 -> 3; matrix products, arithmetic and copies ran while one was open for 0% -> 0% of each run, Pallas kernels for 19% -> 20%
where the time goes in v6:
time: 36.9 us; the launch traced here: 36.5 us
  starting transfers between devices  19.4 us (53%)
  Pallas kernels  11 us (30%)
  waiting for transfers between devices  2.72 us (7%)
  local copies, waits for them, and re-layouts  2.43 us (7%)
  between operations  0.94 us (3%)
    pallas_call x9, Pallas kernels, call(): pl.pallas_call(kernel, out_shape=outs, in_specs=[spec] * len(args), out_s...  11 us
    all_to_all x1, starting transfers between devices, shards(): lax.all_to_all(table, 'row', 0, 0, tiled=True, axis_index_groups=backwards)  6.05 us
    ppermute x1, starting transfers between devices, shards(): feat_far = lax.ppermute(atom_feat, 'row', far)  4.5 us
    all_to_all x1, starting transfers between devices, shards(): lax.all_to_all(normed, 'row', 0, 0, tiled=True, axis_index_groups=same_core)  3.64 us
    ppermute x1, starting transfers between devices, shards(): tokens_far = lax.ppermute(updated, 'row', far)  2.86 us
    unnamed x38, local copies, waits for them, and re-layouts  2.43 us
    ppermute x1, starting transfers between devices, shards(): other = lax.ppermute(mine, 'row', cores)  2.23 us
    ppermute x1, waiting for transfers between devices, shards(): back_core = lax.ppermute(back, 'row', cores)  1.16 us
  transfers between devices with their start and end apart: 7, of which 3 were waited for; matrix products, arithmetic and copies ran while one was open for 0% of the time, Pallas kernels for 20%

profile of v6, /device:TPU:1, one launch (start us, length us, event | category | flops | bytes accessed | tf_op | source)
XLA Modules:
  0.0 36.5 jit_solution(7607520415890731369)
XLA Ops:
  0.6 0.0 copy-start.16
  0.6 0.0 copy-start.12
  0.7 0.0 copy-start.13
  0.7 0.0 copy-start.14
  0.7 0.1 collective-permute-start
  0.8 4.5 %collective-permute-start.1 = (bf16[256,128]{1,0:T(8,128)(2,1)}, bf16[256,128]{1,0:T(8,128)(2,1)S(1)}, u32[]{:S(2)}, u32[]{:S(2)}) collective-permute-start(bf16[256,128]{1,0:T(8,128)(2,1)} %feat_ref.1), channel_id=1, source_target_pairs={{1,2},{3,4},{5,6},{7,8},{9,10},{11,12},{13,14},{2,1},{4,3},{6,5},{... | collective-permute-start | bytes 196616 | tf_op jit(solution)/shard_map/ppermute | solution.py:367
  5.3 0.0 copy-done.16
  5.3 0.0 copy-done.12
  5.3 0.0 copy-done.13
  5.3 0.0 copy-done.14
  5.3 0.0 copy-start.2
  5.4 0.0 copy-start.10
  5.4 0.0 copy-start.15
  5.4 0.7 %shard_map.197 = s32[16,1,128]{2,1,0:T(1,128)} custom-call(s32[8,128]{1,0:T(8,128)S(1)} %shard_map.196.zero_ref, s32[1,16]{1,0:T(1,128)S(1)} %bitcast.9, s32[1,16]{1,0:T(1,128)S(1)} %bitcast.10, s32[1,16]{1,0:T(1,128)S(1)} %bitcast.11, s32[1,8]{1,0:T(1,128)S(1)} %bitcast.12), custom_call_target="tpu_custom_call" | custom-call | flops 2000000000 | bytes 10000000 | tf_op jit(solution)/shard_map/pallas_call | solution.py:322
  6.1 6.1 %all-to-all-start = ((s32[16,1,128]{2,1,0:T(1,128)}), s32[16,1,128]{2,1,0:T(1,128)S(1)}, u32[]{:S(2)}, u32[]{:S(2)}) async-start(s32[16,1,128]{2,1,0:T(1,128)} %shard_map.197), calls=%async_computation | async-start | bytes 16384 | tf_op jit(solution)/shard_map/all_to_all | solution.py:378
  12.1 0.0 copy-done.2
  12.2 0.0 copy-done.10
  12.2 0.0 copy-done.15
  12.2 0.0 copy-start.3
  12.2 0.0 copy-start.5
  12.2 0.0 copy-start.6
  12.2 0.0 copy-start.8
  12.2 0.0 copy-start.17
  12.2 1.8 %shard_map.194.bias_ref = f32[256,256]{1,0:T(8,128)S(1)} custom-call(bf16[16,256,128]{2,1,0:T(8,128)(2,1)S(1)} %copy-done.2, f32[128]{0:T(128)S(1)} %copy-done.15, bf16[16,128]{1,0:T(8,128)(2,1)S(1)} %bitcast.8), custom_call_target="tpu_custom_call" | custom-call | flops 2000000000 | bytes 10000000 | tf_op jit(solution)/shard_map/pallas_call | solution.py:322
  14.0 0.0 copy-start.7
  14.0 0.0 copy-start.9
  14.0 0.0 copy-start.11
  14.0 0.0 collective-permute-done.core_ref
  14.1 0.0 collective-permute-done.1.far_ref
  14.1 0.0 copy-done.3
  14.1 0.0 copy-done.5
  14.1 0.0 copy-done.6
  14.1 0.0 copy-done.8
  14.1 0.0 copy-done.17
  14.1 2.0 %shard_map.195 = (bf16[512,128]{1,0:T(8,128)(2,1)S(1)}, f32[2,256,256]{2,1,0:T(8,128)S(1)}, bf16[256,128]{1,0:T(8,128)(2,1)S(1)}, bf16[256,768]{1,0:T(8,128)(2,1)S(1)}) custom-call(bf16[256,128]{1,0:T(8,128)(2,1)S(1)} %copy-done.6, bf16[256,128]{1,0:T(8,128)(2,1)S(1)} %collective-permute-done.core_ref, bf16[256,128]{1,0:T(8,128)(2,1)S(1)} %collective-permute-done.1.far_ref, ...), custom_call_target="tpu_custom_call" | custom-call | flops 2000000000 | bytes 10000000 | tf_op jit(solution)/shard_map/pallas_call | solution.py:322
  16.1 0.0 all-to-all-done
  16.1 0.0 copy-done.7
  16.1 0.0 copy-done.9
  16.1 0.0 copy-done.11
  16.1 0.0 copy-start.18
  16.1 1.7 %shard_map.198 = (f32[16,768]{1,0:T(8,128)S(1)}, bf16[8,16,768]{2,1,0:T(8,128)(2,1)}) custom-call(bf16[512,128]{1,0:T(8,128)(2,1)S(1)} %get-tuple-element.19.values_ref, f32[2,256,256]{2,1,0:T(8,128)S(1)} %get-tuple-element.20.scores_ref, bf16[256,768]{1,0:T(8,128)(2,1)S(1)} %get-tuple-element.21.lifted_ref, ...), custom_call_target="tpu_custom_call" | custom-call | flops 2000000000 | bytes 10000000 | tf_op jit(solution)/shard_map/pallas_call | solution.py:322
  17.9 3.6 %all-to-all-start.1 = ((bf16[8,16,768]{2,1,0:T(8,128)(2,1)}), bf16[8,16,768]{2,1,0:T(8,128)(2,1)S(1)}, u32[]{:S(2)}, u32[]{:S(2)}) async-start(bf16[8,16,768]{2,1,0:T(8,128)(2,1)} %get-tuple-element.22.normed_ref), calls=%async_computation.1 | async-start | bytes 393216 | tf_op jit(solution)/shard_map/all_to_all | solution.py:416
  21.5 0.0 copy-done.18
  21.5 0.0 copy-start
  21.5 2.3 %copy-done = bf16[768,3072]{1,0:T(8,128)(2,1)S(1)} copy-done((bf16[768,3072]{1,0:T(8,128)(2,1)S(1)}, bf16[768,3072]{1,0:T(8,128)(2,1)}, u32[]{:S(2)}) %copy-start) | copy-done | bytes 4718616
  23.8 0.0 copy-start.1
  23.9 2.2 %shard_map.199 = (bf16[256,768]{1,0:T(8,128)(2,1)S(1)}, f32[16,768]{1,0:T(8,128)S(1)}, f32[256,256]{1,0:T(8,128)S(1)}, bf16[256,128]{1,0:T(8,128)(2,1)S(1)}, bf16[768,768]{1,0:T(8,128)(2,1)S(1)}) custom-call(bf16[8,16,768]{2,1,0:T(8,128)(2,1)} %get-tuple-element.22.normed_ref, s32[16,128]{1,0:T(8,128)S(1)} %bitcast.7, ...), custom_call_target="tpu_custom_call", output_to_operand_aliasing={{2}: (2, {})} | custom-call | flops 2000000000 | bytes 10000000 | tf_op jit(solution)/shard_map/pallas_call | solution.py:322
  26.1 0.0 all-to-all-done.1.mine_ref
  26.1 2.2 %collective-permute-start.2 = (bf16[8,16,768]{2,1,0:T(8,128)(2,1)S(1)}, bf16[8,16,768]{2,1,0:T(8,128)(2,1)S(1)}, u32[]{:S(2)}, u32[]{:S(2)}) collective-permute-start(bf16[8,16,768]{2,1,0:T(8,128)(2,1)S(1)} %all-to-all-done.1.mine_ref), channel_id=1, source_target_pairs={{0,1},{1,0},{2,3},{3,2},{4,5},{5,4},{6,7},{7,6},{8,9},{9,8},{10,11... | collective-permute-start | bytes 589832 | tf_op jit(solution)/shard_map/ppermute | solution.py:435
  28.3 1.1 %collective-permute-done.2.other_ref = bf16[8,16,768]{2,1,0:T(8,128)(2,1)S(1)} collective-permute-done((bf16[8,16,768]{2,1,0:T(8,128)(2,1)S(1)}, bf16[8,16,768]{2,1,0:T(8,128)(2,1)S(1)}, u32[]{:S(2)}, u32[]{:S(2)}) %collective-permute-start.2) | collective-permute-done | bytes 196640 | tf_op jit(solution)/shard_map/ppermute | solution.py:435
  29.4 0.0 copy-done.1
  29.4 0.0 copy-start.4
  29.4 1.0 %shard_map.200.own_ref = bf16[16,768]{1,0:T(8,128)(2,1)S(1)} custom-call(bf16[8,16,768]{2,1,0:T(8,128)(2,1)S(1)} %all-to-all-done.1.mine_ref, bf16[8,16,768]{2,1,0:T(8,128)(2,1)S(1)} %collective-permute-done.2.other_ref, bf16[256,768]{1,0:T(8,128)(2,1)S(1)} %get-tuple-element.25.query_ref, f32[256,256]{1,0:T(8,128)S(1)} %get-tuple-element.26.biased_ref, ...), custom_call_target="tpu_custom_call" | custom-call | flops 2000000000 | bytes 10000000 | tf_op jit(solution)/shard_map/pallas_call | solution.py:322
  30.4 2.9 %collective-permute-start.4 = (bf16[16,768]{1,0:T(8,128)(2,1)S(1)}, bf16[16,768]{1,0:T(8,128)(2,1)S(1)}, u32[]{:S(2)}, u32[]{:S(2)}) collective-permute-start(bf16[16,768]{1,0:T(8,128)(2,1)S(1)} %shard_map.200.own_ref), channel_id=1, source_target_pairs={{1,2},{3,4},{5,6},{7,8},{9,10},{11,12},{13,14},{2,1},{4,3},{6,5},{... | collective-permute-start | bytes 73736 | tf_op jit(solution)/shard_map/ppermute | solution.py:448
  33.3 0.0 copy-done.4
  33.3 0.6 %shard_map.201 = (bf16[16,128]{1,0:T(8,128)(2,1)S(1)}, f32[256,128]{1,0:T(8,128)S(1)}, bf16[16,768]{1,0:T(8,128)(2,1)}) custom-call(bf16[256,128]{1,0:T(8,128)(2,1)S(1)} %get-tuple-element.18.mid_ref, bf16[16,768]{1,0:T(8,128)(2,1)S(1)} %shard_map.200.own_ref, bf16[256,128]{1,0:T(8,128)(2,1)S(1)} %get-tuple-element.30.pick_ref, bf16[768,128]{1,0:T(8,128)(2,1)S(1)} %copy-done.4), custom_call_target="tpu_custom_call" | custom-call | flops 2000000000 | bytes 10000000 | tf_op jit(solution)/shard_map/pallas_call | solution.py:322
  34.0 0.0 collective-permute-start.3
  34.0 1.2 %collective-permute-done.3.core_ref = bf16[16,128]{1,0:T(8,128)(2,1)S(1)} collective-permute-done((bf16[16,128]{1,0:T(8,128)(2,1)S(1)}, bf16[16,128]{1,0:T(8,128)(2,1)S(1)}, u32[]{:S(2)}, u32[]{:S(2)}) %collective-permute-start.3) | collective-permute-done | bytes 4128 | tf_op jit(solution)/shard_map/ppermute | solution.py:457
  35.1 0.5 %collective-permute-done.4.far_ref = bf16[16,768]{1,0:T(8,128)(2,1)S(1)} collective-permute-done((bf16[16,768]{1,0:T(8,128)(2,1)S(1)}, bf16[16,768]{1,0:T(8,128)(2,1)S(1)}, u32[]{:S(2)}, u32[]{:S(2)}) %collective-permute-start.4) | collective-permute-done | bytes 24608 | tf_op jit(solution)/shard_map/ppermute | solution.py:448
  35.6 0.9 %shard_map.202 = bf16[256,128]{1,0:T(8,128)(2,1)} custom-call(f32[256,128]{1,0:T(8,128)S(1)} %get-tuple-element.31.partial_ref, bf16[16,128]{1,0:T(8,128)(2,1)S(1)} %collective-permute-done.3.core_ref, bf16[16,768]{1,0:T(8,128)(2,1)S(1)} %collective-permute-done.4.far_ref, bf16[256,128]{1,0:T(8,128)(2,1)S(1)} %get-tuple-element.30.pick_ref, ...), custom_call_target="tpu_custom_call" | custom-call | flops 2000000000 | bytes 10000000 | tf_op jit(solution)/shard_map/pallas_call | solution.py:322
  (1 shorter events, 0.0 us)
Async XLA Ops:
  0.6 4.7 %copy-start.16 = (s32[8]{0:T(128)S(1)}, s32[8]{0:T(128)}, u32[]{:S(2)}) copy-start(s32[8]{0:T(128)} %param.20) | copy-start | bytes 100
  0.6 4.7 %copy-start.12 = (s32[16]{0:T(128)S(1)}, s32[16]{0:T(128)}, u32[]{:S(2)}) copy-start(s32[16]{0:T(128)} %param.21) | copy-start | bytes 196
  0.7 4.7 %copy-start.13 = (s32[16]{0:T(128)S(1)}, s32[16]{0:T(128)}, u32[]{:S(2)}) copy-start(s32[16]{0:T(128)} %param.23) | copy-start | bytes 196
  0.7 4.7 %copy-start.14 = (s32[16]{0:T(128)S(1)}, s32[16]{0:T(128)}, u32[]{:S(2)}) copy-start(s32[16]{0:T(128)} %param.22) | copy-start | bytes 196
  0.7 13.4 %collective-permute-start = (bf16[256,128]{1,0:T(8,128)(2,1)}, bf16[256,128]{1,0:T(8,128)(2,1)S(1)}, u32[]{:S(2)}, u32[]{:S(2)}) collective-permute-start(bf16[256,128]{1,0:T(8,128)(2,1)} %feat_ref.1), channel_id=1, source_target_pairs={{0,1},{1,0},{2,3},{3,2},{4,5},{5,4},{6,7},{7,6},{8,9},{9,8},{10,11... | collective-permute-start | bytes 196616 | tf_op jit(solution)/shard_map/ppermute | solution.py:368
  0.8 13.3 %collective-permute-start.1 = (bf16[256,128]{1,0:T(8,128)(2,1)}, bf16[256,128]{1,0:T(8,128)(2,1)S(1)}, u32[]{:S(2)}, u32[]{:S(2)}) collective-permute-start(bf16[256,128]{1,0:T(8,128)(2,1)} %feat_ref.1), channel_id=1, source_target_pairs={{1,2},{3,4},{5,6},{7,8},{9,10},{11,12},{13,14},{2,1},{4,3},{6,5},{... | collective-permute-start | bytes 196616 | tf_op jit(solution)/shard_map/ppermute | solution.py:367
  5.3 6.8 %copy-start.2 = (bf16[16,256,128]{2,1,0:T(8,128)(2,1)S(1)}, bf16[16,256,128]{2,1,0:T(8,128)(2,1)}, u32[]{:S(2)}) copy-start(bf16[16,256,128]{2,1,0:T(8,128)(2,1)} %pair_ref.1) | copy-start | bytes 3145732
  5.4 6.8 %copy-start.10 = (bf16[128,16]{0,1:T(8,128)(2,1)S(1)}, bf16[128,16]{0,1:T(8,128)(2,1)}, u32[]{:S(2)}) copy-start(bf16[128,16]{0,1:T(8,128)(2,1)} %param.35) | copy-start | bytes 12292
  5.4 6.8 %copy-start.15 = (f32[128]{0:T(128)S(1)}, f32[128]{0:T(128)}, u32[]{:S(2)}) copy-start(f32[128]{0:T(128)} %gain_ref.3) | copy-start | bytes 1540
  6.1 10.0 %all-to-all-start = ((s32[16,1,128]{2,1,0:T(1,128)}), s32[16,1,128]{2,1,0:T(1,128)S(1)}, u32[]{:S(2)}, u32[]{:S(2)}) async-start(s32[16,1,128]{2,1,0:T(1,128)} %shard_map.197), calls=%async_computation | async-start | bytes 16384 | tf_op jit(solution)/shard_map/all_to_all | solution.py:378
  12.2 1.9 %copy-start.3 = (bf16[128,768]{1,0:T(8,128)(2,1)S(1)}, bf16[128,768]{1,0:T(8,128)(2,1)}, u32[]{:S(2)}) copy-start(bf16[128,768]{1,0:T(8,128)(2,1)} %pool_ref.3) | copy-start | bytes 589828
  12.2 1.9 %copy-start.5 = (bf16[128,384]{1,0:T(8,128)(2,1)S(1)}, bf16[128,384]{1,0:T(8,128)(2,1)}, u32[]{:S(2)}) copy-start(bf16[128,384]{1,0:T(8,128)(2,1)} %qkv_ref.1) | copy-start | bytes 294916
  12.2 1.9 %copy-start.6 = (bf16[256,128]{1,0:T(8,128)(2,1)S(1)}, bf16[256,128]{1,0:T(8,128)(2,1)}, u32[]{:S(2)}) copy-start(bf16[256,128]{1,0:T(8,128)(2,1)} %feat_ref.1) | copy-start | bytes 196612
  12.2 1.9 %copy-start.8 = (bf16[128,128]{1,0:T(8,128)(2,1)S(1)}, bf16[128,128]{1,0:T(8,128)(2,1)}, u32[]{:S(2)}) copy-start(bf16[128,128]{1,0:T(8,128)(2,1)} %out_ref.4) | copy-start | bytes 98308
  12.2 1.9 %copy-start.17 = (f32[128]{0:T(128)S(1)}, f32[128]{0:T(128)}, u32[]{:S(2)}) copy-start(f32[128]{0:T(128)} %gain_ref.4) | copy-start | bytes 1540
  14.0 2.1 %copy-start.7 = (bf16[32,768]{1,0:T(8,128)(2,1)S(1)}, bf16[32,768]{1,0:T(8,128)(2,1)}, u32[]{:S(2)}) copy-start(bf16[32,768]{1,0:T(8,128)(2,1)} %restype_ref.1) | copy-start | bytes 147460
  14.0 2.1 %copy-start.9 = (bf16[16,768]{1,0:T(8,128)(2,1)S(1)}, bf16[16,768]{1,0:T(8,128)(2,1)}, u32[]{:S(2)}) copy-start(bf16[16,768]{1,0:T(8,128)(2,1)} %single_ref.1) | copy-start | bytes 73732
  14.0 2.1 %copy-start.11 = (f32[768]{0:T(1024)S(1)}, f32[768]{0:T(1024)}, u32[]{:S(2)}) copy-start(f32[768]{0:T(1024)} %gain_ref.5) | copy-start | bytes 9220
  16.1 5.4 %copy-start.18 = (f32[16]{0:T(128)S(1)}, f32[16]{0:T(128)}, u32[]{:S(2)}) copy-start(f32[16]{0:T(128)} %chain_weight_ref.1) | copy-start | bytes 196
  17.9 8.2 %all-to-all-start.1 = ((bf16[8,16,768]{2,1,0:T(8,128)(2,1)}), bf16[8,16,768]{2,1,0:T(8,128)(2,1)S(1)}, u32[]{:S(2)}, u32[]{:S(2)}) async-start(bf16[8,16,768]{2,1,0:T(8,128)(2,1)} %get-tuple-element.22.normed_ref), calls=%async_computation.1 | async-start | bytes 393216 | tf_op jit(solution)/shard_map/all_to_all | solution.py:416
  21.5 2.3 %copy-start = (bf16[768,3072]{1,0:T(8,128)(2,1)S(1)}, bf16[768,3072]{1,0:T(8,128)(2,1)}, u32[]{:S(2)}) copy-start(bf16[768,3072]{1,0:T(8,128)(2,1)} %proj_ref.1) | copy-start | bytes 14155780
  23.8 5.6 %copy-start.1 = (bf16[768,768]{1,0:T(8,128)(2,1)S(1)}, bf16[768,768]{1,0:T(8,128)(2,1)}, u32[]{:S(2)}) copy-start(bf16[768,768]{1,0:T(8,128)(2,1)} %out_ref.5) | copy-start | bytes 3538948
  26.1 3.3 %collective-permute-start.2 = (bf16[8,16,768]{2,1,0:T(8,128)(2,1)S(1)}, bf16[8,16,768]{2,1,0:T(8,128)(2,1)S(1)}, u32[]{:S(2)}, u32[]{:S(2)}) collective-permute-start(bf16[8,16,768]{2,1,0:T(8,128)(2,1)S(1)} %all-to-all-done.1.mine_ref), channel_id=1, source_target_pairs={{0,1},{1,0},{2,3},{3,2},{4,5},{5,4},{6,7},{7,6},{8,9},{9,8},{10,11... | collective-permute-start | bytes 589832 | tf_op jit(solution)/shard_map/ppermute | solution.py:435
  29.4 3.9 %copy-start.4 = (bf16[768,128]{1,0:T(8,128)(2,1)S(1)}, bf16[768,128]{1,0:T(8,128)(2,1)}, u32[]{:S(2)}) copy-start(bf16[768,128]{1,0:T(8,128)(2,1)} %weight_ref.3) | copy-start | bytes 589828
  30.4 5.1 %collective-permute-start.4 = (bf16[16,768]{1,0:T(8,128)(2,1)S(1)}, bf16[16,768]{1,0:T(8,128)(2,1)S(1)}, u32[]{:S(2)}, u32[]{:S(2)}) collective-permute-start(bf16[16,768]{1,0:T(8,128)(2,1)S(1)} %shard_map.200.own_ref), channel_id=1, source_target_pairs={{1,2},{3,4},{5,6},{7,8},{9,10},{11,12},{13,14},{2,1},{4,3},{6,5},{... | collective-permute-start | bytes 73736 | tf_op jit(solution)/shard_map/ppermute | solution.py:448
  34.0 1.2 %collective-permute-start.3 = (bf16[16,128]{1,0:T(8,128)(2,1)S(1)}, bf16[16,128]{1,0:T(8,128)(2,1)S(1)}, u32[]{:S(2)}, u32[]{:S(2)}) collective-permute-start(bf16[16,128]{1,0:T(8,128)(2,1)S(1)} %get-tuple-element.32), channel_id=1, source_target_pairs={{0,1},{1,0},{2,3},{3,2},{4,5},{5,4},{6,7},{7,6},{8,9},{9,8},{10,11... | collective-permute-start | bytes 12296 | tf_op jit(solution)/shard_map/ppermute | solution.py:457

commit v7 on v6

--- a/solution.py
+++ b/solution.py
@@ -85,8 +85,13 @@
 
 def pair_kernel(pair_ref, gain_ref, weight_ref, bias_ref):
     gain, weight = gain_ref[...], weight_ref[...]
+    width = pair_ref.shape[2]
+    average = jnp.full((width, width), 1.0 / width, BF16)
     for t in range(pair_ref.shape[0]):
-        normed = norm(pair_ref[t].astype(F32), gain).astype(BF16)
+        pair = pair_ref[t]
+        centered = pair.astype(F32) - dot(pair, average)
+        variance = jnp.mean(centered * centered, axis=-1, keepdims=True)
+        normed = (centered * lax.rsqrt(variance + EPS) * gain).astype(BF16)
         bias_ref[t * HEADS : (t + 1) * HEADS, :] = dot_nt(weight, normed)
 
 

time: 36.9 us -> 36.7 us (level)
  Pallas kernels: 11 us -> 10.2 us
  starting transfers between devices: 19.4 us -> 20.1 us
    pallas_call x9, Pallas kernels: 11 us -> 10.2 us  [call(): pl.pallas_call(kernel, out_shape=outs, in_specs=[spec] * len(args), out_s...]
    all_to_all x1, starting transfers between devices: 3.64 us -> 4.3 us  [shards(): lax.all_to_all(normed, 'row', 0, 0, tiled=True, axis_index_groups=same_core)]
  transfers between devices with their start and end apart: 7 -> 7, of which waited for: 3 -> 3; matrix products, arithmetic and copies ran while one was open for 0% -> 0% of each run, Pallas kernels for 20% -> 18%
where the time goes in v7:
time: 36.7 us; the launch traced here: 36.3 us
  starting transfers between devices  20.1 us (55%)
  Pallas kernels  10.2 us (28%)
  waiting for transfers between devices  2.63 us (7%)
  local copies, waits for them, and re-layouts  2.43 us (7%)
  between operations  0.93 us (3%)
    pallas_call x9, Pallas kernels, call(): pl.pallas_call(kernel, out_shape=outs, in_specs=[spec] * len(args), out_s...  10.2 us
    all_to_all x1, starting transfers between devices, shards(): lax.all_to_all(table, 'row', 0, 0, tiled=True, axis_index_groups=backwards)  6.05 us
    ppermute x1, starting transfers between devices, shards(): feat_far = lax.ppermute(atom_feat, 'row', far)  4.5 us
    all_to_all x1, starting transfers between devices, shards(): lax.all_to_all(normed, 'row', 0, 0, tiled=True, axis_index_groups=same_core)  4.3 us
    ppermute x1, starting transfers between devices, shards(): tokens_far = lax.ppermute(updated, 'row', far)  2.98 us
    unnamed x38, local copies, waits for them, and re-layouts  2.43 us
    ppermute x1, starting transfers between devices, shards(): other = lax.ppermute(mine, 'row', cores)  2.19 us
    ppermute x1, waiting for transfers between devices, shards(): back_core = lax.ppermute(back, 'row', cores)  1.16 us
  transfers between devices with their start and end apart: 7, of which 3 were waited for; matrix products, arithmetic and copies ran while one was open for 0% of the time, Pallas kernels for 18%

profile of v7, /device:TPU:1, one launch (start us, length us, event | category | flops | bytes accessed | tf_op | source)
XLA Modules:
  0.0 36.3 jit_solution(12227775837378571733)
XLA Ops:
  0.6 0.0 copy-start.16
  0.6 0.0 copy-start.12
  0.7 0.0 copy-start.13
  0.7 0.0 copy-start.14
  0.7 0.1 collective-permute-start
  0.8 4.5 %collective-permute-start.1 = (bf16[256,128]{1,0:T(8,128)(2,1)}, bf16[256,128]{1,0:T(8,128)(2,1)S(1)}, u32[]{:S(2)}, u32[]{:S(2)}) collective-permute-start(bf16[256,128]{1,0:T(8,128)(2,1)} %feat_ref.1), channel_id=1, source_target_pairs={{1,2},{3,4},{5,6},{7,8},{9,10},{11,12},{13,14},{2,1},{4,3},{6,5},{... | collective-permute-start | bytes 196616 | tf_op jit(solution)/shard_map/ppermute | solution.py:372
  5.3 0.0 copy-done.16
  5.3 0.0 copy-done.12
  5.3 0.0 copy-done.13
  5.3 0.0 copy-done.14
  5.3 0.0 copy-start.2
  5.4 0.0 copy-start.10
  5.4 0.0 copy-start.15
  5.4 0.7 %shard_map.197 = s32[16,1,128]{2,1,0:T(1,128)} custom-call(s32[8,128]{1,0:T(8,128)S(1)} %shard_map.196.zero_ref, s32[1,16]{1,0:T(1,128)S(1)} %bitcast.9, s32[1,16]{1,0:T(1,128)S(1)} %bitcast.10, s32[1,16]{1,0:T(1,128)S(1)} %bitcast.11, s32[1,8]{1,0:T(1,128)S(1)} %bitcast.12), custom_call_target="tpu_custom_call" | custom-call | flops 2000000000 | bytes 10000000 | tf_op jit(solution)/shard_map/pallas_call | solution.py:327
  6.1 6.1 %all-to-all-start = ((s32[16,1,128]{2,1,0:T(1,128)}), s32[16,1,128]{2,1,0:T(1,128)S(1)}, u32[]{:S(2)}, u32[]{:S(2)}) async-start(s32[16,1,128]{2,1,0:T(1,128)} %shard_map.197), calls=%async_computation | async-start | bytes 16384 | tf_op jit(solution)/shard_map/all_to_all | solution.py:383
  12.1 0.0 copy-done.2
  12.2 0.0 copy-done.10
  12.2 0.0 copy-done.15
  12.2 0.0 copy-start.3
  12.2 0.0 copy-start.5
  12.2 0.0 copy-start.6
  12.2 0.0 copy-start.8
  12.2 0.0 copy-start.17
  12.2 0.9 %shard_map.194.bias_ref = f32[256,256]{1,0:T(8,128)S(1)} custom-call(bf16[16,256,128]{2,1,0:T(8,128)(2,1)S(1)} %copy-done.2, f32[128]{0:T(128)S(1)} %copy-done.15, bf16[16,128]{1,0:T(8,128)(2,1)S(1)} %bitcast.8), custom_call_target="tpu_custom_call" | custom-call | flops 2000000000 | bytes 10000000 | tf_op jit(solution)/shard_map/pallas_call | solution.py:327
  13.2 0.0 copy-start.7
  13.2 0.0 copy-start.9
  13.2 0.0 copy-start.11
  13.2 0.0 collective-permute-done.core_ref
  13.2 0.0 collective-permute-done.1.far_ref
  13.2 0.0 copy-done.3
  13.2 0.0 copy-done.5
  13.2 0.0 copy-done.6
  13.2 0.0 copy-done.8
  13.2 0.0 copy-done.17
  13.3 2.0 %shard_map.195 = (bf16[512,128]{1,0:T(8,128)(2,1)S(1)}, f32[2,256,256]{2,1,0:T(8,128)S(1)}, bf16[256,128]{1,0:T(8,128)(2,1)S(1)}, bf16[256,768]{1,0:T(8,128)(2,1)S(1)}) custom-call(bf16[256,128]{1,0:T(8,128)(2,1)S(1)} %copy-done.6, bf16[256,128]{1,0:T(8,128)(2,1)S(1)} %collective-permute-done.core_ref, bf16[256,128]{1,0:T(8,128)(2,1)S(1)} %collective-permute-done.1.far_ref, ...), custom_call_target="tpu_custom_call" | custom-call | flops 2000000000 | bytes 10000000 | tf_op jit(solution)/shard_map/pallas_call | solution.py:327
  15.2 0.0 all-to-all-done
  15.2 0.0 copy-done.7
  15.2 0.0 copy-done.9
  15.3 0.0 copy-done.11
  15.3 0.0 copy-start.18
  15.3 1.7 %shard_map.198 = (f32[16,768]{1,0:T(8,128)S(1)}, bf16[8,16,768]{2,1,0:T(8,128)(2,1)}) custom-call(bf16[512,128]{1,0:T(8,128)(2,1)S(1)} %get-tuple-element.19.values_ref, f32[2,256,256]{2,1,0:T(8,128)S(1)} %get-tuple-element.20.scores_ref, bf16[256,768]{1,0:T(8,128)(2,1)S(1)} %get-tuple-element.21.lifted_ref, ...), custom_call_target="tpu_custom_call" | custom-call | flops 2000000000 | bytes 10000000 | tf_op jit(solution)/shard_map/pallas_call | solution.py:327
  17.0 4.3 %all-to-all-start.1 = ((bf16[8,16,768]{2,1,0:T(8,128)(2,1)}), bf16[8,16,768]{2,1,0:T(8,128)(2,1)S(1)}, u32[]{:S(2)}, u32[]{:S(2)}) async-start(bf16[8,16,768]{2,1,0:T(8,128)(2,1)} %get-tuple-element.22.normed_ref), calls=%async_computation.1 | async-start | bytes 393216 | tf_op jit(solution)/shard_map/all_to_all | solution.py:421
  21.3 0.0 copy-done.18
  21.3 0.0 copy-start
  21.3 2.3 %copy-done = bf16[768,3072]{1,0:T(8,128)(2,1)S(1)} copy-done((bf16[768,3072]{1,0:T(8,128)(2,1)S(1)}, bf16[768,3072]{1,0:T(8,128)(2,1)}, u32[]{:S(2)}) %copy-start) | copy-done | bytes 4718616
  23.7 0.0 copy-start.1
  23.7 2.2 %shard_map.199 = (bf16[256,768]{1,0:T(8,128)(2,1)S(1)}, f32[16,768]{1,0:T(8,128)S(1)}, f32[256,256]{1,0:T(8,128)S(1)}, bf16[256,128]{1,0:T(8,128)(2,1)S(1)}, bf16[768,768]{1,0:T(8,128)(2,1)S(1)}) custom-call(bf16[8,16,768]{2,1,0:T(8,128)(2,1)} %get-tuple-element.22.normed_ref, s32[16,128]{1,0:T(8,128)S(1)} %bitcast.7, ...), custom_call_target="tpu_custom_call", output_to_operand_aliasing={{2}: (2, {})} | custom-call | flops 2000000000 | bytes 10000000 | tf_op jit(solution)/shard_map/pallas_call | solution.py:327
  25.9 0.0 all-to-all-done.1.mine_ref
  25.9 2.2 %collective-permute-start.2 = (bf16[8,16,768]{2,1,0:T(8,128)(2,1)S(1)}, bf16[8,16,768]{2,1,0:T(8,128)(2,1)S(1)}, u32[]{:S(2)}, u32[]{:S(2)}) collective-permute-start(bf16[8,16,768]{2,1,0:T(8,128)(2,1)S(1)} %all-to-all-done.1.mine_ref), channel_id=1, source_target_pairs={{0,1},{1,0},{2,3},{3,2},{4,5},{5,4},{6,7},{7,6},{8,9},{9,8},{10,11... | collective-permute-start | bytes 589832 | tf_op jit(solution)/shard_map/ppermute | solution.py:440
  28.1 1.1 %collective-permute-done.2.other_ref = bf16[8,16,768]{2,1,0:T(8,128)(2,1)S(1)} collective-permute-done((bf16[8,16,768]{2,1,0:T(8,128)(2,1)S(1)}, bf16[8,16,768]{2,1,0:T(8,128)(2,1)S(1)}, u32[]{:S(2)}, u32[]{:S(2)}) %collective-permute-start.2) | collective-permute-done | bytes 196640 | tf_op jit(solution)/shard_map/ppermute | solution.py:440
  29.2 0.0 copy-done.1
  29.2 0.0 copy-start.4
  29.2 1.0 %shard_map.200.own_ref = bf16[16,768]{1,0:T(8,128)(2,1)S(1)} custom-call(bf16[8,16,768]{2,1,0:T(8,128)(2,1)S(1)} %all-to-all-done.1.mine_ref, bf16[8,16,768]{2,1,0:T(8,128)(2,1)S(1)} %collective-permute-done.2.other_ref, bf16[256,768]{1,0:T(8,128)(2,1)S(1)} %get-tuple-element.25.query_ref, f32[256,256]{1,0:T(8,128)S(1)} %get-tuple-element.26.biased_ref, ...), custom_call_target="tpu_custom_call" | custom-call | flops 2000000000 | bytes 10000000 | tf_op jit(solution)/shard_map/pallas_call | solution.py:327
  30.2 3.0 %collective-permute-start.4 = (bf16[16,768]{1,0:T(8,128)(2,1)S(1)}, bf16[16,768]{1,0:T(8,128)(2,1)S(1)}, u32[]{:S(2)}, u32[]{:S(2)}) collective-permute-start(bf16[16,768]{1,0:T(8,128)(2,1)S(1)} %shard_map.200.own_ref), channel_id=1, source_target_pairs={{1,2},{3,4},{5,6},{7,8},{9,10},{11,12},{13,14},{2,1},{4,3},{6,5},{... | collective-permute-start | bytes 73736 | tf_op jit(solution)/shard_map/ppermute | solution.py:453
  33.2 0.0 copy-done.4
  33.2 0.6 %shard_map.201 = (bf16[16,128]{1,0:T(8,128)(2,1)S(1)}, f32[256,128]{1,0:T(8,128)S(1)}, bf16[16,768]{1,0:T(8,128)(2,1)}) custom-call(bf16[256,128]{1,0:T(8,128)(2,1)S(1)} %get-tuple-element.18.mid_ref, bf16[16,768]{1,0:T(8,128)(2,1)S(1)} %shard_map.200.own_ref, bf16[256,128]{1,0:T(8,128)(2,1)S(1)} %get-tuple-element.30.pick_ref, bf16[768,128]{1,0:T(8,128)(2,1)S(1)} %copy-done.4), custom_call_target="tpu_custom_call" | custom-call | flops 2000000000 | bytes 10000000 | tf_op jit(solution)/shard_map/pallas_call | solution.py:327
  33.9 0.0 collective-permute-start.3
  33.9 1.2 %collective-permute-done.3.core_ref = bf16[16,128]{1,0:T(8,128)(2,1)S(1)} collective-permute-done((bf16[16,128]{1,0:T(8,128)(2,1)S(1)}, bf16[16,128]{1,0:T(8,128)(2,1)S(1)}, u32[]{:S(2)}, u32[]{:S(2)}) %collective-permute-start.3) | collective-permute-done | bytes 4128 | tf_op jit(solution)/shard_map/ppermute | solution.py:462
  35.0 0.3 collective-permute-done.4.far_ref
  35.4 0.9 %shard_map.202 = bf16[256,128]{1,0:T(8,128)(2,1)} custom-call(f32[256,128]{1,0:T(8,128)S(1)} %get-tuple-element.31.partial_ref, bf16[16,128]{1,0:T(8,128)(2,1)S(1)} %collective-permute-done.3.core_ref, bf16[16,768]{1,0:T(8,128)(2,1)S(1)} %collective-permute-done.4.far_ref, bf16[256,128]{1,0:T(8,128)(2,1)S(1)} %get-tuple-element.30.pick_ref, ...), custom_call_target="tpu_custom_call" | custom-call | flops 2000000000 | bytes 10000000 | tf_op jit(solution)/shard_map/pallas_call | solution.py:327
  (1 shorter events, 0.0 us)
Async XLA Ops:
  0.6 4.7 %copy-start.16 = (s32[8]{0:T(128)S(1)}, s32[8]{0:T(128)}, u32[]{:S(2)}) copy-start(s32[8]{0:T(128)} %param.20) | copy-start | bytes 100
  0.6 4.7 %copy-start.12 = (s32[16]{0:T(128)S(1)}, s32[16]{0:T(128)}, u32[]{:S(2)}) copy-start(s32[16]{0:T(128)} %param.21) | copy-start | bytes 196
  0.7 4.7 %copy-start.13 = (s32[16]{0:T(128)S(1)}, s32[16]{0:T(128)}, u32[]{:S(2)}) copy-start(s32[16]{0:T(128)} %param.23) | copy-start | bytes 196
  0.7 4.7 %copy-start.14 = (s32[16]{0:T(128)S(1)}, s32[16]{0:T(128)}, u32[]{:S(2)}) copy-start(s32[16]{0:T(128)} %param.22) | copy-start | bytes 196
  0.7 12.5 %collective-permute-start = (bf16[256,128]{1,0:T(8,128)(2,1)}, bf16[256,128]{1,0:T(8,128)(2,1)S(1)}, u32[]{:S(2)}, u32[]{:S(2)}) collective-permute-start(bf16[256,128]{1,0:T(8,128)(2,1)} %feat_ref.1), channel_id=1, source_target_pairs={{0,1},{1,0},{2,3},{3,2},{4,5},{5,4},{6,7},{7,6},{8,9},{9,8},{10,11... | collective-permute-start | bytes 196616 | tf_op jit(solution)/shard_map/ppermute | solution.py:373
  0.8 12.4 %collective-permute-start.1 = (bf16[256,128]{1,0:T(8,128)(2,1)}, bf16[256,128]{1,0:T(8,128)(2,1)S(1)}, u32[]{:S(2)}, u32[]{:S(2)}) collective-permute-start(bf16[256,128]{1,0:T(8,128)(2,1)} %feat_ref.1), channel_id=1, source_target_pairs={{1,2},{3,4},{5,6},{7,8},{9,10},{11,12},{13,14},{2,1},{4,3},{6,5},{... | collective-permute-start | bytes 196616 | tf_op jit(solution)/shard_map/ppermute | solution.py:372
  5.3 6.8 %copy-start.2 = (bf16[16,256,128]{2,1,0:T(8,128)(2,1)S(1)}, bf16[16,256,128]{2,1,0:T(8,128)(2,1)}, u32[]{:S(2)}) copy-start(bf16[16,256,128]{2,1,0:T(8,128)(2,1)} %pair_ref.1) | copy-start | bytes 3145732
  5.4 6.8 %copy-start.10 = (bf16[128,16]{0,1:T(8,128)(2,1)S(1)}, bf16[128,16]{0,1:T(8,128)(2,1)}, u32[]{:S(2)}) copy-start(bf16[128,16]{0,1:T(8,128)(2,1)} %param.35) | copy-start | bytes 12292
  5.4 6.8 %copy-start.15 = (f32[128]{0:T(128)S(1)}, f32[128]{0:T(128)}, u32[]{:S(2)}) copy-start(f32[128]{0:T(128)} %gain_ref.3) | copy-start | bytes 1540
  6.1 9.1 %all-to-all-start = ((s32[16,1,128]{2,1,0:T(1,128)}), s32[16,1,128]{2,1,0:T(1,128)S(1)}, u32[]{:S(2)}, u32[]{:S(2)}) async-start(s32[16,1,128]{2,1,0:T(1,128)} %shard_map.197), calls=%async_computation | async-start | bytes 16384 | tf_op jit(solution)/shard_map/all_to_all | solution.py:383
  12.2 1.0 %copy-start.3 = (bf16[128,768]{1,0:T(8,128)(2,1)S(1)}, bf16[128,768]{1,0:T(8,128)(2,1)}, u32[]{:S(2)}) copy-start(bf16[128,768]{1,0:T(8,128)(2,1)} %pool_ref.3) | copy-start | bytes 589828
  12.2 1.0 %copy-start.5 = (bf16[128,384]{1,0:T(8,128)(2,1)S(1)}, bf16[128,384]{1,0:T(8,128)(2,1)}, u32[]{:S(2)}) copy-start(bf16[128,384]{1,0:T(8,128)(2,1)} %qkv_ref.1) | copy-start | bytes 294916
  12.2 1.0 %copy-start.6 = (bf16[256,128]{1,0:T(8,128)(2,1)S(1)}, bf16[256,128]{1,0:T(8,128)(2,1)}, u32[]{:S(2)}) copy-start(bf16[256,128]{1,0:T(8,128)(2,1)} %feat_ref.1) | copy-start | bytes 196612
  12.2 1.0 %copy-start.8 = (bf16[128,128]{1,0:T(8,128)(2,1)S(1)}, bf16[128,128]{1,0:T(8,128)(2,1)}, u32[]{:S(2)}) copy-start(bf16[128,128]{1,0:T(8,128)(2,1)} %out_ref.4) | copy-start | bytes 98308
  12.2 1.0 %copy-start.17 = (f32[128]{0:T(128)S(1)}, f32[128]{0:T(128)}, u32[]{:S(2)}) copy-start(f32[128]{0:T(128)} %gain_ref.4) | copy-start | bytes 1540
  13.2 2.1 %copy-start.7 = (bf16[32,768]{1,0:T(8,128)(2,1)S(1)}, bf16[32,768]{1,0:T(8,128)(2,1)}, u32[]{:S(2)}) copy-start(bf16[32,768]{1,0:T(8,128)(2,1)} %restype_ref.1) | copy-start | bytes 147460
  13.2 2.1 %copy-start.9 = (bf16[16,768]{1,0:T(8,128)(2,1)S(1)}, bf16[16,768]{1,0:T(8,128)(2,1)}, u32[]{:S(2)}) copy-start(bf16[16,768]{1,0:T(8,128)(2,1)} %single_ref.1) | copy-start | bytes 73732
  13.2 2.1 %copy-start.11 = (f32[768]{0:T(1024)S(1)}, f32[768]{0:T(1024)}, u32[]{:S(2)}) copy-start(f32[768]{0:T(1024)} %gain_ref.5) | copy-start | bytes 9220
  15.3 6.0 %copy-start.18 = (f32[16]{0:T(128)S(1)}, f32[16]{0:T(128)}, u32[]{:S(2)}) copy-start(f32[16]{0:T(128)} %chain_weight_ref.1) | copy-start | bytes 196
  17.0 8.9 %all-to-all-start.1 = ((bf16[8,16,768]{2,1,0:T(8,128)(2,1)}), bf16[8,16,768]{2,1,0:T(8,128)(2,1)S(1)}, u32[]{:S(2)}, u32[]{:S(2)}) async-start(bf16[8,16,768]{2,1,0:T(8,128)(2,1)} %get-tuple-element.22.normed_ref), calls=%async_computation.1 | async-start | bytes 393216 | tf_op jit(solution)/shard_map/all_to_all | solution.py:421
  21.3 2.3 %copy-start = (bf16[768,3072]{1,0:T(8,128)(2,1)S(1)}, bf16[768,3072]{1,0:T(8,128)(2,1)}, u32[]{:S(2)}) copy-start(bf16[768,3072]{1,0:T(8,128)(2,1)} %proj_ref.1) | copy-start | bytes 14155780
  23.7 5.6 %copy-start.1 = (bf16[768,768]{1,0:T(8,128)(2,1)S(1)}, bf16[768,768]{1,0:T(8,128)(2,1)}, u32[]{:S(2)}) copy-start(bf16[768,768]{1,0:T(8,128)(2,1)} %out_ref.5) | copy-start | bytes 3538948
  25.9 3.3 %collective-permute-start.2 = (bf16[8,16,768]{2,1,0:T(8,128)(2,1)S(1)}, bf16[8,16,768]{2,1,0:T(8,128)(2,1)S(1)}, u32[]{:S(2)}, u32[]{:S(2)}) collective-permute-start(bf16[8,16,768]{2,1,0:T(8,128)(2,1)S(1)} %all-to-all-done.1.mine_ref), channel_id=1, source_target_pairs={{0,1},{1,0},{2,3},{3,2},{4,5},{5,4},{6,7},{7,6},{8,9},{9,8},{10,11... | collective-permute-start | bytes 589832 | tf_op jit(solution)/shard_map/ppermute | solution.py:440
  29.2 4.0 %copy-start.4 = (bf16[768,128]{1,0:T(8,128)(2,1)S(1)}, bf16[768,128]{1,0:T(8,128)(2,1)}, u32[]{:S(2)}) copy-start(bf16[768,128]{1,0:T(8,128)(2,1)} %weight_ref.3) | copy-start | bytes 589828
  30.2 5.1 %collective-permute-start.4 = (bf16[16,768]{1,0:T(8,128)(2,1)S(1)}, bf16[16,768]{1,0:T(8,128)(2,1)S(1)}, u32[]{:S(2)}, u32[]{:S(2)}) collective-permute-start(bf16[16,768]{1,0:T(8,128)(2,1)S(1)} %shard_map.200.own_ref), channel_id=1, source_target_pairs={{1,2},{3,4},{5,6},{7,8},{9,10},{11,12},{13,14},{2,1},{4,3},{6,5},{... | collective-permute-start | bytes 73736 | tf_op jit(solution)/shard_map/ppermute | solution.py:453
  33.9 1.2 %collective-permute-start.3 = (bf16[16,128]{1,0:T(8,128)(2,1)S(1)}, bf16[16,128]{1,0:T(8,128)(2,1)S(1)}, u32[]{:S(2)}, u32[]{:S(2)}) collective-permute-start(bf16[16,128]{1,0:T(8,128)(2,1)S(1)} %get-tuple-element.32), channel_id=1, source_target_pairs={{0,1},{1,0},{2,3},{3,2},{4,5},{5,4},{6,7},{7,6},{8,9},{9,8},{10,11... | collective-permute-start | bytes 12296 | tf_op jit(solution)/shard_map/ppermute | solution.py:462

commit v8 on v7

--- a/solution.py
+++ b/solution.py
@@ -139,8 +139,12 @@
     me = lax.axis_index("row")
     rows = feat_ref.shape[0]
     left, right = edges(core_ref[...], far_ref[...], rows)
-    feat = jnp.concatenate([left, feat_ref[...], right], axis=0).astype(F32)
-    proj = dot(norm(feat, gain_ref[...]).astype(BF16), qkv_ref[...]).astype(BF16)
+    feat = jnp.concatenate([left, feat_ref[...], right], axis=0)
+    centered = feat.astype(F32) - dot(feat, jnp.full((CA, CA), 1.0 / CA, BF16))
+    variance = jnp.mean(centered * centered, axis=-1, keepdims=True)
+    normed = (centered * lax.rsqrt(variance + EPS) * gain_ref[...]).astype(BF16)
+    feat = feat.astype(F32)
+    proj = dot(normed, qkv_ref[...]).astype(BF16)
     values_ref[...] = proj[:, 2 * CA :]
     for i, (at, base) in enumerate(((HALF - REACH, 0), (HALF + rows, rows))):
         part = window_scores(

time: 36.7 us -> 36.7 us (level)
  no operation moved by 1% of the time
where the time goes in v8:
time: 36.7 us; the launch traced here: 36.3 us
  starting transfers between devices  20.2 us (55%)
  Pallas kernels  10.1 us (28%)
  waiting for transfers between devices  2.63 us (7%)
  local copies, waits for them, and re-layouts  2.43 us (7%)
  between operations  0.93 us (3%)
    pallas_call x9, Pallas kernels, call(): pl.pallas_call(kernel, out_shape=outs, in_specs=[spec] * len(args), out_s...  10.1 us
    all_to_all x1, starting transfers between devices, shards(): lax.all_to_all(table, 'row', 0, 0, tiled=True, axis_index_groups=backwards)  6.05 us
    ppermute x1, starting transfers between devices, shards(): feat_far = lax.ppermute(atom_feat, 'row', far)  4.5 us
    all_to_all x1, starting transfers between devices, shards(): lax.all_to_all(normed, 'row', 0, 0, tiled=True, axis_index_groups=same_core)  4.4 us
    ppermute x1, starting transfers between devices, shards(): tokens_far = lax.ppermute(updated, 'row', far)  2.98 us
    unnamed x38, local copies, waits for them, and re-layouts  2.43 us
    ppermute x1, starting transfers between devices, shards(): other = lax.ppermute(mine, 'row', cores)  2.19 us
    ppermute x1, waiting for transfers between devices, shards(): back_core = lax.ppermute(back, 'row', cores)  1.16 us
  transfers between devices with their start and end apart: 7, of which 3 were waited for; matrix products, arithmetic and copies ran while one was open for 0% of the time, Pallas kernels for 18%

profile of v8, /device:TPU:1, one launch (start us, length us, event | category | flops | bytes accessed | tf_op | source)
XLA Modules:
  0.0 36.3 jit_solution(8614447118969348481)
XLA Ops:
  0.6 0.0 copy-start.16
  0.6 0.0 copy-start.12
  0.7 0.0 copy-start.13
  0.7 0.0 copy-start.14
  0.7 0.1 collective-permute-start
  0.8 4.5 %collective-permute-start.1 = (bf16[256,128]{1,0:T(8,128)(2,1)}, bf16[256,128]{1,0:T(8,128)(2,1)S(1)}, u32[]{:S(2)}, u32[]{:S(2)}) collective-permute-start(bf16[256,128]{1,0:T(8,128)(2,1)} %feat_ref.1), channel_id=1, source_target_pairs={{1,2},{3,4},{5,6},{7,8},{9,10},{11,12},{13,14},{2,1},{4,3},{6,5},{... | collective-permute-start | bytes 196616 | tf_op jit(solution)/shard_map/ppermute | solution.py:376
  5.3 0.0 copy-done.16
  5.3 0.0 copy-done.12
  5.3 0.0 copy-done.13
  5.3 0.0 copy-done.14
  5.3 0.0 copy-start.2
  5.4 0.0 copy-start.10
  5.4 0.0 copy-start.15
  5.4 0.7 %shard_map.197 = s32[16,1,128]{2,1,0:T(1,128)} custom-call(s32[8,128]{1,0:T(8,128)S(1)} %shard_map.196.zero_ref, s32[1,16]{1,0:T(1,128)S(1)} %bitcast.9, s32[1,16]{1,0:T(1,128)S(1)} %bitcast.10, s32[1,16]{1,0:T(1,128)S(1)} %bitcast.11, s32[1,8]{1,0:T(1,128)S(1)} %bitcast.12), custom_call_target="tpu_custom_call" | custom-call | flops 2000000000 | bytes 10000000 | tf_op jit(solution)/shard_map/pallas_call | solution.py:331
  6.1 6.1 %all-to-all-start = ((s32[16,1,128]{2,1,0:T(1,128)}), s32[16,1,128]{2,1,0:T(1,128)S(1)}, u32[]{:S(2)}, u32[]{:S(2)}) async-start(s32[16,1,128]{2,1,0:T(1,128)} %shard_map.197), calls=%async_computation | async-start | bytes 16384 | tf_op jit(solution)/shard_map/all_to_all | solution.py:387
  12.1 0.0 copy-done.2
  12.2 0.0 copy-done.10
  12.2 0.0 copy-done.15
  12.2 0.0 copy-start.3
  12.2 0.0 copy-start.5
  12.2 0.0 copy-start.6
  12.2 0.0 copy-start.8
  12.2 0.0 copy-start.17
  12.2 0.9 %shard_map.194.bias_ref = f32[256,256]{1,0:T(8,128)S(1)} custom-call(bf16[16,256,128]{2,1,0:T(8,128)(2,1)S(1)} %copy-done.2, f32[128]{0:T(128)S(1)} %copy-done.15, bf16[16,128]{1,0:T(8,128)(2,1)S(1)} %bitcast.8), custom_call_target="tpu_custom_call" | custom-call | flops 2000000000 | bytes 10000000 | tf_op jit(solution)/shard_map/pallas_call | solution.py:331
  13.2 0.0 copy-start.7
  13.2 0.0 copy-start.9
  13.2 0.0 copy-start.11
  13.2 0.0 collective-permute-done.core_ref
  13.2 0.0 collective-permute-done.1.far_ref
  13.2 0.0 copy-done.3
  13.2 0.0 copy-done.5
  13.2 0.0 copy-done.6
  13.2 0.0 copy-done.8
  13.2 0.0 copy-done.17
  13.3 1.9 %shard_map.195 = (bf16[512,128]{1,0:T(8,128)(2,1)S(1)}, f32[2,256,256]{2,1,0:T(8,128)S(1)}, bf16[256,128]{1,0:T(8,128)(2,1)S(1)}, bf16[256,768]{1,0:T(8,128)(2,1)S(1)}) custom-call(bf16[256,128]{1,0:T(8,128)(2,1)S(1)} %copy-done.6, bf16[256,128]{1,0:T(8,128)(2,1)S(1)} %collective-permute-done.core_ref, bf16[256,128]{1,0:T(8,128)(2,1)S(1)} %collective-permute-done.1.far_ref, ...), custom_call_target="tpu_custom_call" | custom-call | flops 2000000000 | bytes 10000000 | tf_op jit(solution)/shard_map/pallas_call | solution.py:331
  15.1 0.0 all-to-all-done
  15.1 0.0 copy-done.7
  15.1 0.0 copy-done.9
  15.2 0.0 copy-done.11
  15.2 0.0 copy-start.18
  15.2 1.7 %shard_map.198 = (f32[16,768]{1,0:T(8,128)S(1)}, bf16[8,16,768]{2,1,0:T(8,128)(2,1)}) custom-call(bf16[512,128]{1,0:T(8,128)(2,1)S(1)} %get-tuple-element.19.values_ref, f32[2,256,256]{2,1,0:T(8,128)S(1)} %get-tuple-element.20.scores_ref, bf16[256,768]{1,0:T(8,128)(2,1)S(1)} %get-tuple-element.21.lifted_ref, ...), custom_call_target="tpu_custom_call" | custom-call | flops 2000000000 | bytes 10000000 | tf_op jit(solution)/shard_map/pallas_call | solution.py:331
  16.9 4.4 %all-to-all-start.1 = ((bf16[8,16,768]{2,1,0:T(8,128)(2,1)}), bf16[8,16,768]{2,1,0:T(8,128)(2,1)S(1)}, u32[]{:S(2)}, u32[]{:S(2)}) async-start(bf16[8,16,768]{2,1,0:T(8,128)(2,1)} %get-tuple-element.22.normed_ref), calls=%async_computation.1 | async-start | bytes 393216 | tf_op jit(solution)/shard_map/all_to_all | solution.py:425
  21.3 0.0 copy-done.18
  21.3 0.0 copy-start
  21.3 2.3 %copy-done = bf16[768,3072]{1,0:T(8,128)(2,1)S(1)} copy-done((bf16[768,3072]{1,0:T(8,128)(2,1)S(1)}, bf16[768,3072]{1,0:T(8,128)(2,1)}, u32[]{:S(2)}) %copy-start) | copy-done | bytes 4718616
  23.7 0.0 copy-start.1
  23.7 2.2 %shard_map.199 = (bf16[256,768]{1,0:T(8,128)(2,1)S(1)}, f32[16,768]{1,0:T(8,128)S(1)}, f32[256,256]{1,0:T(8,128)S(1)}, bf16[256,128]{1,0:T(8,128)(2,1)S(1)}, bf16[768,768]{1,0:T(8,128)(2,1)S(1)}) custom-call(bf16[8,16,768]{2,1,0:T(8,128)(2,1)} %get-tuple-element.22.normed_ref, s32[16,128]{1,0:T(8,128)S(1)} %bitcast.7, ...), custom_call_target="tpu_custom_call", output_to_operand_aliasing={{2}: (2, {})} | custom-call | flops 2000000000 | bytes 10000000 | tf_op jit(solution)/shard_map/pallas_call | solution.py:331
  25.9 0.0 all-to-all-done.1.mine_ref
  25.9 2.2 %collective-permute-start.2 = (bf16[8,16,768]{2,1,0:T(8,128)(2,1)S(1)}, bf16[8,16,768]{2,1,0:T(8,128)(2,1)S(1)}, u32[]{:S(2)}, u32[]{:S(2)}) collective-permute-start(bf16[8,16,768]{2,1,0:T(8,128)(2,1)S(1)} %all-to-all-done.1.mine_ref), channel_id=1, source_target_pairs={{0,1},{1,0},{2,3},{3,2},{4,5},{5,4},{6,7},{7,6},{8,9},{9,8},{10,11... | collective-permute-start | bytes 589832 | tf_op jit(solution)/shard_map/ppermute | solution.py:444
  28.1 1.1 %collective-permute-done.2.other_ref = bf16[8,16,768]{2,1,0:T(8,128)(2,1)S(1)} collective-permute-done((bf16[8,16,768]{2,1,0:T(8,128)(2,1)S(1)}, bf16[8,16,768]{2,1,0:T(8,128)(2,1)S(1)}, u32[]{:S(2)}, u32[]{:S(2)}) %collective-permute-start.2) | collective-permute-done | bytes 196640 | tf_op jit(solution)/shard_map/ppermute | solution.py:444
  29.2 0.0 copy-done.1
  29.2 0.0 copy-start.4
  29.2 1.0 %shard_map.200.own_ref = bf16[16,768]{1,0:T(8,128)(2,1)S(1)} custom-call(bf16[8,16,768]{2,1,0:T(8,128)(2,1)S(1)} %all-to-all-done.1.mine_ref, bf16[8,16,768]{2,1,0:T(8,128)(2,1)S(1)} %collective-permute-done.2.other_ref, bf16[256,768]{1,0:T(8,128)(2,1)S(1)} %get-tuple-element.25.query_ref, f32[256,256]{1,0:T(8,128)S(1)} %get-tuple-element.26.biased_ref, ...), custom_call_target="tpu_custom_call" | custom-call | flops 2000000000 | bytes 10000000 | tf_op jit(solution)/shard_map/pallas_call | solution.py:331
  30.2 3.0 %collective-permute-start.4 = (bf16[16,768]{1,0:T(8,128)(2,1)S(1)}, bf16[16,768]{1,0:T(8,128)(2,1)S(1)}, u32[]{:S(2)}, u32[]{:S(2)}) collective-permute-start(bf16[16,768]{1,0:T(8,128)(2,1)S(1)} %shard_map.200.own_ref), channel_id=1, source_target_pairs={{1,2},{3,4},{5,6},{7,8},{9,10},{11,12},{13,14},{2,1},{4,3},{6,5},{... | collective-permute-start | bytes 73736 | tf_op jit(solution)/shard_map/ppermute | solution.py:457
  33.2 0.0 copy-done.4
  33.2 0.6 %shard_map.201 = (bf16[16,128]{1,0:T(8,128)(2,1)S(1)}, f32[256,128]{1,0:T(8,128)S(1)}, bf16[16,768]{1,0:T(8,128)(2,1)}) custom-call(bf16[256,128]{1,0:T(8,128)(2,1)S(1)} %get-tuple-element.18.mid_ref, bf16[16,768]{1,0:T(8,128)(2,1)S(1)} %shard_map.200.own_ref, bf16[256,128]{1,0:T(8,128)(2,1)S(1)} %get-tuple-element.30.pick_ref, bf16[768,128]{1,0:T(8,128)(2,1)S(1)} %copy-done.4), custom_call_target="tpu_custom_call" | custom-call | flops 2000000000 | bytes 10000000 | tf_op jit(solution)/shard_map/pallas_call | solution.py:331
  33.9 0.0 collective-permute-start.3
  33.9 1.2 %collective-permute-done.3.core_ref = bf16[16,128]{1,0:T(8,128)(2,1)S(1)} collective-permute-done((bf16[16,128]{1,0:T(8,128)(2,1)S(1)}, bf16[16,128]{1,0:T(8,128)(2,1)S(1)}, u32[]{:S(2)}, u32[]{:S(2)}) %collective-permute-start.3) | collective-permute-done | bytes 4128 | tf_op jit(solution)/shard_map/ppermute | solution.py:466
  35.0 0.3 collective-permute-done.4.far_ref
  35.4 0.9 %shard_map.202 = bf16[256,128]{1,0:T(8,128)(2,1)} custom-call(f32[256,128]{1,0:T(8,128)S(1)} %get-tuple-element.31.partial_ref, bf16[16,128]{1,0:T(8,128)(2,1)S(1)} %collective-permute-done.3.core_ref, bf16[16,768]{1,0:T(8,128)(2,1)S(1)} %collective-permute-done.4.far_ref, bf16[256,128]{1,0:T(8,128)(2,1)S(1)} %get-tuple-element.30.pick_ref, ...), custom_call_target="tpu_custom_call" | custom-call | flops 2000000000 | bytes 10000000 | tf_op jit(solution)/shard_map/pallas_call | solution.py:331
  (1 shorter events, 0.0 us)
Async XLA Ops:
  0.6 4.7 %copy-start.16 = (s32[8]{0:T(128)S(1)}, s32[8]{0:T(128)}, u32[]{:S(2)}) copy-start(s32[8]{0:T(128)} %param.20) | copy-start | bytes 100
  0.6 4.7 %copy-start.12 = (s32[16]{0:T(128)S(1)}, s32[16]{0:T(128)}, u32[]{:S(2)}) copy-start(s32[16]{0:T(128)} %param.21) | copy-start | bytes 196
  0.7 4.7 %copy-start.13 = (s32[16]{0:T(128)S(1)}, s32[16]{0:T(128)}, u32[]{:S(2)}) copy-start(s32[16]{0:T(128)} %param.23) | copy-start | bytes 196
  0.7 4.7 %copy-start.14 = (s32[16]{0:T(128)S(1)}, s32[16]{0:T(128)}, u32[]{:S(2)}) copy-start(s32[16]{0:T(128)} %param.22) | copy-start | bytes 196
  0.7 12.5 %collective-permute-start = (bf16[256,128]{1,0:T(8,128)(2,1)}, bf16[256,128]{1,0:T(8,128)(2,1)S(1)}, u32[]{:S(2)}, u32[]{:S(2)}) collective-permute-start(bf16[256,128]{1,0:T(8,128)(2,1)} %feat_ref.1), channel_id=1, source_target_pairs={{0,1},{1,0},{2,3},{3,2},{4,5},{5,4},{6,7},{7,6},{8,9},{9,8},{10,11... | collective-permute-start | bytes 196616 | tf_op jit(solution)/shard_map/ppermute | solution.py:377
  0.8 12.4 %collective-permute-start.1 = (bf16[256,128]{1,0:T(8,128)(2,1)}, bf16[256,128]{1,0:T(8,128)(2,1)S(1)}, u32[]{:S(2)}, u32[]{:S(2)}) collective-permute-start(bf16[256,128]{1,0:T(8,128)(2,1)} %feat_ref.1), channel_id=1, source_target_pairs={{1,2},{3,4},{5,6},{7,8},{9,10},{11,12},{13,14},{2,1},{4,3},{6,5},{... | collective-permute-start | bytes 196616 | tf_op jit(solution)/shard_map/ppermute | solution.py:376
  5.3 6.8 %copy-start.2 = (bf16[16,256,128]{2,1,0:T(8,128)(2,1)S(1)}, bf16[16,256,128]{2,1,0:T(8,128)(2,1)}, u32[]{:S(2)}) copy-start(bf16[16,256,128]{2,1,0:T(8,128)(2,1)} %pair_ref.1) | copy-start | bytes 3145732
  5.4 6.8 %copy-start.10 = (bf16[128,16]{0,1:T(8,128)(2,1)S(1)}, bf16[128,16]{0,1:T(8,128)(2,1)}, u32[]{:S(2)}) copy-start(bf16[128,16]{0,1:T(8,128)(2,1)} %param.35) | copy-start | bytes 12292
  5.4 6.8 %copy-start.15 = (f32[128]{0:T(128)S(1)}, f32[128]{0:T(128)}, u32[]{:S(2)}) copy-start(f32[128]{0:T(128)} %gain_ref.3) | copy-start | bytes 1540
  6.1 9.0 %all-to-all-start = ((s32[16,1,128]{2,1,0:T(1,128)}), s32[16,1,128]{2,1,0:T(1,128)S(1)}, u32[]{:S(2)}, u32[]{:S(2)}) async-start(s32[16,1,128]{2,1,0:T(1,128)} %shard_map.197), calls=%async_computation | async-start | bytes 16384 | tf_op jit(solution)/shard_map/all_to_all | solution.py:387
  12.2 1.0 %copy-start.3 = (bf16[128,768]{1,0:T(8,128)(2,1)S(1)}, bf16[128,768]{1,0:T(8,128)(2,1)}, u32[]{:S(2)}) copy-start(bf16[128,768]{1,0:T(8,128)(2,1)} %pool_ref.3) | copy-start | bytes 589828
  12.2 1.0 %copy-start.5 = (bf16[128,384]{1,0:T(8,128)(2,1)S(1)}, bf16[128,384]{1,0:T(8,128)(2,1)}, u32[]{:S(2)}) copy-start(bf16[128,384]{1,0:T(8,128)(2,1)} %qkv_ref.1) | copy-start | bytes 294916
  12.2 1.0 %copy-start.6 = (bf16[256,128]{1,0:T(8,128)(2,1)S(1)}, bf16[256,128]{1,0:T(8,128)(2,1)}, u32[]{:S(2)}) copy-start(bf16[256,128]{1,0:T(8,128)(2,1)} %feat_ref.1) | copy-start | bytes 196612
  12.2 1.0 %copy-start.8 = (bf16[128,128]{1,0:T(8,128)(2,1)S(1)}, bf16[128,128]{1,0:T(8,128)(2,1)}, u32[]{:S(2)}) copy-start(bf16[128,128]{1,0:T(8,128)(2,1)} %out_ref.4) | copy-start | bytes 98308
  12.2 1.0 %copy-start.17 = (f32[128]{0:T(128)S(1)}, f32[128]{0:T(128)}, u32[]{:S(2)}) copy-start(f32[128]{0:T(128)} %gain_ref.4) | copy-start | bytes 1540
  13.2 2.0 %copy-start.7 = (bf16[32,768]{1,0:T(8,128)(2,1)S(1)}, bf16[32,768]{1,0:T(8,128)(2,1)}, u32[]{:S(2)}) copy-start(bf16[32,768]{1,0:T(8,128)(2,1)} %restype_ref.1) | copy-start | bytes 147460
  13.2 2.0 %copy-start.9 = (bf16[16,768]{1,0:T(8,128)(2,1)S(1)}, bf16[16,768]{1,0:T(8,128)(2,1)}, u32[]{:S(2)}) copy-start(bf16[16,768]{1,0:T(8,128)(2,1)} %single_ref.1) | copy-start | bytes 73732
  13.2 2.0 %copy-start.11 = (f32[768]{0:T(1024)S(1)}, f32[768]{0:T(1024)}, u32[]{:S(2)}) copy-start(f32[768]{0:T(1024)} %gain_ref.5) | copy-start | bytes 9220
  15.2 6.1 %copy-start.18 = (f32[16]{0:T(128)S(1)}, f32[16]{0:T(128)}, u32[]{:S(2)}) copy-start(f32[16]{0:T(128)} %chain_weight_ref.1) | copy-start | bytes 196
  16.9 9.0 %all-to-all-start.1 = ((bf16[8,16,768]{2,1,0:T(8,128)(2,1)}), bf16[8,16,768]{2,1,0:T(8,128)(2,1)S(1)}, u32[]{:S(2)}, u32[]{:S(2)}) async-start(bf16[8,16,768]{2,1,0:T(8,128)(2,1)} %get-tuple-element.22.normed_ref), calls=%async_computation.1 | async-start | bytes 393216 | tf_op jit(solution)/shard_map/all_to_all | solution.py:425
  21.3 2.3 %copy-start = (bf16[768,3072]{1,0:T(8,128)(2,1)S(1)}, bf16[768,3072]{1,0:T(8,128)(2,1)}, u32[]{:S(2)}) copy-start(bf16[768,3072]{1,0:T(8,128)(2,1)} %proj_ref.1) | copy-start | bytes 14155780
  23.7 5.6 %copy-start.1 = (bf16[768,768]{1,0:T(8,128)(2,1)S(1)}, bf16[768,768]{1,0:T(8,128)(2,1)}, u32[]{:S(2)}) copy-start(bf16[768,768]{1,0:T(8,128)(2,1)} %out_ref.5) | copy-start | bytes 3538948
  25.9 3.3 %collective-permute-start.2 = (bf16[8,16,768]{2,1,0:T(8,128)(2,1)S(1)}, bf16[8,16,768]{2,1,0:T(8,128)(2,1)S(1)}, u32[]{:S(2)}, u32[]{:S(2)}) collective-permute-start(bf16[8,16,768]{2,1,0:T(8,128)(2,1)S(1)} %all-to-all-done.1.mine_ref), channel_id=1, source_target_pairs={{0,1},{1,0},{2,3},{3,2},{4,5},{5,4},{6,7},{7,6},{8,9},{9,8},{10,11... | collective-permute-start | bytes 589832 | tf_op jit(solution)/shard_map/ppermute | solution.py:444
  29.2 4.0 %copy-start.4 = (bf16[768,128]{1,0:T(8,128)(2,1)S(1)}, bf16[768,128]{1,0:T(8,128)(2,1)}, u32[]{:S(2)}) copy-start(bf16[768,128]{1,0:T(8,128)(2,1)} %weight_ref.3) | copy-start | bytes 589828
  30.2 5.1 %collective-permute-start.4 = (bf16[16,768]{1,0:T(8,128)(2,1)S(1)}, bf16[16,768]{1,0:T(8,128)(2,1)S(1)}, u32[]{:S(2)}, u32[]{:S(2)}) collective-permute-start(bf16[16,768]{1,0:T(8,128)(2,1)S(1)} %shard_map.200.own_ref), channel_id=1, source_target_pairs={{1,2},{3,4},{5,6},{7,8},{9,10},{11,12},{13,14},{2,1},{4,3},{6,5},{... | collective-permute-start | bytes 73736 | tf_op jit(solution)/shard_map/ppermute | solution.py:457
  33.9 1.2 %collective-permute-start.3 = (bf16[16,128]{1,0:T(8,128)(2,1)S(1)}, bf16[16,128]{1,0:T(8,128)(2,1)S(1)}, u32[]{:S(2)}, u32[]{:S(2)}) collective-permute-start(bf16[16,128]{1,0:T(8,128)(2,1)S(1)} %get-tuple-element.32), channel_id=1, source_target_pairs={{0,1},{1,0},{2,3},{3,2},{4,5},{5,4},{6,7},{7,6},{8,9},{9,8},{10,11... | collective-permute-start | bytes 12296 | tf_op jit(solution)/shard_map/ppermute | solution.py:466
